TPU v7x, 32 devices: a whole 2x2x4 slice. The times are simulated.
32 devices in a mesh: cohort: 2 (over y), people: 4 (over z), markers: 4 (over x, core).
Axes of the slice: x: 2, y: 2, z: 4, core: 2. Of those that a mesh axis runs over, the one named last changes fastest.
Arguments:
- genotype: int32 [12288, 2048], P(('cohort', 'people'), 'markers'), parts along dimension 0, may hold values from 0 to 170, as said below
- allele_freq: float32 [16384], P(('cohort', 'markers')), parts along dimension 0, may hold values from 0.05 to 0.5
- person_weight: float32 [12288], P(('cohort', 'people')), parts along dimension 0, may hold values from 0.5 to 18, as said below
- basis: bfloat16 [64, 8192], P('cohort', 'markers'), parts along dimension 0, may hold values from -0.0625 to 0.0625
- residuals: bfloat16 [128, 6144], P('cohort', 'people'), parts along dimension 0, may hold values from -6 to 6
- block_markers: int32 [2048], P('markers'), may hold values from 0 to 8191, as said below
Outputs:
- components: float32 [64, 6144], P('cohort', 'people'), parts along dimension 0
- coefficients: float32 [64, 64], P('cohort'), parts along dimension 0
- basis_next: float32 [4, 64, 2048], P('markers', 'cohort', 'people'), parts along dimension 1
- scores: float32 [4, 128, 512], P('markers', 'cohort', 'people'), parts along dimension 1
There are 2 independent parts, one for each index of `cohort`. A program takes and returns all parts, laid end to end along the dimension named above; an argument that names none is the same for every part. Nothing has to cross between parts.
Inputs may be any that keep to these rules, and one draw needn't show every extreme that they name: `genotype`: each word packs the dosages (0, 1 or 2) of four consecutive markers of one person, marker 4 w + j in bits 2 j and 2 j + 1. `block_markers`: the j-th run of 512 entries holds distinct increasing markers among j * 2048 to (j + 1) * 2048 - 1, always including both of these ends. `person_weight`: positive weights.
All inputs are finite; a program needn't handle non-finite values.
Results may differ from a plain program's by a relative error of at most 0.0054.
Values sent between devices are 32-bit elements; how exact they have to be, the bound alone decides.
No kernel may reach another device: no remote copies, remote signals or barrier semaphores. Data moves between devices by JAX's collectives and lax.ppermute only.
A program may use at most 128 MiB of HBM per device.

v0:
```python
import math

import jax
import jax.numpy as jnp
from jax import lax
from jax.sharding import PartitionSpec as P


def from_partner(block, axis, apart):
    count = lax.axis_size(axis)
    route = []
    for low in range(count):
        high = low | 1 << apart
        if high != low and high < count:
            route += [(low, high), (high, low)]
    return lax.ppermute(block, axis, route)


def decode(packed, freq, weight):
    shifts = 2 * jnp.arange(4, dtype=jnp.int32)
    dosage = jnp.bitwise_and(jnp.right_shift(packed[:, :, None], shifts[None, None, :]), 3)
    dosage = dosage.reshape(packed.shape[0], packed.shape[1] * 4).astype(jnp.float32)
    standard = (dosage - 2.0 * freq[None, :]) / jnp.sqrt(2.0 * freq * (1.0 - freq))[None, :]
    return (weight[:, None] * standard).astype(jnp.bfloat16)


def shards(genotype, allele_freq, person_weight, basis, residuals, block_markers):
    weighted = decode(genotype, allele_freq, person_weight)
    rows_here = weighted.shape[0]
    marker_cols = weighted.shape[1]
    marker_count = lax.axis_size("markers")
    marker_index = lax.axis_index("markers")
    share_rows = rows_here // marker_count
    partial_value = lax.dot_general(
        basis, weighted, (((1,), (1,)), ((), ())), preferred_element_type=jnp.float32
    )
    full_sketch = lax.psum(partial_value, "markers")
    own_sketch = lax.dynamic_slice_in_dim(full_sketch, marker_index * share_rows, share_rows, 1)
    own_residual = lax.dynamic_slice_in_dim(
        residuals, marker_index * share_rows, share_rows, 1
    ).astype(jnp.float32)
    gram_local = jnp.dot(own_sketch, own_sketch.T, precision=lax.Precision.HIGHEST)
    factor_up = jnp.linalg.cholesky(gram_local).T
    levels = lax.axis_size(("people", "markers")).bit_length() - 1
    for level in range(levels):
        partner = from_partner(factor_up, ("people", "markers"), level)
        combined = jnp.dot(factor_up.T, factor_up, precision=lax.Precision.HIGHEST) + jnp.dot(
            partner.T, partner, precision=lax.Precision.HIGHEST
        )
        factor_up = jnp.linalg.cholesky(combined).T
    factor_low = factor_up.T
    ortho = jax.scipy.linalg.solve_triangular(factor_low, full_sketch, lower=True)
    ortho_share = lax.dynamic_slice_in_dim(ortho, marker_index * share_rows, share_rows, 1)
    coefficients = lax.psum(
        jnp.dot(ortho_share, own_residual.T, precision=lax.Precision.HIGHEST), ("people", "markers")
    )
    projected = (
        residuals.astype(jnp.float32)
        - jnp.dot(coefficients.T, ortho, precision=lax.Precision.HIGHEST)
    ).astype(jnp.bfloat16)
    ortho_half = ortho.astype(jnp.bfloat16)
    basis_partial = jnp.dot(ortho_half, weighted, preferred_element_type=jnp.float32)
    columns = block_markers - marker_index * marker_cols
    chosen = jnp.take(weighted, columns, axis=1)
    score_partial = jnp.dot(projected, chosen, preferred_element_type=jnp.float32)
    people_count = lax.axis_size("people")
    people_index = lax.axis_index("people")
    basis_total, score_total = lax.psum((basis_partial, score_partial), "people")
    basis_width = basis_total.shape[1] // people_count
    score_width = score_total.shape[1] // people_count
    basis_own = lax.dynamic_slice_in_dim(basis_total, people_index * basis_width, basis_width, 1)
    score_own = lax.dynamic_slice_in_dim(score_total, people_index * score_width, score_width, 1)
    total_people = rows_here * people_count
    root_people = math.sqrt(total_people)
    components = root_people * ortho
    scores = (score_own / root_people)[None]
    return (components, coefficients, basis_own[None], scores)


def solution(mesh):
    placed = (
        P(("cohort", "people"), "markers"),
        P(("cohort", "markers")),
        P(("cohort", "people")),
        P("cohort", "markers"),
        P("cohort", "people"),
        P("markers"),
    )
    return jax.shard_map(
        shards,
        mesh=mesh,
        in_specs=placed,
        out_specs=(
            P("cohort", "people"),
            P("cohort", None),
            P("markers", "cohort", "people"),
            P("markers", "cohort", "people"),
        ),
        check_vma=False,
    )
```

profile of v0, /device:TPU:0, one launch (start us, length us, event | category | flops | bytes accessed | tf_op | source)
XLA Modules:
  0.0 226.6 jit_solution(14469000959002660257)
XLA Ops:
  7.2 0.0 copy-start
  7.2 0.0 all-reduce.4.cloned.1.call-start
  7.2 2.4 %copy.24 = s32[1536,512]{0,1:T(8,128)S(1)} copy(s32[1536,512]{1,0:T(8,128)} %param.7) | data formatting | bytes 6291456 | tf_op args[0]
  9.6 6.0 %shift_right_arithmetic.20 = s32[1536,512,4]{0,2,1:T(4,128)} broadcast(s32[1536,512]{0,1:T(8,128)S(1)} %copy.24), dimensions={0,1} | broadcast | bytes 15728640 | tf_op jit(solution)/shard_map/shift_right_arithmetic | solution.py:21
  15.6 14.9 %shift_right_arithmetic.21 = s32[1536,2048]{0,1:T(8,128)} reshape(s32[1536,512,4]{0,2,1:T(4,128)} %shift_right_arithmetic.20) | data formatting | bytes 25165824 | tf_op jit(solution)/shard_map/shift_right_arithmetic | solution.py:21
  30.6 0.0 copy-done.5
  30.6 0.2 shift_right_arithmetic.23
  30.8 6.5 %multiply_convert_fusion = bf16[1536,2048]{0,1:T(8,128)(2,1)S(1)} fusion(s32[1536,2048]{0,1:T(8,128)} %shift_right_arithmetic.21, f32[2048]{0:T(1024)S(1)} %get-tuple-element.10, f32[2048]{0:T(1024)S(1)} %get-tuple-element.9, s32[2048]{0:T(1024)S(1)} %shift_right_arithmetic.23, f32[1536]{0:T(1024)S(1)} %copy-done.4), kind=kLoop, calls=%fused_computation.1 | loop fusion | flops 22020096 | bytes 18905088 | tf_op jit(solution)/shard_map/convert_element_type | solution.py:24
  37.3 2.7 %copy-done.1 = bf16[1536,2048]{0,1:T(8,128)(2,1)} copy-done((bf16[1536,2048]{0,1:T(8,128)(2,1)}, bf16[1536,2048]{0,1:T(8,128)(2,1)S(1)}, u32[]{:S(2)}) %copy-start.1) | copy-done | bytes 6291480
  39.9 1.8 convolution_bitcast_fusion
  41.7 0.0 all-reduce.4.cloned.1.call-update
  41.8 0.0 all-reduce.6.cloned.1.call-start
  41.9 7.2 %gather_fusion = bf16[512,1536]{1,0:T(8,128)(2,1)S(1)} fusion(bf16[1536,2048]{0,1:T(8,128)(2,1)} %copy-done.1, s32[1024]{0:T(1024)S(1)} %pad_clamp_fusion), kind=kCustom, calls=%fused_computation | custom fusion | bytes 3147776 | tf_op jit(solution)/shard_map/jit(_take)/gather | solution.py:64
  49.1 0.0 copy-start.2
  49.1 27.2 %all-reduce.4.cloned.1.call-done = f32[32,1536]{1,0:T(8,128)} async-done(((f32[32,1536]{1,0:T(8,128)}), f32[32,1536]{1,0:T(8,128)}) %all-reduce.4.cloned.1.call-update) | async-done | bytes 196624 | tf_op jit(solution)/shard_map/psum | solution.py:37
  76.3 1.1 fusion.10
  77.3 0.1 copy.25
  77.4 2.9 %cholesky.89 = f32[32,32]{1,0:T(8,128)S(1)} custom-call(f32[32,32]{1,0:T(8,128)S(1)} %fusion.19), custom_call_target="Cholesky" | custom-call | tf_op jit(solution)/shard_map/jit(cholesky)/cholesky | solution.py:43
  80.4 0.6 compare_reduce_fusion.4
  81.0 0.6 fusion.28
  81.7 0.1 collective-permute-start
  81.8 0.8 fusion.29
  82.6 0.4 collective-permute-done
  82.9 0.1 convolution_add_fusion.3
  83.1 0.1 copy.28
  83.2 2.9 %cholesky.100 = f32[32,32]{1,0:T(8,128)S(1)} custom-call(f32[32,32]{1,0:T(8,128)S(1)} %fusion.18), custom_call_target="Cholesky" | custom-call | tf_op jit(solution)/shard_map/jit(cholesky)/cholesky | solution.py:50
  86.1 0.6 compare_reduce_fusion.3
  86.8 0.6 fusion.30
  87.4 0.2 collective-permute-start.1
  87.6 0.8 fusion.31
  88.4 2.8 %collective-permute-done.1 = f32[32,32]{0,1:T(8,128)S(1)} collective-permute-done((f32[32,32]{0,1:T(8,128)S(1)}, f32[32,32]{0,1:T(8,128)S(1)}, u32[]{:S(2)}, u32[]{:S(2)}) %collective-permute-start.1) | collective-permute-done | bytes 4128 | tf_op jit(solution)/shard_map/ppermute | solution.py:16
  91.2 0.1 convolution_add_fusion.2
  91.4 0.1 copy.31
  91.5 2.9 %cholesky.111 = f32[32,32]{1,0:T(8,128)S(1)} custom-call(f32[32,32]{1,0:T(8,128)S(1)} %fusion.17), custom_call_target="Cholesky" | custom-call | tf_op jit(solution)/shard_map/jit(cholesky)/cholesky | solution.py:50
  94.4 0.6 compare_reduce_fusion.2
  95.1 0.6 fusion.32
  95.7 1.6 collective-permute-start.2
  97.3 0.8 fusion.33
  98.1 1.5 collective-permute-done.2
  99.5 0.1 convolution_add_fusion.1
  99.7 0.1 copy.34
  99.8 2.9 %cholesky.122 = f32[32,32]{1,0:T(8,128)S(1)} custom-call(f32[32,32]{1,0:T(8,128)S(1)} %fusion.16), custom_call_target="Cholesky" | custom-call | tf_op jit(solution)/shard_map/jit(cholesky)/cholesky | solution.py:50
  102.7 0.6 compare_reduce_fusion.1
  103.4 0.6 fusion.34
  104.0 2.5 %collective-permute-start.3 = (f32[32,32]{0,1:T(8,128)S(1)}, f32[32,32]{0,1:T(8,128)S(1)}, u32[]{:S(2)}, u32[]{:S(2)}) collective-permute-start(f32[32,32]{0,1:T(8,128)S(1)} %fusion.34), channel_id=1, source_target_pairs={{0,8},{8,0},{1,9},{9,1},{2,10},{10,2},{3,11},{11,3},{4,12},{12,4},... | collective-permute-start | bytes 12296 | tf_op jit(solution)/shard_map/ppermute | solution.py:16
  106.5 0.8 fusion.35
  107.3 1.4 collective-permute-done.3
  108.7 0.1 convolution_add_fusion
  108.9 0.1 copy.37
  109.0 2.9 %cholesky.133 = f32[32,32]{1,0:T(8,128)S(1)} custom-call(f32[32,32]{1,0:T(8,128)S(1)} %fusion.15), custom_call_target="Cholesky" | custom-call | tf_op jit(solution)/shard_map/jit(cholesky)/cholesky | solution.py:50
  111.9 0.6 compare_reduce_fusion
  112.6 0.7 fusion.12
  113.2 2.4 %custom-call.6 = f32[1,32,32]{1,2,0:T(8,128)S(1)} custom-call(f32[1,32,32]{2,1,0:T(8,128)S(1)} %fusion.12), custom_call_target="InvertDiagBlocksLowerTriangular" | custom-call | tf_op jit(solution)/shard_map/jit(_solve_triangular)/triangular_solve | solution.py:52
  115.7 2.0 broadcast_multiply_fusion
  117.7 5.4 %fusion.5 = f32[32,2048]{1,0:T(8,128)} fusion(bf16[1536,2048]{0,1:T(8,128)(2,1)} %copy-done.1, f32[32,1536]{1,0:T(8,128)S(1)} %get-tuple-element.12), kind=kOutput, calls=%fused_computation.13 | convolution fusion | flops 201375744 | bytes 6750208 | tf_op jit(solution)/shard_map/dot_general | solution.py:62
  123.1 0.2 fusion.7
  123.2 57.6 %psum.29 = f32[32,64]{1,0:T(8,128)S(1)} all-reduce(f32[32,64]{1,0:T(8,128)S(1)} %fusion.7), channel_id=1, replica_groups=mesh['cohort'=2,'people'=4,'markers'=4] {'people','markers'}, use_global_device_ids=true, to_apply=%region_3.5 | all-reduce | flops 2048 | bytes 16384 | tf_op jit(solution)/shard_map/psum | solution.py:54
  180.9 0.5 fusion
  181.4 1.3 fusion.1
  182.7 0.0 all-reduce.6.cloned.1.call-update
  182.8 34.2 %all-reduce.6.cloned.1.call-done = (f32[32,2048]{1,0:T(8,128)}, f32[64,512]{1,0:T(8,128)}) async-done(((f32[32,2048]{1,0:T(8,128)}, f32[64,512]{1,0:T(8,128)}), (f32[32,2048]{1,0:T(8,128)}, f32[64,512]{1,0:T(8,128)})) %all-reduce.6.cloned.1.call-update) | async-done | bytes 393232 | tf_op jit(solution)/shard_map/psum | solution.py:68
  216.9 1.5 dynamic-slice_bitcast_fusion
  218.4 1.4 multiply_bitcast_fusion
  219.8 0.0 copy-done.3
  (24 shorter events, 0.3 us)
Async XLA Ops:
  7.2 32.8 %copy-start = (bf16[32,2048]{1,0:T(8,128)(2,1)S(1)}, bf16[32,2048]{1,0:T(8,128)(2,1)}, u32[]{:S(2)}) copy-start(bf16[32,2048]{1,0:T(8,128)(2,1)} %param.10) | copy-start | bytes 393220
  7.2 69.1 %all-reduce.4.cloned.1.call-start = ((), (), s32[]{:S(2)}) async-start(), calls=%async_computation | async-start | bytes 393216 | tf_op jit(solution)/shard_map/psum | solution.py:37
  15.6 14.9 %copy-start.5 = (f32[2048]{0:T(1024)S(1)}, f32[2048]{0:T(1024)}, u32[]{:S(2)}) copy-start(f32[2048]{0:T(1024)} %param.8) | copy-start | bytes 24580
  15.6 15.1 %copy-start.4 = (f32[1536]{0:T(1024)S(1)}, f32[1536]{0:T(1024)}, u32[]{:S(2)}) copy-start(f32[1536]{0:T(1024)} %param.9) | copy-start | bytes 18436
  37.3 2.7 %copy-start.1 = (bf16[1536,2048]{0,1:T(8,128)(2,1)}, bf16[1536,2048]{0,1:T(8,128)(2,1)S(1)}, u32[]{:S(2)}) copy-start(bf16[1536,2048]{0,1:T(8,128)(2,1)S(1)} %multiply_convert_fusion) | copy-start | bytes 18874372
  39.9 1.9 copy-start.6
  41.8 175.2 %all-reduce.6.cloned.1.call-start = ((), (), s32[]{:S(2)}) async-start(), calls=%async_computation.1 | async-start | bytes 786432 | tf_op jit(solution)/shard_map/psum | solution.py:68
  49.1 74.0 %copy-start.2 = (bf16[64,1536]{1,0:T(8,128)(2,1)S(1)}, bf16[64,1536]{1,0:T(8,128)(2,1)}, u32[]{:S(2)}) copy-start(bf16[64,1536]{1,0:T(8,128)(2,1)} %param.11) | copy-start | bytes 589828
  81.7 1.2 collective-permute-start
  87.4 3.8 %collective-permute-start.1 = (f32[32,32]{0,1:T(8,128)S(1)}, f32[32,32]{0,1:T(8,128)S(1)}, u32[]{:S(2)}, u32[]{:S(2)}) collective-permute-start(f32[32,32]{0,1:T(8,128)S(1)} %fusion.30), channel_id=1, source_target_pairs={{0,2},{2,0},{1,3},{3,1},{4,6},{6,4},{5,7},{7,5},{8,10},{10,8},{9,1... | collective-permute-start | bytes 12296 | tf_op jit(solution)/shard_map/ppermute | solution.py:16
  95.7 3.8 %collective-permute-start.2 = (f32[32,32]{0,1:T(8,128)S(1)}, f32[32,32]{0,1:T(8,128)S(1)}, u32[]{:S(2)}, u32[]{:S(2)}) collective-permute-start(f32[32,32]{0,1:T(8,128)S(1)} %fusion.32), channel_id=1, source_target_pairs={{0,4},{4,0},{1,5},{5,1},{2,6},{6,2},{3,7},{7,3},{8,12},{12,8},{9,1... | collective-permute-start | bytes 12296 | tf_op jit(solution)/shard_map/ppermute | solution.py:16
  104.0 4.7 %collective-permute-start.3 = (f32[32,32]{0,1:T(8,128)S(1)}, f32[32,32]{0,1:T(8,128)S(1)}, u32[]{:S(2)}, u32[]{:S(2)}) collective-permute-start(f32[32,32]{0,1:T(8,128)S(1)} %fusion.34), channel_id=1, source_target_pairs={{0,8},{8,0},{1,9},{9,1},{2,10},{10,2},{3,11},{11,3},{4,12},{12,4},... | collective-permute-start | bytes 12296 | tf_op jit(solution)/shard_map/ppermute | solution.py:16
  180.9 38.9 %copy-start.3 = (f32[32,64]{1,0:T(8,128)}, f32[32,64]{1,0:T(8,128)S(1)}, u32[]{:S(2)}) copy-start(f32[32,64]{1,0:T(8,128)S(1)} %psum.29) | copy-start | bytes 24580
Sparse Core Ops, SparseCore 0:
  41.9 34.3 all-reduce.3
  182.9 34.0 all-reduce.5
where the time goes:
time: 227 us
  waiting for transfers between devices  67.5 us (30%)
  blocking collectives  57.6 us (25%)
  local copies, waits for them, and re-layouts  35.2 us (16%)
  other arithmetic  31.6 us (14%)
  matrix products  16 us (7%)
  between operations  14.3 us (6%)
  starting transfers between devices  4.36 us (2%)
    psum x1, blocking collectives, shards(): lax.psum(jnp.dot(ortho_share, own_residual.T, precision=lax.Precision.HIG...  57.6 us
    psum x1, waiting for transfers between devices, shards(): lax.psum((basis_partial, score_partial), 'people')  34.2 us
    psum x1, waiting for transfers between devices, shards(): full_sketch = lax.psum(partial_value, 'markers')  27.2 us
    shift_right_arithmetic x4, local copies, waits for them, and re-layouts, decode(): jnp.right_shift(packed[:, :, None], shifts[None, None, :])  21.1 us
    another operation x12, other arithmetic, shards(): factor_up = jnp.linalg.cholesky(combined).T  14.4 us
    gather x1, local copies, waits for them, and re-layouts, shards(): chosen = jnp.take(weighted, columns, axis=1)  7.19 us
    convert_element_type x1, other arithmetic, decode(): return (weight[:, None] * standard).astype(jnp.bfloat16)  6.47 us
    ppermute x4, waiting for transfers between devices, from_partner(): return lax.ppermute(block, axis, route)  6.08 us
  transfers between devices with their start and end apart: 6, of which 6 were waited for; matrix products, arithmetic and copies ran while one was open for 5% of the time, Pallas kernels for 0%

commit v1 on v0

v1 whole, which is shorter than its diff:
```python
import functools
import math

import jax
import jax.numpy as jnp
from jax import lax
from jax.experimental import pallas as pl
from jax.experimental.pallas import tpu as pltpu
from jax.sharding import PartitionSpec as P

LANES = 128
PER_WORD = 4
GROUP = LANES * PER_WORD
VMEM_LIMIT = 40 * 1024 * 1024
HIGHEST = lax.Precision.HIGHEST


def from_partner(block, axis, apart):
    count = lax.axis_size(axis)
    route = [(low, low ^ apart) for low in range(count)]
    return lax.ppermute(block, axis, route)


def split2(value):
    high = value.astype(jnp.bfloat16)
    low = (value - high.astype(jnp.float32)).astype(jnp.bfloat16)
    return high, low


def split3(value):
    high, rest = value.astype(jnp.bfloat16), None
    rest = value - high.astype(jnp.float32)
    middle, low = split2(rest)
    return high, middle, low


def digits(words):
    out = []
    for j in range(PER_WORD):
        one = words if j == 0 else jnp.right_shift(words, 2 * j)
        one = one if j == PER_WORD - 1 else jnp.bitwise_and(one, 3)
        out.append(one.astype(jnp.float32).astype(jnp.bfloat16))
    return out


def natural_of_column(shape):
    column = lax.broadcasted_iota(jnp.int32, shape, len(shape) - 1)
    return PER_WORD * jnp.bitwise_and(column, LANES - 1) + jnp.right_shift(column, 7)


def to_digit_order():
    row = lax.broadcasted_iota(jnp.int32, (GROUP, GROUP), 0)
    column = natural_of_column((1, GROUP))
    return jnp.where(row == column, 1.0, 0.0).astype(jnp.bfloat16)


def to_natural_order():
    row = lax.broadcasted_iota(jnp.int32, (GROUP, GROUP), 0)
    natural = PER_WORD * jnp.bitwise_and(row, LANES - 1) + jnp.right_shift(row, 7)
    column = lax.broadcasted_iota(jnp.int32, (GROUP, GROUP), 1)
    return jnp.where(natural == column, 1.0, 0.0).astype(jnp.bfloat16)


def dot32(a, b):
    return jnp.dot(a, b, preferred_element_type=jnp.float32)


def sketch_kernel(chunk, words_ref, freq_ref, weight_ref, basis_ref, out_ref, order_ref, held, held_sem):
    people = held.shape[0]
    steps = people // chunk
    copies = []
    for step in range(steps):
        rows = pl.ds(step * chunk, chunk)
        copy = pltpu.make_async_copy(words_ref.at[rows, :], held.at[rows, :], held_sem.at[step])
        copy.start()
        copies.append(copy)
    k = basis_ref.shape[0]
    markers = basis_ref.shape[1]
    words = markers // PER_WORD
    freq = freq_ref[...]
    scaled = basis_ref[...].astype(jnp.float32) * lax.rsqrt(2.0 * freq * (1.0 - freq))
    offset = jnp.sum(scaled * (2.0 * freq), axis=1, keepdims=True)
    high, low = split2(scaled)
    f_parts = split3(jnp.broadcast_to(freq, (8, markers)))
    stacked = jnp.concatenate((high, low) + f_parts, axis=0)
    order = to_digit_order()
    pieces = [[None] * (markers // GROUP) for _ in range(PER_WORD)]
    for group in range(markers // GROUP):
        moved = dot32(stacked[:, group * GROUP:(group + 1) * GROUP], order)
        for j in range(PER_WORD):
            pieces[j][group] = moved[:2 * k, j * LANES:(j + 1) * LANES].astype(jnp.bfloat16)
        freq_moved = moved[2 * k:2 * k + 8] + moved[2 * k + 8:2 * k + 16] + moved[2 * k + 16:2 * k + 24]
        order_ref[:, group * GROUP:(group + 1) * GROUP] = freq_moved
    arranged = [jnp.concatenate(pieces[j], axis=1) for j in range(PER_WORD)]
    for step in range(steps):
        copies[step].wait()
        rows = pl.ds(step * chunk, chunk)
        planes = digits(held[rows, :])
        total = None
        for j in range(PER_WORD):
            term = lax.dot_general(
                arranged[j], planes[j], (((1,), (1,)), ((), ())), preferred_element_type=jnp.float32
            )
            total = term if total is None else total + term
        out_ref[:, rows] = (total[:k] + total[k:] - offset) * weight_ref[:, rows]


def sketch_partial(genotype, freq, weight, basis, chunk):
    people, words = genotype.shape
    k, markers = basis.shape
    vmem = pl.BlockSpec(memory_space=pltpu.VMEM)
    return pl.pallas_call(
        functools.partial(sketch_kernel, chunk),
        out_shape=(
            jax.ShapeDtypeStruct((k, people), jnp.float32),
            jax.ShapeDtypeStruct((8, markers), jnp.float32),
        ),
        in_specs=[pl.BlockSpec(memory_space=pl.ANY), vmem, vmem, vmem],
        out_specs=(vmem, vmem),
        scratch_shapes=[
            pltpu.VMEM((people, words), jnp.int32),
            pltpu.SemaphoreType.DMA((people // chunk,)),
        ],
        compiler_params=pltpu.CompilerParams(vmem_limit_bytes=VMEM_LIMIT),
        name="sketch",
    )(genotype, freq, weight, basis)


def product_kernel(
    first_ref, second_ref, residual_ref, weight_ref, freq_ref, chosen_ref, words_ref,
    sketch_ref, basis_ref, score_ref, gram_ref, held, held_sem
):
    people, words = held.shape
    groups = words // LANES
    copies = []
    for group in range(groups):
        columns = pl.ds(group * LANES, LANES)
        copy = pltpu.make_async_copy(words_ref.at[:, columns], held.at[:, columns], held_sem.at[group])
        copy.start()
        copies.append(copy)
    sketch = first_ref[...] + second_ref[...]
    sketch_ref[...] = sketch
    k = sketch.shape[0]
    rows = jnp.concatenate([sketch, residual_ref[...].astype(jnp.float32)], axis=0)
    n_rows = rows.shape[0]
    gram_ref[:, :n_rows] = lax.dot_general(
        sketch, rows, (((1,), (1,)), ((), ())), precision=HIGHEST, preferred_element_type=jnp.float32
    )
    gram_ref[:, n_rows:] = jnp.zeros((k, gram_ref.shape[1] - n_rows), jnp.float32)
    rows = rows * weight_ref[...]
    row_sum = jnp.sum(rows, axis=1, keepdims=True)
    high, low = split2(rows)
    both = jnp.concatenate([high, low], axis=0)
    chosen = chosen_ref[...]
    score = None
    for group in range(groups):
        span = pl.ds(group * GROUP, GROUP)
        copies[group].wait()
        planes = jnp.concatenate(digits(held[:, group * LANES:(group + 1) * LANES]), axis=1)
        raw = dot32(both, planes)
        freq = freq_ref[0:1, span]
        value = (raw[:n_rows] + raw[n_rows:] - row_sum * (2.0 * freq)) * lax.rsqrt(2.0 * freq * (1.0 - freq))
        basis_ref[:, span] = value[:k]
        row = lax.broadcasted_iota(jnp.int32, (GROUP, 1), 0)
        natural = PER_WORD * jnp.bitwise_and(row, LANES - 1) + jnp.right_shift(row, 7) + group * GROUP
        pick = jnp.where(natural == chosen, 1.0, 0.0).astype(jnp.bfloat16)
        v_high, v_low = split2(value)
        term = dot32(v_high, pick) + dot32(v_low, pick)
        score = term if score is None else score + term
    score_ref[...] = score


def products(first, second, residuals, weight, freq, chosen, genotype):
    k, people = first.shape
    r = residuals.shape[0]
    words = genotype.shape[1]
    vmem = pl.BlockSpec(memory_space=pltpu.VMEM)
    return pl.pallas_call(
        product_kernel,
        out_shape=(
            jax.ShapeDtypeStruct((k, people), jnp.float32),
            jax.ShapeDtypeStruct((k, words * PER_WORD), jnp.float32),
            jax.ShapeDtypeStruct((k + r, chosen.shape[1]), jnp.float32),
            jax.ShapeDtypeStruct((k, LANES), jnp.float32),
        ),
        in_specs=[vmem] * 6 + [pl.BlockSpec(memory_space=pl.ANY)],
        out_specs=(vmem,) * 4,
        scratch_shapes=[
            pltpu.VMEM((people, words), jnp.int32),
            pltpu.SemaphoreType.DMA((words // LANES,)),
        ],
        compiler_params=pltpu.CompilerParams(vmem_limit_bytes=VMEM_LIMIT),
        name="products",
    )(first, second, residuals, weight, freq, chosen, genotype)


def eliminate(system, k):
    row_at = lax.broadcasted_iota(jnp.int32, (k, 1), 0)
    for j in range(k):
        pivot = system[j:j + 1, j:j + 1]
        scaled = system[j:j + 1, :] * lax.rsqrt(pivot)
        factor = system[:, j:j + 1] * lax.rsqrt(pivot)
        updated = system - factor * scaled
        system = jnp.where(row_at == j, scaled, jnp.where(row_at > j, updated, system))
    return system


def finish_kernel(
    root_people, k, r, digit_order, sketch_ref, gram_ref, *refs
):
    count = (len(refs) - 4) // 2
    basis_refs, score_refs = refs[:count], refs[count:2 * count]
    components_ref, coefficients_ref, next_ref, out_ref = refs[2 * count:]
    row_at = lax.broadcasted_iota(jnp.int32, (k, k), 0)
    column_at = lax.broadcasted_iota(jnp.int32, (k, k), 1)
    identity = jnp.where(row_at == column_at, 1.0, 0.0)
    grams = [gram_ref[i] for i in range(gram_ref.shape[0])]
    while len(grams) > 1:
        grams = [a + b for a, b in zip(grams[::2], grams[1::2])]
    system = jnp.concatenate([grams[0][:, :k + r], identity], axis=1)
    system = eliminate(system, k)
    coefficients = system[:, k:k + r]
    inverse = system[:, k + r:]
    coefficients_ref[...] = coefficients
    highest = functools.partial(jnp.dot, precision=HIGHEST, preferred_element_type=jnp.float32)
    components_ref[...] = root_people * highest(inverse, sketch_ref[...])
    basis_total, score_total = basis_refs[0][...], score_refs[0][...]
    for ref in basis_refs[1:]:
        basis_total = basis_total + ref[...]
    for ref in score_refs[1:]:
        score_total = score_total + ref[...]
    basis = highest(inverse, basis_total)
    if digit_order:
        order = to_natural_order()
        parts = split3(basis)
        basis = dot32(parts[0], order) + dot32(parts[1], order) + dot32(parts[2], order)
    next_ref[...] = basis
    removed = lax.dot_general(
        coefficients, highest(inverse, score_total[:k]), (((0,), (0,)), ((), ())),
        precision=HIGHEST, preferred_element_type=jnp.float32,
    )
    out_ref[...] = (score_total[k:] - removed) * (1.0 / root_people)


def finish(root_people, r, digit_order, sketch, grams, basis_parts, score_parts):
    k = sketch.shape[0]
    vmem = pl.BlockSpec(memory_space=pltpu.VMEM)
    return pl.pallas_call(
        functools.partial(finish_kernel, root_people, k, r, digit_order),
        out_shape=(
            jax.ShapeDtypeStruct(sketch.shape, jnp.float32),
            jax.ShapeDtypeStruct((k, r), jnp.float32),
            jax.ShapeDtypeStruct(basis_parts[0].shape, jnp.float32),
            jax.ShapeDtypeStruct((r, score_parts[0].shape[1]), jnp.float32),
        ),
        in_specs=[vmem] * (2 + len(basis_parts) + len(score_parts)),
        out_specs=(vmem,) * 4,
        compiler_params=pltpu.CompilerParams(vmem_limit_bytes=VMEM_LIMIT),
        name="finish",
    )(sketch, grams, *basis_parts, *score_parts)


def shards(genotype, allele_freq, person_weight, basis, residuals, block_markers):
    people, words = genotype.shape
    markers = words * PER_WORD
    k, r = basis.shape[0], residuals.shape[0]
    marker_count = lax.axis_size("markers")
    people_count = lax.axis_size("people")
    people_index = lax.axis_index("people")
    weight = person_weight[None, :]
    chosen = (block_markers - lax.axis_index("markers") * markers)[None, :]
    sketch, freq = sketch_partial(genotype, allele_freq[None, :], weight, basis, people // 4)
    apart = 1
    while apart * 2 < marker_count:
        sketch = sketch + from_partner(sketch, "markers", apart)
        apart *= 2
    other = from_partner(sketch, "markers", apart)
    sketch, basis_part, score_part, gram = products(
        sketch, other, residuals, weight, freq, chosen, genotype
    )
    basis_width = markers // people_count
    score_width = score_part.shape[1] // people_count
    if people_count == 4 and basis_width == GROUP:
        grams, basis_parts, score_parts = [gram], [], []
        for apart in range(4):
            target = jnp.bitwise_xor(people_index, apart)
            one_basis = lax.dynamic_slice_in_dim(basis_part, target * basis_width, basis_width, 1)
            one_score = lax.dynamic_slice_in_dim(score_part, target * score_width, score_width, 1)
            if apart == 0:
                basis_parts.append(one_basis)
                score_parts.append(one_score)
                continue
            sent = jnp.concatenate([one_basis] + [one_score[i * k:(i + 1) * k] for i in range((k + r) // k)] + [gram], axis=1)
            got = from_partner(sent, "people", apart)
            basis_parts.append(got[:, :basis_width])
            score_parts.append(jnp.concatenate([got[:, basis_width + i * score_width:basis_width + (i + 1) * score_width] for i in range((k + r) // k)], axis=0))
            grams.append(got[:, -LANES:])
        grams = jnp.stack(grams)
    else:
        basis_part = basis_part.reshape(k, markers // GROUP, PER_WORD, LANES)
        basis_part = jnp.swapaxes(basis_part, 2, 3).reshape(k, markers)
        basis_total, score_total, grams = lax.psum((basis_part, score_part, gram), "people")
        basis_parts = [lax.dynamic_slice_in_dim(basis_total, people_index * basis_width, basis_width, 1)]
        score_parts = [lax.dynamic_slice_in_dim(score_total, people_index * score_width, score_width, 1)]
        grams = grams[None]
    components, coefficients, basis_own, score_own = finish(
        math.sqrt(people * people_count), r, len(basis_parts) > 1, sketch, grams, basis_parts, score_parts
    )
    return components, coefficients, basis_own[None], score_own[None]


def solution(mesh):
    placed = (
        P(("cohort", "people"), "markers"),
        P(("cohort", "markers")),
        P(("cohort", "people")),
        P("cohort", "markers"),
        P("cohort", "people"),
        P("markers"),
    )
    return jax.shard_map(
        shards,
        mesh=mesh,
        in_specs=placed,
        out_specs=(
            P("cohort", "people"),
            P("cohort", None),
            P("markers", "cohort", "people"),
            P("markers", "cohort", "people"),
        ),
        check_vma=False,
    )
```

time: 227 us -> 46.5 us (0.20)
  blocking collectives: 57.6 us -> 0 us
  waiting for transfers between devices: 67.5 us -> 16.2 us
  other arithmetic: 31.6 us -> 0.05 us
  local copies, waits for them, and re-layouts: 35.2 us -> 7.45 us
  matrix products: 16 us -> 0 us
  Pallas kernels: 0 us -> 13.7 us
  between operations: 14.3 us -> 0.81 us
  starting transfers between devices: 4.36 us -> 7.94 us
    psum x2 -> x0, waiting for transfers between devices: 61.4 us -> none  [the longest x1 34.2 us: shards(): lax.psum((basis_partial, score_partial), 'people')]
    psum x1 -> x0, blocking collectives: 57.6 us -> none  [shards(): lax.psum(jnp.dot(ortho_share, own_residual.T, precision=lax.Precision.HIG...]
    shift_right_arithmetic x4 -> x0, local copies, waits for them, and re-layouts: 21.1 us -> none  [decode(): jnp.right_shift(packed[:, :, None], shifts[None, None, :])]
    another operation x17 -> x1, other arithmetic: 21.1 us -> 0.01 us  [shards(): grams = jnp.stack(grams)]
    dot_general x14 -> x0, matrix products: 14.1 us -> none  [the longest x1 5.42 us: shards(): jnp.dot(ortho_half, weighted, preferred_element_type=jnp.float32)]
    pallas_call x0 -> x3, Pallas kernels: none -> 13.7 us  [the longest x1 5.15 us: products(): pl.pallas_call(product_kernel, out_shape=(jax.ShapeDtypeStruct((k, people...]
    ppermute x4 -> x5, waiting for transfers between devices: 6.08 us -> 16.2 us  [from_partner(): return lax.ppermute(block, axis, route)]
    gather x1 -> x0, local copies, waits for them, and re-layouts: 7.19 us -> none  [shards(): chosen = jnp.take(weighted, columns, axis=1)]
  transfers between devices with their start and end apart: 6 -> 5, of which waited for: 6 -> 4; matrix products, arithmetic and copies ran while one was open for 5% -> 0% of each run, Pallas kernels for 0% -> 0%
where the time goes in v1:
time: 46.5 us; the launch traced here: 46.1 us
  waiting for transfers between devices  16.2 us (35%)
  Pallas kernels  13.7 us (29%)
  starting transfers between devices  7.94 us (17%)
  local copies, waits for them, and re-layouts  7.45 us (16%)
  between operations  0.81 us (2%)
    ppermute x5, waiting for transfers between devices, from_partner(): return lax.ppermute(block, axis, route)  16.2 us
    ppermute x5, starting transfers between devices, from_partner(): return lax.ppermute(block, axis, route)  7.94 us
    unnamed x24, local copies, waits for them, and re-layouts  6.66 us
    pallas_call x1, Pallas kernels, products(): pl.pallas_call(product_kernel, out_shape=(jax.ShapeDtypeStruct((k, people...  5.15 us
    pallas_call x1, Pallas kernels, finish(): pl.pallas_call(functools.partial(finish_kernel, root_people, k, r, digit_...  4.33 us
    pallas_call x1, Pallas kernels, sketch_partial(): pl.pallas_call(functools.partial(sketch_kernel, chunk), out_shape=(jax.Sh...  4.21 us
  transfers between devices with their start and end apart: 5, of which 4 were waited for; matrix products, arithmetic and copies ran while one was open for 0% of the time, Pallas kernels for 0%

profile of v1, /device:TPU:0, one launch (start us, length us, event | category | flops | bytes accessed | tf_op | source)
XLA Modules:
  0.0 46.1 jit_solution(9951195126740019883)
XLA Ops:
  0.6 0.0 copy-start.9
  0.6 0.7 %broadcast_in_dim.16.weight_ref = f32[1,1536]{1,0:T(1,128)S(1)} reshape(f32[1536]{0:T(1024)} %param.8) | data formatting | bytes 12288 | tf_op jit(solution)/shard_map/broadcast_in_dim | solution.py:270
  1.3 0.0 copy-start.6
  1.4 0.0 copy-start
  1.4 1.9 %copy-done = s32[1536,512]{1,0:T(8,128)S(1)} copy-done((s32[1536,512]{1,0:T(8,128)S(1)}, s32[1536,512]{1,0:T(8,128)}, u32[]{:S(2)}) %copy-start) | copy-done | bytes 3145752
  3.2 0.0 copy-start.3
  3.2 0.9 %copy-done.3 = bf16[32,2048]{1,0:T(8,128)(2,1)S(1)} copy-done((bf16[32,2048]{1,0:T(8,128)(2,1)S(1)}, bf16[32,2048]{1,0:T(8,128)(2,1)}, u32[]{:S(2)}) %copy-start.3) | copy-done | bytes 131096
  4.2 0.0 copy-start.8
  4.2 0.7 %copy-done.8 = f32[2048]{0:T(1024)S(1)} copy-done((f32[2048]{0:T(1024)S(1)}, f32[2048]{0:T(1024)}, u32[]{:S(2)}) %copy-start.8) | copy-done | bytes 8216
  4.8 0.0 copy-start.1
  4.8 4.2 %sketch.1 = (f32[32,1536]{1,0:T(8,128)S(1)}, f32[8,2048]{1,0:T(8,128)S(1)}) custom-call(s32[1536,512]{1,0:T(8,128)S(1)} %copy-done, f32[1,2048]{1,0:T(1,128)S(1)} %bitcast.12, f32[1,1536]{1,0:T(1,128)S(1)} %broadcast_in_dim.16.weight_ref, bf16[32,2048]{1,0:T(8,128)(2,1)S(1)} %copy-done.3), custom_call_target="tpu_custom_call" | custom-call | tf_op jit(solution)/shard_map/sketch/pallas_call | solution.py:112
  9.1 0.0 copy-done.6
  9.1 0.0 copy-start.4
  9.1 0.6 %copy-done.4 = f32[8,2048]{1,0:T(8,128)} copy-done((f32[8,2048]{1,0:T(8,128)}, f32[8,2048]{1,0:T(8,128)S(1)}, u32[]{:S(2)}) %copy-start.4) | copy-done | bytes 65560
  9.7 0.5 collective-permute-start
  10.2 1.1 %collective-permute-done = f32[32,1536]{1,0:T(8,128)S(1)} collective-permute-done((f32[32,1536]{1,0:T(8,128)S(1)}, f32[32,1536]{1,0:T(8,128)S(1)}, u32[]{:S(2)}, u32[]{:S(2)}) %collective-permute-start) | collective-permute-done | bytes 196640 | tf_op jit(solution)/shard_map/ppermute | solution.py:21
  11.3 2.9 %collective-permute-start.1 = (f32[32,1536]{1,0:T(8,128)S(1)}, f32[32,1536]{1,0:T(8,128)S(1)}, u32[]{:S(2)}, u32[]{:S(2)}) collective-permute-start(f32[32,1536]{1,0:T(8,128)S(1)} %add.27.first_ref), channel_id=1, source_target_pairs={{0,2},{1,3},{2,0},{3,1},{4,6},{5,7},{6,4},{7,5},{8,10},{9,11},{10,... | collective-permute-start | bytes 589832 | tf_op jit(solution)/shard_map/ppermute | solution.py:21
  14.2 0.0 copy-done.9
  14.2 5.2 %collective-permute-done.1.second_ref = f32[32,1536]{1,0:T(8,128)S(1)} collective-permute-done((f32[32,1536]{1,0:T(8,128)S(1)}, f32[32,1536]{1,0:T(8,128)S(1)}, u32[]{:S(2)}, u32[]{:S(2)}) %collective-permute-start.1) | collective-permute-done | bytes 196640 | tf_op jit(solution)/shard_map/ppermute | solution.py:21
  19.4 0.0 copy-done.1
  19.4 0.0 copy-start.2
  19.4 0.9 %copy-done.2 = bf16[64,1536]{1,0:T(8,128)(2,1)S(1)} copy-done((bf16[64,1536]{1,0:T(8,128)(2,1)S(1)}, bf16[64,1536]{1,0:T(8,128)(2,1)}, u32[]{:S(2)}) %copy-start.2) | copy-done | bytes 196632
  20.3 0.0 copy-start.5
  20.3 0.8 %copy-done.5 = f32[8,2048]{1,0:T(8,128)S(1)} copy-done((f32[8,2048]{1,0:T(8,128)S(1)}, f32[8,2048]{1,0:T(8,128)}, u32[]{:S(2)}) %copy-start.5) | copy-done | bytes 65560
  21.2 0.0 copy-start.7
  21.2 0.7 %copy-done.7 = f32[1,1536]{1,0:T(1,128)S(1)} copy-done((f32[1,1536]{1,0:T(1,128)S(1)}, f32[1,1536]{1,0:T(1,128)}, u32[]{:S(2)}) %copy-start.7) | copy-done | bytes 6168
  21.8 5.2 %products.1 = (f32[32,1536]{1,0:T(8,128)S(1)}, f32[32,2048]{1,0:T(8,128)S(1)}, f32[96,512]{1,0:T(8,128)S(1)}, f32[32,128]{1,0:T(8,128)S(1)}) custom-call(f32[32,1536]{1,0:T(8,128)S(1)} %add.27.first_ref, f32[32,1536]{1,0:T(8,128)S(1)} %collective-permute-done.1.second_ref, bf16[64,1536]{1,0:T(8,128)(2,1)S(1)} %copy-done.2, f32[1,1536]{1,0:T(1,128)S(1)} %copy-done.7, ...), custom_call_target="tpu_custom_call" | custom-call | tf_op jit(solution)/shard_map/products/pallas_call | solution.py:178
  27.2 3.9 %collective-permute-start.4 = (f32[32,1024]{1,0:T(8,128)S(1)}, f32[32,1024]{1,0:T(8,128)S(1)}, u32[]{:S(2)}, u32[]{:S(2)}) collective-permute-start(f32[32,1024]{1,0:T(8,128)S(1)} %get-tuple-element.49), channel_id=1, source_target_pairs={{0,12},{4,8},{8,4},{12,0},{1,13},{5,9},{9,5},{13,1},{2,14},{6,10},... | collective-permute-start | bytes 393224 | tf_op jit(solution)/shard_map/ppermute | solution.py:21
  31.1 0.0 collective-permute-start.3
  31.1 0.6 %collective-permute-start.2 = (f32[32,1024]{1,0:T(8,128)S(1)}, f32[32,1024]{1,0:T(8,128)S(1)}, u32[]{:S(2)}, u32[]{:S(2)}) collective-permute-start(f32[32,1024]{1,0:T(8,128)S(1)} %get-tuple-element.48), channel_id=1, source_target_pairs={{0,4},{4,0},{8,12},{12,8},{1,5},{5,1},{9,13},{13,9},{2,6},{6,2},{1... | collective-permute-start | bytes 393224 | tf_op jit(solution)/shard_map/ppermute | solution.py:21
  31.7 3.8 %collective-permute-done.4 = f32[32,1024]{1,0:T(8,128)S(1)} collective-permute-done((f32[32,1024]{1,0:T(8,128)S(1)}, f32[32,1024]{1,0:T(8,128)S(1)}, u32[]{:S(2)}, u32[]{:S(2)}) %collective-permute-start.4) | collective-permute-done | bytes 131104 | tf_op jit(solution)/shard_map/ppermute | solution.py:21
  35.6 6.1 %collective-permute-done.3 = f32[32,1024]{1,0:T(8,128)S(1)} collective-permute-done((f32[32,1024]{1,0:T(8,128)S(1)}, f32[32,1024]{1,0:T(8,128)S(1)}, u32[]{:S(2)}, u32[]{:S(2)}) %collective-permute-start.3) | collective-permute-done | bytes 131104 | tf_op jit(solution)/shard_map/ppermute | solution.py:21
  41.7 0.0 collective-permute-done.2
  41.8 4.3 %finish.1 = (f32[32,1536]{1,0:T(8,128)}, f32[32,64]{1,0:T(8,128)}, f32[32,512]{1,0:T(8,128)}, f32[64,128]{1,0:T(8,128)}) custom-call(f32[32,1536]{1,0:T(8,128)S(1)} %get-tuple-element.16.sketch_ref, f32[4,32,128]{2,1,0:T(8,128)S(1)} %pad_maximum_fusion.gram_ref, f32[32,512]{1,0:T(8,128)S(1)} %get-tuple-element.24.refs_0_, f32[32,512]{1,0:T(8,128)S(1)} %slice.99.refs_1_, ...), custom_call_target="tpu_custom_call" | custom-call | tf_op jit(solution)/shard_map/finish/pallas_call | solution.py:248
  (19 shorter events, 0.2 us)
Async XLA Ops:
  0.6 13.6 %copy-start.9 = (s32[512]{0:T(512)S(1)}, s32[512]{0:T(512)}, u32[]{:S(2)}) copy-start(s32[512]{0:T(512)} %param.11) | copy-start | bytes 6148
  1.3 7.7 %copy-start.6 = (f32[1,1536]{1,0:T(1,128)}, f32[1,1536]{1,0:T(1,128)S(1)}, u32[]{:S(2)}) copy-start(f32[1,1536]{1,0:T(1,128)S(1)} %broadcast_in_dim.16.weight_ref) | copy-start | bytes 18436
  1.4 1.9 %copy-start = (s32[1536,512]{1,0:T(8,128)S(1)}, s32[1536,512]{1,0:T(8,128)}, u32[]{:S(2)}) copy-start(s32[1536,512]{1,0:T(8,128)} %words_ref.3) | copy-start | bytes 9437188
  3.2 0.9 %copy-start.3 = (bf16[32,2048]{1,0:T(8,128)(2,1)S(1)}, bf16[32,2048]{1,0:T(8,128)(2,1)}, u32[]{:S(2)}) copy-start(bf16[32,2048]{1,0:T(8,128)(2,1)} %basis_ref.1) | copy-start | bytes 393220
  4.2 0.7 %copy-start.8 = (f32[2048]{0:T(1024)S(1)}, f32[2048]{0:T(1024)}, u32[]{:S(2)}) copy-start(f32[2048]{0:T(1024)} %param.7) | copy-start | bytes 24580
  4.8 14.5 %copy-start.1 = (s32[1536,512]{1,0:T(8,128)S(1)}, s32[1536,512]{1,0:T(8,128)}, u32[]{:S(2)}) copy-start(s32[1536,512]{1,0:T(8,128)} %words_ref.3) | copy-start | bytes 9437188
  9.1 0.6 %copy-start.4 = (f32[8,2048]{1,0:T(8,128)}, f32[8,2048]{1,0:T(8,128)S(1)}, u32[]{:S(2)}) copy-start(f32[8,2048]{1,0:T(8,128)S(1)} %get-tuple-element.15.freq_ref) | copy-start | bytes 196612
  9.7 1.5 %collective-permute-start = (f32[32,1536]{1,0:T(8,128)S(1)}, f32[32,1536]{1,0:T(8,128)S(1)}, u32[]{:S(2)}, u32[]{:S(2)}) collective-permute-start(f32[32,1536]{1,0:T(8,128)S(1)} %get-tuple-element.14), channel_id=1, source_target_pairs={{0,1},{1,0},{2,3},{3,2},{4,5},{5,4},{6,7},{7,6},{8,9},{9,8},{10,11... | collective-permute-start | bytes 589832 | tf_op jit(solution)/shard_map/ppermute | solution.py:21
  11.3 8.1 %collective-permute-start.1 = (f32[32,1536]{1,0:T(8,128)S(1)}, f32[32,1536]{1,0:T(8,128)S(1)}, u32[]{:S(2)}, u32[]{:S(2)}) collective-permute-start(f32[32,1536]{1,0:T(8,128)S(1)} %add.27.first_ref), channel_id=1, source_target_pairs={{0,2},{1,3},{2,0},{3,1},{4,6},{5,7},{6,4},{7,5},{8,10},{9,11},{10,... | collective-permute-start | bytes 589832 | tf_op jit(solution)/shard_map/ppermute | solution.py:21
  19.4 0.9 %copy-start.2 = (bf16[64,1536]{1,0:T(8,128)(2,1)S(1)}, bf16[64,1536]{1,0:T(8,128)(2,1)}, u32[]{:S(2)}) copy-start(bf16[64,1536]{1,0:T(8,128)(2,1)} %residual_ref.1) | copy-start | bytes 589828
  20.3 0.8 %copy-start.5 = (f32[8,2048]{1,0:T(8,128)S(1)}, f32[8,2048]{1,0:T(8,128)}, u32[]{:S(2)}) copy-start(f32[8,2048]{1,0:T(8,128)} %copy-done.4) | copy-start | bytes 196612
  21.2 0.7 %copy-start.7 = (f32[1,1536]{1,0:T(1,128)S(1)}, f32[1,1536]{1,0:T(1,128)}, u32[]{:S(2)}) copy-start(f32[1,1536]{1,0:T(1,128)} %copy-done.6) | copy-start | bytes 18436
  27.2 8.4 %collective-permute-start.4 = (f32[32,1024]{1,0:T(8,128)S(1)}, f32[32,1024]{1,0:T(8,128)S(1)}, u32[]{:S(2)}, u32[]{:S(2)}) collective-permute-start(f32[32,1024]{1,0:T(8,128)S(1)} %get-tuple-element.49), channel_id=1, source_target_pairs={{0,12},{4,8},{8,4},{12,0},{1,13},{5,9},{9,5},{13,1},{2,14},{6,10},... | collective-permute-start | bytes 393224 | tf_op jit(solution)/shard_map/ppermute | solution.py:21
  31.1 10.5 %collective-permute-start.3 = (f32[32,1024]{1,0:T(8,128)S(1)}, f32[32,1024]{1,0:T(8,128)S(1)}, u32[]{:S(2)}, u32[]{:S(2)}) collective-permute-start(f32[32,1024]{1,0:T(8,128)S(1)} %get-tuple-element.50), channel_id=1, source_target_pairs={{0,8},{4,12},{8,0},{12,4},{1,9},{5,13},{9,1},{13,5},{2,10},{6,14},... | collective-permute-start | bytes 393224 | tf_op jit(solution)/shard_map/ppermute | solution.py:21
  31.1 10.6 %collective-permute-start.2 = (f32[32,1024]{1,0:T(8,128)S(1)}, f32[32,1024]{1,0:T(8,128)S(1)}, u32[]{:S(2)}, u32[]{:S(2)}) collective-permute-start(f32[32,1024]{1,0:T(8,128)S(1)} %get-tuple-element.48), channel_id=1, source_target_pairs={{0,4},{4,0},{8,12},{12,8},{1,5},{5,1},{9,13},{13,9},{2,6},{6,2},{1... | collective-permute-start | bytes 393224 | tf_op jit(solution)/shard_map/ppermute | solution.py:21

commit v2 on v1

v2 whole, which is shorter than its diff:
```python
import functools
import math

import jax
import jax.numpy as jnp
from jax import lax
from jax.experimental import pallas as pl
from jax.experimental.pallas import tpu as pltpu
from jax.sharding import PartitionSpec as P

LANES = 128
PER_WORD = 4
GROUP = LANES * PER_WORD
VMEM_LIMIT = 40 * 1024 * 1024
HIGHEST = lax.Precision.HIGHEST
IN_HBM = pl.BlockSpec(memory_space=pltpu.HBM)
IN_VMEM = pl.BlockSpec(memory_space=pltpu.VMEM)


def from_partner(block, axis, apart):
    count = lax.axis_size(axis)
    route = [(low, low ^ apart) for low in range(count)]
    return lax.ppermute(block, axis, route)


def split2(value):
    high = value.astype(jnp.bfloat16)
    low = (value - high.astype(jnp.float32)).astype(jnp.bfloat16)
    return high, low


def split3(value):
    high, rest = value.astype(jnp.bfloat16), None
    rest = value - high.astype(jnp.float32)
    middle, low = split2(rest)
    return high, middle, low


def digits(words):
    out = []
    for j in range(PER_WORD):
        one = words if j == 0 else jnp.right_shift(words, 2 * j)
        one = one if j == PER_WORD - 1 else jnp.bitwise_and(one, 3)
        out.append(one.astype(jnp.float32).astype(jnp.bfloat16))
    return out


def natural_of_column(shape):
    column = lax.broadcasted_iota(jnp.int32, shape, len(shape) - 1)
    return PER_WORD * jnp.bitwise_and(column, LANES - 1) + jnp.right_shift(column, 7)


def to_digit_order():
    row = lax.broadcasted_iota(jnp.int32, (GROUP, GROUP), 0)
    column = natural_of_column((1, GROUP))
    return jnp.where(row == column, 1.0, 0.0).astype(jnp.bfloat16)


def to_natural_order():
    row = lax.broadcasted_iota(jnp.int32, (GROUP, GROUP), 0)
    natural = PER_WORD * jnp.bitwise_and(row, LANES - 1) + jnp.right_shift(row, 7)
    column = lax.broadcasted_iota(jnp.int32, (GROUP, GROUP), 1)
    return jnp.where(natural == column, 1.0, 0.0).astype(jnp.bfloat16)


def dot32(a, b):
    return jnp.dot(a, b, preferred_element_type=jnp.float32)


def start_copy(source, target, sem):
    copy = pltpu.make_async_copy(source, target, sem)
    copy.start()
    return copy


def group_of(slot, direct):
    return jnp.bitwise_xor(lax.axis_index("people"), slot) if direct else slot


def sketch_kernel(
    chunk, words_ref, freq_ref, weight_ref, basis_ref, out_ref, order_ref, planes_ref,
    words, freq_here, weight_here, basis_here, words_sem, sems
):
    people = words.shape[0]
    steps = people // chunk
    small = [
        start_copy(freq_ref, freq_here, sems.at[0]),
        start_copy(basis_ref, basis_here, sems.at[1]),
        start_copy(weight_ref, weight_here, sems.at[2]),
    ]
    copies = []
    for step in range(steps):
        rows = pl.ds(step * chunk, chunk)
        copies.append(start_copy(words_ref.at[rows, :], words.at[rows, :], words_sem.at[step]))
    k, markers = basis_here.shape
    per_digit = markers // PER_WORD
    order = to_digit_order()
    for copy in small:
        copy.wait()
    freq = freq_here[...].reshape(1, markers)
    weight = weight_here[...].reshape(1, people)
    scaled = basis_here[...].astype(jnp.float32) * lax.rsqrt(2.0 * freq * (1.0 - freq))
    offset = jnp.sum(scaled * (2.0 * freq), axis=1, keepdims=True)
    high, low = split2(scaled)
    f_parts = split3(jnp.broadcast_to(freq, (8, markers)))
    stacked = jnp.concatenate((high, low) + f_parts, axis=0)
    pieces = [[None] * (markers // GROUP) for _ in range(PER_WORD)]
    for group in range(markers // GROUP):
        moved = dot32(stacked[:, group * GROUP:(group + 1) * GROUP], order)
        for j in range(PER_WORD):
            pieces[j][group] = moved[:2 * k, j * LANES:(j + 1) * LANES].astype(jnp.bfloat16)
        freq_moved = moved[2 * k:2 * k + 8] + moved[2 * k + 8:2 * k + 16] + moved[2 * k + 16:2 * k + 24]
        order_ref[:, group * GROUP:(group + 1) * GROUP] = freq_moved
    arranged = [jnp.concatenate(pieces[j], axis=1) for j in range(PER_WORD)]
    for step in range(steps):
        copies[step].wait()
        rows = pl.ds(step * chunk, chunk)
        planes = digits(words[rows, :])
        total = None
        for j in range(PER_WORD):
            for group in range(markers // GROUP):
                at = group * GROUP + j * LANES
                planes_ref[rows, at:at + LANES] = planes[j][:, group * LANES:(group + 1) * LANES]
            term = lax.dot_general(
                arranged[j], planes[j], (((1,), (1,)), ((), ())), preferred_element_type=jnp.float32
            )
            total = term if total is None else total + term
        out_ref[:, rows] = (total[:k] + total[k:] - offset) * weight[:, step * chunk:(step + 1) * chunk]


def sketch_partial(genotype, freq, weight, basis, chunk):
    people, words = genotype.shape
    k, markers = basis.shape
    return pl.pallas_call(
        functools.partial(sketch_kernel, chunk),
        out_shape=(
            jax.ShapeDtypeStruct((k, people), jnp.float32),
            jax.ShapeDtypeStruct((8, markers), jnp.float32),
            jax.ShapeDtypeStruct((people, markers), jnp.bfloat16),
        ),
        in_specs=[IN_HBM] * 4,
        out_specs=(IN_VMEM,) * 3,
        scratch_shapes=[
            pltpu.VMEM((people, words), jnp.int32),
            pltpu.VMEM(freq.shape, jnp.float32),
            pltpu.VMEM(weight.shape, jnp.float32),
            pltpu.VMEM(basis.shape, jnp.bfloat16),
            pltpu.SemaphoreType.DMA((people // chunk,)),
            pltpu.SemaphoreType.DMA((3,)),
        ],
        compiler_params=pltpu.CompilerParams(vmem_limit_bytes=VMEM_LIMIT),
        name="sketch",
    )(genotype, freq, weight, basis)


def standard(rows, planes_ref, order_ref, span):
    n_rows = rows.shape[0]
    row_sum = jnp.sum(rows, axis=1, keepdims=True)
    raw = dot32(jnp.concatenate(split2(rows), axis=0), planes_ref[:, span])
    freq = order_ref[0:1, span]
    return (raw[:n_rows] + raw[n_rows:] - row_sum * (2.0 * freq)) * lax.rsqrt(2.0 * freq * (1.0 - freq))


def trait_kernel(
    direct, planes_ref, order_ref, residual_ref, weight_ref, chosen_ref, *refs
):
    outs, (pick_ref, total, residual_here, weight_here, chosen_here, sems) = refs[:-6], refs[-6:]
    copies = [
        start_copy(residual_ref, residual_here, sems.at[0]),
        start_copy(weight_ref, weight_here, sems.at[1]),
        start_copy(chosen_ref, chosen_here, sems.at[2]),
    ]
    markers = planes_ref.shape[1]
    for copy in copies:
        copy.wait()
    n_chosen = chosen_here.shape[0]
    chosen = chosen_here[...].reshape(1, n_chosen) - lax.axis_index("markers") * markers
    rows = residual_here[...].astype(jnp.float32) * weight_here[...].reshape(1, -1)
    score = None
    for group in range(markers // GROUP):
        span = slice(group * GROUP, (group + 1) * GROUP)
        row = lax.broadcasted_iota(jnp.int32, (GROUP, 1), 0)
        natural = PER_WORD * jnp.bitwise_and(row, LANES - 1) + jnp.right_shift(row, 7) + group * GROUP
        pick = jnp.where(natural == chosen, 1.0, 0.0).astype(jnp.bfloat16)
        pick_ref[span, :] = pick
        high, low = split2(standard(rows, planes_ref, order_ref, span))
        term = dot32(high, pick) + dot32(low, pick)
        score = term if score is None else score + term
    total[...] = score
    width = n_chosen // len(outs)
    for slot, out in enumerate(outs):
        at = pl.multiple_of(group_of(slot, direct) * width, width)
        out[...] = total[:, pl.ds(at, width)]


def trait_scores(planes, order, residuals, weight, chosen, direct):
    people, markers = planes.shape
    r = residuals.shape[0]
    groups = markers // GROUP
    n_chosen = chosen.shape[0]
    out = pl.pallas_call(
        functools.partial(trait_kernel, direct),
        out_shape=tuple(
            jax.ShapeDtypeStruct((r, n_chosen // groups), jnp.float32) for _ in range(groups)
        ) + (jax.ShapeDtypeStruct((markers, n_chosen), jnp.bfloat16),),
        in_specs=[IN_VMEM] * 2 + [IN_HBM] * 3,
        out_specs=(IN_VMEM,) * (groups + 1),
        scratch_shapes=[
            pltpu.VMEM((r, n_chosen), jnp.float32),
            pltpu.VMEM(residuals.shape, residuals.dtype),
            pltpu.VMEM(weight.shape, jnp.float32),
            pltpu.VMEM(chosen.shape, jnp.int32),
            pltpu.SemaphoreType.DMA((3,)),
        ],
        compiler_params=pltpu.CompilerParams(vmem_limit_bytes=VMEM_LIMIT),
        cost_estimate=pl.CostEstimate(flops=2 * 2 * r * people * markers, bytes_accessed=2 * people * markers, transcendentals=0),
        name="traits",
    )(planes, order, residuals, weight, chosen)
    return list(out[:-1]), out[-1]


def product_kernel(
    direct, first_ref, second_ref, planes_ref, order_ref, pick_ref, residual_ref, weight_ref, *refs
):
    outs = refs[:-7]
    gram_ref, sketch_ref, value, score, residual_here, weight_here, sems = refs[-7:]
    copies = [
        start_copy(residual_ref, residual_here, sems.at[0]),
        start_copy(weight_ref, weight_here, sems.at[1]),
    ]
    sketch = first_ref[...] + second_ref[...]
    sketch_ref[...] = sketch
    k = sketch.shape[0]
    for copy in copies:
        copy.wait()
    rows = jnp.concatenate([sketch, residual_here[...].astype(jnp.float32)], axis=0)
    n_rows = rows.shape[0]
    gram_ref[:, :n_rows] = lax.dot_general(
        sketch, rows, (((1,), (1,)), ((), ())), precision=HIGHEST, preferred_element_type=jnp.float32
    )
    gram_ref[:, n_rows:] = jnp.zeros((k, gram_ref.shape[1] - n_rows), jnp.float32)
    rows = sketch * weight_here[...].reshape(1, -1)
    total = None
    for group in range(len(outs)):
        span = slice(group * GROUP, (group + 1) * GROUP)
        piece = standard(rows, planes_ref, order_ref, span)
        value[:, span] = piece
        high, low = split2(piece)
        both = dot32(jnp.concatenate([high, low], axis=0), pick_ref[span, :])
        term = both[:k] + both[k:]
        total = term if total is None else total + term
    score[...] = total
    width = total.shape[1] // len(outs)
    for slot, out in enumerate(outs):
        group = group_of(slot, direct)
        out[:, :GROUP] = value[:, pl.ds(pl.multiple_of(group * GROUP, GROUP), GROUP)]
        out[:, GROUP:] = score[:, pl.ds(pl.multiple_of(group * width, width), width)]


def products(first, second, planes, order, pick, residuals, weight, direct):
    k, people = first.shape
    markers, n_chosen = pick.shape
    groups = markers // GROUP
    out = pl.pallas_call(
        functools.partial(product_kernel, direct),
        out_shape=tuple(
            jax.ShapeDtypeStruct((k, GROUP + n_chosen // groups), jnp.float32) for _ in range(groups)
        ) + (
            jax.ShapeDtypeStruct((k, LANES), jnp.float32),
            jax.ShapeDtypeStruct((k, people), jnp.float32),
        ),
        in_specs=[IN_VMEM] * 5 + [IN_HBM] * 2,
        out_specs=(IN_VMEM,) * (groups + 2),
        scratch_shapes=[
            pltpu.VMEM((k, markers), jnp.float32),
            pltpu.VMEM((k, n_chosen), jnp.float32),
            pltpu.VMEM(residuals.shape, residuals.dtype),
            pltpu.VMEM(weight.shape, jnp.float32),
            pltpu.SemaphoreType.DMA((2,)),
        ],
        compiler_params=pltpu.CompilerParams(vmem_limit_bytes=VMEM_LIMIT),
        name="products",
    )(first, second, planes, order, pick, residuals, weight)
    return list(out[:-2]), out[-2], out[-1]


def eliminate(system, k):
    row_at = lax.broadcasted_iota(jnp.int32, (k, 1), 0)
    for j in range(k):
        pivot = system[j:j + 1, j:j + 1]
        scaled = system[j:j + 1, :] * lax.rsqrt(pivot)
        factor = system[:, j:j + 1] * lax.rsqrt(pivot)
        updated = system - factor * scaled
        system = jnp.where(row_at == j, scaled, jnp.where(row_at > j, updated, system))
    return system


def factor_kernel(root_people, r, sketch_ref, *refs):
    gram_refs, (components_ref, coefficients_ref, system_ref) = refs[:-3], refs[-3:]
    k = sketch_ref.shape[0]
    row_at = lax.broadcasted_iota(jnp.int32, (k, k), 0)
    column_at = lax.broadcasted_iota(jnp.int32, (k, k), 1)
    identity = jnp.where(row_at == column_at, 1.0, 0.0)
    grams = [ref[...] for ref in gram_refs]
    while len(grams) > 1:
        grams = [a + b for a, b in zip(grams[::2], grams[1::2])]
    system = eliminate(jnp.concatenate([grams[0][:, :k + r], identity], axis=1), k)
    system_ref[...] = system
    coefficients_ref[...] = system[:, k:k + r]
    components_ref[...] = root_people * jnp.dot(
        system[:, k + r:], sketch_ref[...], precision=HIGHEST, preferred_element_type=jnp.float32
    )


def factor(root_people, r, sketch, grams):
    k, people = sketch.shape
    return pl.pallas_call(
        functools.partial(factor_kernel, root_people, r),
        out_shape=(
            jax.ShapeDtypeStruct(sketch.shape, jnp.float32),
            jax.ShapeDtypeStruct((k, r), jnp.float32),
            jax.ShapeDtypeStruct((k, 2 * k + r), jnp.float32),
        ),
        in_specs=[IN_VMEM] * (1 + len(grams)),
        out_specs=(IN_VMEM,) * 3,
        compiler_params=pltpu.CompilerParams(vmem_limit_bytes=VMEM_LIMIT),
        name="factor",
    )(sketch, *grams)


def finish_kernel(root_people, r, digit_order, system_ref, *refs):
    count = (len(refs) - 2) // 2
    parts, scores = refs[:count], refs[count:2 * count]
    next_ref, out_ref = refs[2 * count:]
    k = system_ref.shape[0]
    coefficients = system_ref[:, k:k + r]
    inverse = system_ref[:, k + r:]
    total, score = parts[0][...], scores[0][...]
    for ref in parts[1:]:
        total = total + ref[...]
    for ref in scores[1:]:
        score = score + ref[...]
    solved = jnp.dot(inverse, total, precision=HIGHEST, preferred_element_type=jnp.float32)
    width = next_ref.shape[1]
    basis = solved[:, :width]
    if digit_order:
        order = to_natural_order()
        high, middle, low = split3(basis)
        basis = dot32(high, order) + dot32(middle, order) + dot32(low, order)
    next_ref[...] = basis
    removed = lax.dot_general(
        coefficients, solved[:, width:], (((0,), (0,)), ((), ())),
        precision=HIGHEST, preferred_element_type=jnp.float32,
    )
    out_ref[...] = (score - removed) * (1.0 / root_people)


def finish(root_people, r, digit_order, system, parts, scores):
    k = system.shape[0]
    width = scores[0].shape[1]
    return pl.pallas_call(
        functools.partial(finish_kernel, root_people, r, digit_order),
        out_shape=(
            jax.ShapeDtypeStruct((k, parts[0].shape[1] - width), jnp.float32),
            jax.ShapeDtypeStruct((r, width), jnp.float32),
        ),
        in_specs=[IN_VMEM] * (1 + len(parts) + len(scores)),
        out_specs=(IN_VMEM,) * 2,
        compiler_params=pltpu.CompilerParams(vmem_limit_bytes=VMEM_LIMIT),
        name="finish",
    )(system, *parts, *scores)


def shards(genotype, allele_freq, person_weight, basis, residuals, block_markers):
    people, words = genotype.shape
    markers = words * PER_WORD
    k, r = basis.shape[0], residuals.shape[0]
    marker_count = lax.axis_size("markers")
    people_count = lax.axis_size("people")
    groups = markers // GROUP
    direct = people_count == groups and groups == 4
    sketch, order, planes = sketch_partial(genotype, allele_freq, person_weight, basis, people // 4)
    apart = 1
    while apart * 2 < marker_count:
        sketch = sketch + from_partner(sketch, "markers", apart)
        apart *= 2
    other = from_partner(sketch, "markers", apart)
    scores, pick = trait_scores(planes, order, residuals, person_weight, block_markers, direct)
    if direct:
        scores = scores[:1] + [from_partner(scores[i], "people", i) for i in range(1, groups)]
    parts, gram, sketch = products(sketch, other, planes, order, pick, residuals, person_weight, direct)
    if direct:
        grams = [gram] + [from_partner(gram, "people", i) for i in range(1, groups)]
        parts = parts[:1] + [from_partner(parts[i], "people", i) for i in range(1, groups)]
    else:
        value = jnp.stack([part[:, :GROUP] for part in parts], axis=1)
        value = value.reshape(k, groups, PER_WORD, LANES).swapaxes(2, 3).reshape(k, markers)
        projected = jnp.concatenate([part[:, GROUP:] for part in parts], axis=1)
        score = jnp.concatenate(scores, axis=1)
        value, projected, score, gram = lax.psum((value, projected, score, gram), "people")
        index = lax.axis_index("people")

        def own(whole):
            width = whole.shape[1] // people_count
            return lax.dynamic_slice_in_dim(whole, index * width, width, 1)
        parts = [jnp.concatenate([own(value), own(projected)], axis=1)]
        scores, grams = [own(score)], [gram]
    root_people = math.sqrt(people * people_count)
    components, coefficients, system = factor(root_people, r, sketch, grams)
    basis_own, score_own = finish(root_people, r, direct, system, parts, scores)
    return components, coefficients, basis_own[None], score_own[None]


def solution(mesh):
    placed = (
        P(("cohort", "people"), "markers"),
        P(("cohort", "markers")),
        P(("cohort", "people")),
        P("cohort", "markers"),
        P("cohort", "people"),
        P("markers"),
    )
    return jax.shard_map(
        shards,
        mesh=mesh,
        in_specs=placed,
        out_specs=(
            P("cohort", "people"),
            P("cohort", None),
            P("markers", "cohort", "people"),
            P("markers", "cohort", "people"),
        ),
        check_vma=False,
    )
```

time: 46.5 us -> 44.7 us (0.961)
  starting transfers between devices: 7.94 us -> 19.7 us
  waiting for transfers between devices: 16.2 us -> 4.99 us
  local copies, waits for them, and re-layouts: 7.45 us -> 4.19 us
  Pallas kernels: 13.7 us -> 14.8 us
    ppermute x5 -> x11, starting transfers between devices: 7.94 us -> 19.7 us  [from_partner(): return lax.ppermute(block, axis, route)]
    ppermute x5 -> x11, waiting for transfers between devices: 16.2 us -> 4.99 us  [from_partner(): return lax.ppermute(block, axis, route)]
    unnamed x24 -> x14, local copies, waits for them, and re-layouts: 6.66 us -> 4.19 us
    broadcast_in_dim x1 -> x0, local copies, waits for them, and re-layouts: 0.71 us -> none  [shards(): weight = person_weight[None, :]]
    pallas_call x2 -> x4, Pallas kernels: 9.48 us -> 10.2 us  [the longest x1 3.74 us: factor(): pl.pallas_call(functools.partial(factor_kernel, root_people, r), out_shap...]
  transfers between devices with their start and end apart: 5 -> 11, of which waited for: 4 -> 4; matrix products, arithmetic and copies ran while one was open for 0% -> 0% of each run, Pallas kernels for 0% -> 20%
where the time goes in v2:
time: 44.7 us; the launch traced here: 44.4 us
  starting transfers between devices  19.7 us (44%)
  Pallas kernels  14.8 us (33%)
  waiting for transfers between devices  4.99 us (11%)
  local copies, waits for them, and re-layouts  4.19 us (9%)
  between operations  0.7 us (2%)
    ppermute x11, starting transfers between devices, from_partner(): return lax.ppermute(block, axis, route)  19.7 us
    ppermute x11, waiting for transfers between devices, from_partner(): return lax.ppermute(block, axis, route)  4.99 us
    pallas_call x1, Pallas kernels, sketch_partial(): pl.pallas_call(functools.partial(sketch_kernel, chunk), out_shape=(jax.Sh...  4.58 us
    unnamed x14, local copies, waits for them, and re-layouts  4.19 us
    pallas_call x1, Pallas kernels, factor(): pl.pallas_call(functools.partial(factor_kernel, root_people, r), out_shap...  3.74 us
    pallas_call x1, Pallas kernels, trait_scores(): pl.pallas_call(functools.partial(trait_kernel, direct), out_shape=tuple((...  2.74 us
    pallas_call x1, Pallas kernels, products(): pl.pallas_call(functools.partial(product_kernel, direct), out_shape=tuple...  2.38 us
    pallas_call x1, Pallas kernels, finish(): pl.pallas_call(functools.partial(finish_kernel, root_people, r, digit_ord...  1.31 us
  transfers between devices with their start and end apart: 11, of which 4 were waited for; matrix products, arithmetic and copies ran while one was open for 0% of the time, Pallas kernels for 20%

profile of v2, /device:TPU:0, one launch (start us, length us, event | category | flops | bytes accessed | tf_op | source)
XLA Modules:
  0.0 44.4 jit_solution(6426310041831516669)
XLA Ops:
  0.6 0.0 copy-start
  0.6 1.9 %copy-done = s32[1536,512]{1,0:T(8,128)S(1)} copy-done((s32[1536,512]{1,0:T(8,128)S(1)}, s32[1536,512]{1,0:T(8,128)}, u32[]{:S(2)}) %copy-start) | copy-done | bytes 3145752
  2.5 0.0 copy-start.2
  2.5 0.9 %copy-done.2 = bf16[32,2048]{1,0:T(8,128)(2,1)S(1)} copy-done((bf16[32,2048]{1,0:T(8,128)(2,1)S(1)}, bf16[32,2048]{1,0:T(8,128)(2,1)}, u32[]{:S(2)}) %copy-start.2) | copy-done | bytes 131096
  3.4 0.0 copy-start.3
  3.4 0.7 %copy-done.3 = f32[1536]{0:T(1024)S(1)} copy-done((f32[1536]{0:T(1024)S(1)}, f32[1536]{0:T(1024)}, u32[]{:S(2)}) %copy-start.3) | copy-done | bytes 6168
  4.1 0.0 copy-start.5
  4.1 0.7 %copy-done.5 = f32[2048]{0:T(1024)S(1)} copy-done((f32[2048]{0:T(1024)S(1)}, f32[2048]{0:T(1024)}, u32[]{:S(2)}) %copy-start.5) | copy-done | bytes 8216
  4.8 0.0 copy-start.1
  4.8 0.0 copy-start.4
  4.8 0.0 copy-start.6
  4.8 4.6 %sketch.1 = (f32[32,1536]{1,0:T(8,128)S(1)}, f32[8,2048]{1,0:T(8,128)S(1)}, bf16[1536,2048]{1,0:T(8,128)(2,1)S(1)}) custom-call(s32[1536,512]{1,0:T(8,128)S(1)} %copy-done, f32[2048]{0:T(1024)S(1)} %copy-done.5, f32[1536]{0:T(1024)S(1)} %copy-done.3, bf16[32,2048]{1,0:T(8,128)(2,1)S(1)} %copy-done.2), custom_call_target="tpu_custom_call" | custom-call | tf_op jit(solution)/shard_map/sketch/pallas_call | solution.py:134
  9.4 0.5 %collective-permute-start = (f32[32,1536]{1,0:T(8,128)S(1)}, f32[32,1536]{1,0:T(8,128)S(1)}, u32[]{:S(2)}, u32[]{:S(2)}) collective-permute-start(f32[32,1536]{1,0:T(8,128)S(1)} %get-tuple-element.23), channel_id=1, source_target_pairs={{0,1},{1,0},{2,3},{3,2},{4,5},{5,4},{6,7},{7,6},{8,9},{9,8},{10,11... | collective-permute-start | bytes 589832 | tf_op jit(solution)/shard_map/ppermute | solution.py:23
  9.9 1.1 %collective-permute-done = f32[32,1536]{1,0:T(8,128)S(1)} collective-permute-done((f32[32,1536]{1,0:T(8,128)S(1)}, f32[32,1536]{1,0:T(8,128)S(1)}, u32[]{:S(2)}, u32[]{:S(2)}) %collective-permute-start) | collective-permute-done | bytes 196640 | tf_op jit(solution)/shard_map/ppermute | solution.py:23
  11.0 2.9 %collective-permute-start.1 = (f32[32,1536]{1,0:T(8,128)S(1)}, f32[32,1536]{1,0:T(8,128)S(1)}, u32[]{:S(2)}, u32[]{:S(2)}) collective-permute-start(f32[32,1536]{1,0:T(8,128)S(1)} %add.3.first_ref), channel_id=1, source_target_pairs={{0,2},{1,3},{2,0},{3,1},{4,6},{5,7},{6,4},{7,5},{8,10},{9,11},{10,... | collective-permute-start | bytes 589832 | tf_op jit(solution)/shard_map/ppermute | solution.py:23
  14.0 0.0 copy-done.1
  14.0 0.0 copy-done.4
  14.0 0.0 copy-done.6
  14.0 2.7 %traits.1 = (f32[64,128]{1,0:T(8,128)S(1)}, f32[64,128]{1,0:T(8,128)S(1)}, f32[64,128]{1,0:T(8,128)S(1)}, f32[64,128]{1,0:T(8,128)S(1)}, bf16[2048,512]{1,0:T(8,128)(2,1)S(1)}) custom-call(bf16[1536,2048]{1,0:T(8,128)(2,1)S(1)} %get-tuple-element.24.planes_ref, f32[8,2048]{1,0:T(8,128)S(1)} %get-tuple-element.25.order_ref, bf16[64,1536]{1,0:T(8,128)(2,1)S(1)} %copy-done.1, ...), custom_call_target="tpu_custom_call" | custom-call | flops 805306368 | bytes 6291456 | tf_op jit(solution)/shard_map/traits/pallas_call | solution.py:201
  16.7 1.6 %collective-permute-start.8 = (f32[64,128]{1,0:T(8,128)S(1)}, f32[64,128]{1,0:T(8,128)S(1)}, u32[]{:S(2)}, u32[]{:S(2)}) collective-permute-start(f32[64,128]{1,0:T(8,128)S(1)} %get-tuple-element.37), channel_id=1, source_target_pairs={{0,4},{4,0},{8,12},{12,8},{1,5},{5,1},{9,13},{13,9},{2,6},{6,2},{1... | collective-permute-start | bytes 98312 | tf_op jit(solution)/shard_map/ppermute | solution.py:23
  18.4 0.8 %collective-permute-done.1.second_ref = f32[32,1536]{1,0:T(8,128)S(1)} collective-permute-done((f32[32,1536]{1,0:T(8,128)S(1)}, f32[32,1536]{1,0:T(8,128)S(1)}, u32[]{:S(2)}, u32[]{:S(2)}) %collective-permute-start.1) | collective-permute-done | bytes 196640 | tf_op jit(solution)/shard_map/ppermute | solution.py:23
  19.2 2.4 %products.1 = (f32[32,640]{1,0:T(8,128)S(1)}, f32[32,640]{1,0:T(8,128)S(1)}, f32[32,640]{1,0:T(8,128)S(1)}, f32[32,640]{1,0:T(8,128)S(1)}, f32[32,128]{1,0:T(8,128)S(1)}, /*index=5*/f32[32,1536]{1,0:T(8,128)S(1)}) custom-call(f32[32,1536]{1,0:T(8,128)S(1)} %add.3.first_ref, f32[32,1536]{1,0:T(8,128)S(1)} %collective-permute-done.1.second_ref, ...), custom_call_target="tpu_custom_call" | custom-call | tf_op jit(solution)/shard_map/products/pallas_call | solution.py:264
  21.6 1.9 %collective-permute-start.5 = (f32[32,640]{1,0:T(8,128)S(1)}, f32[32,640]{1,0:T(8,128)S(1)}, u32[]{:S(2)}, u32[]{:S(2)}) collective-permute-start(f32[32,640]{1,0:T(8,128)S(1)} %get-tuple-element.33), channel_id=1, source_target_pairs={{0,4},{4,0},{8,12},{12,8},{1,5},{5,1},{9,13},{13,9},{2,6},{6,2},{1... | collective-permute-start | bytes 245768 | tf_op jit(solution)/shard_map/ppermute | solution.py:23
  23.4 2.6 %collective-permute-start.6 = (f32[32,640]{1,0:T(8,128)S(1)}, f32[32,640]{1,0:T(8,128)S(1)}, u32[]{:S(2)}, u32[]{:S(2)}) collective-permute-start(f32[32,640]{1,0:T(8,128)S(1)} %get-tuple-element.34), channel_id=1, source_target_pairs={{0,8},{4,12},{8,0},{12,4},{1,9},{5,13},{9,1},{13,5},{2,10},{6,14},... | collective-permute-start | bytes 245768 | tf_op jit(solution)/shard_map/ppermute | solution.py:23
  26.0 0.0 collective-permute-start.7
  26.0 3.8 %collective-permute-start.4 = (f32[32,128]{1,0:T(8,128)S(1)}, f32[32,128]{1,0:T(8,128)S(1)}, u32[]{:S(2)}, u32[]{:S(2)}) collective-permute-start(f32[32,128]{1,0:T(8,128)S(1)} %get-tuple-element.28.refs_0_), channel_id=1, source_target_pairs={{0,12},{4,8},{8,4},{12,0},{1,13},{5,9},{9,5},{13,1},{2,14},{6,10},... | collective-permute-start | bytes 49160 | tf_op jit(solution)/shard_map/ppermute | solution.py:23
  29.9 0.0 collective-permute-done.8.refs_5_
  29.9 0.0 collective-permute-start.3
  29.9 2.7 %collective-permute-done.4.refs_3_ = f32[32,128]{1,0:T(8,128)S(1)} collective-permute-done((f32[32,128]{1,0:T(8,128)S(1)}, f32[32,128]{1,0:T(8,128)S(1)}, u32[]{:S(2)}, u32[]{:S(2)}) %collective-permute-start.4) | collective-permute-done | bytes 16416 | tf_op jit(solution)/shard_map/ppermute | solution.py:23
  32.6 2.2 %collective-permute-start.2 = (f32[32,128]{1,0:T(8,128)S(1)}, f32[32,128]{1,0:T(8,128)S(1)}, u32[]{:S(2)}, u32[]{:S(2)}) collective-permute-start(f32[32,128]{1,0:T(8,128)S(1)} %get-tuple-element.28.refs_0_), channel_id=1, source_target_pairs={{0,4},{4,0},{8,12},{12,8},{1,5},{5,1},{9,13},{13,9},{2,6},{6,2},{1... | collective-permute-start | bytes 49160 | tf_op jit(solution)/shard_map/ppermute | solution.py:23
  34.8 0.0 collective-permute-done.3.refs_2_
  34.8 1.3 %collective-permute-start.9 = (f32[64,128]{1,0:T(8,128)S(1)}, f32[64,128]{1,0:T(8,128)S(1)}, u32[]{:S(2)}, u32[]{:S(2)}) collective-permute-start(f32[64,128]{1,0:T(8,128)S(1)} %get-tuple-element.38), channel_id=1, source_target_pairs={{0,8},{4,12},{8,0},{12,4},{1,9},{5,13},{9,1},{13,5},{2,10},{6,14},... | collective-permute-start | bytes 98312 | tf_op jit(solution)/shard_map/ppermute | solution.py:23
  36.1 0.4 collective-permute-done.2.refs_1_
  36.5 2.8 %collective-permute-start.10 = (f32[64,128]{1,0:T(8,128)S(1)}, f32[64,128]{1,0:T(8,128)S(1)}, u32[]{:S(2)}, u32[]{:S(2)}) collective-permute-start(f32[64,128]{1,0:T(8,128)S(1)} %get-tuple-element.39), channel_id=1, source_target_pairs={{0,12},{4,8},{8,4},{12,0},{1,13},{5,9},{9,5},{13,1},{2,14},{6,10},... | collective-permute-start | bytes 98312 | tf_op jit(solution)/shard_map/ppermute | solution.py:23
  39.3 3.7 %factor.1 = (f32[32,1536]{1,0:T(8,128)}, f32[32,64]{1,0:T(8,128)}, f32[32,128]{1,0:T(8,128)S(1)}) custom-call(f32[32,1536]{1,0:T(8,128)S(1)} %get-tuple-element.27.sketch_ref, f32[32,128]{1,0:T(8,128)S(1)} %get-tuple-element.28.refs_0_, f32[32,128]{1,0:T(8,128)S(1)} %collective-permute-done.2.refs_1_, f32[32,128]{1,0:T(8,128)S(1)} %collective-permute-done.3.refs_2_, ...), custom_call_target="tpu_custom_call" | custom-call | tf_op jit(solution)/shard_map/factor/pallas_call | solution.py:317
  43.0 0.0 collective-permute-done.9.refs_6_
  43.0 0.0 collective-permute-done.10.refs_7_
  43.1 0.0 collective-permute-done.5.refs_1_
  43.1 0.0 collective-permute-done.6.refs_2_
  43.1 0.0 collective-permute-done.7.refs_3_
  43.1 1.3 %finish.1 = (f32[32,512]{1,0:T(8,128)}, f32[64,128]{1,0:T(8,128)}) custom-call(f32[32,128]{1,0:T(8,128)S(1)} %get-tuple-element.31.system_ref, f32[32,640]{1,0:T(8,128)S(1)} %get-tuple-element.32.refs_0_, f32[32,640]{1,0:T(8,128)S(1)} %collective-permute-done.5.refs_1_, f32[32,640]{1,0:T(8,128)S(1)} %collective-permute-done.6.refs_2_, ...), custom_call_target="tpu_custom_call" | custom-call | tf_op jit(solution)/shard_map/finish/pallas_call | solution.py:361
  (1 shorter events, 0.0 us)
Async XLA Ops:
  0.6 1.9 %copy-start = (s32[1536,512]{1,0:T(8,128)S(1)}, s32[1536,512]{1,0:T(8,128)}, u32[]{:S(2)}) copy-start(s32[1536,512]{1,0:T(8,128)} %words_ref.1) | copy-start | bytes 9437188
  2.5 0.9 %copy-start.2 = (bf16[32,2048]{1,0:T(8,128)(2,1)S(1)}, bf16[32,2048]{1,0:T(8,128)(2,1)}, u32[]{:S(2)}) copy-start(bf16[32,2048]{1,0:T(8,128)(2,1)} %basis_ref.1) | copy-start | bytes 393220
  3.4 0.7 %copy-start.3 = (f32[1536]{0:T(1024)S(1)}, f32[1536]{0:T(1024)}, u32[]{:S(2)}) copy-start(f32[1536]{0:T(1024)} %weight_ref.5) | copy-start | bytes 18436
  4.1 0.7 %copy-start.5 = (f32[2048]{0:T(1024)S(1)}, f32[2048]{0:T(1024)}, u32[]{:S(2)}) copy-start(f32[2048]{0:T(1024)} %freq_ref.1) | copy-start | bytes 24580
  4.8 9.1 %copy-start.1 = (bf16[64,1536]{1,0:T(8,128)(2,1)S(1)}, bf16[64,1536]{1,0:T(8,128)(2,1)}, u32[]{:S(2)}) copy-start(bf16[64,1536]{1,0:T(8,128)(2,1)} %residual_ref.3) | copy-start | bytes 589828
  4.8 9.1 %copy-start.4 = (f32[1536]{0:T(1024)S(1)}, f32[1536]{0:T(1024)}, u32[]{:S(2)}) copy-start(f32[1536]{0:T(1024)} %weight_ref.5) | copy-start | bytes 18436
  4.8 9.1 %copy-start.6 = (s32[512]{0:T(512)S(1)}, s32[512]{0:T(512)}, u32[]{:S(2)}) copy-start(s32[512]{0:T(512)} %chosen_ref.1) | copy-start | bytes 6148
  9.4 1.6 %collective-permute-start = (f32[32,1536]{1,0:T(8,128)S(1)}, f32[32,1536]{1,0:T(8,128)S(1)}, u32[]{:S(2)}, u32[]{:S(2)}) collective-permute-start(f32[32,1536]{1,0:T(8,128)S(1)} %get-tuple-element.23), channel_id=1, source_target_pairs={{0,1},{1,0},{2,3},{3,2},{4,5},{5,4},{6,7},{7,6},{8,9},{9,8},{10,11... | collective-permute-start | bytes 589832 | tf_op jit(solution)/shard_map/ppermute | solution.py:23
  11.0 8.1 %collective-permute-start.1 = (f32[32,1536]{1,0:T(8,128)S(1)}, f32[32,1536]{1,0:T(8,128)S(1)}, u32[]{:S(2)}, u32[]{:S(2)}) collective-permute-start(f32[32,1536]{1,0:T(8,128)S(1)} %add.3.first_ref), channel_id=1, source_target_pairs={{0,2},{1,3},{2,0},{3,1},{4,6},{5,7},{6,4},{7,5},{8,10},{9,11},{10,... | collective-permute-start | bytes 589832 | tf_op jit(solution)/shard_map/ppermute | solution.py:23
  16.7 13.2 %collective-permute-start.8 = (f32[64,128]{1,0:T(8,128)S(1)}, f32[64,128]{1,0:T(8,128)S(1)}, u32[]{:S(2)}, u32[]{:S(2)}) collective-permute-start(f32[64,128]{1,0:T(8,128)S(1)} %get-tuple-element.37), channel_id=1, source_target_pairs={{0,4},{4,0},{8,12},{12,8},{1,5},{5,1},{9,13},{13,9},{2,6},{6,2},{1... | collective-permute-start | bytes 98312 | tf_op jit(solution)/shard_map/ppermute | solution.py:23
  21.6 21.5 %collective-permute-start.5 = (f32[32,640]{1,0:T(8,128)S(1)}, f32[32,640]{1,0:T(8,128)S(1)}, u32[]{:S(2)}, u32[]{:S(2)}) collective-permute-start(f32[32,640]{1,0:T(8,128)S(1)} %get-tuple-element.33), channel_id=1, source_target_pairs={{0,4},{4,0},{8,12},{12,8},{1,5},{5,1},{9,13},{13,9},{2,6},{6,2},{1... | collective-permute-start | bytes 245768 | tf_op jit(solution)/shard_map/ppermute | solution.py:23
  23.4 19.6 %collective-permute-start.6 = (f32[32,640]{1,0:T(8,128)S(1)}, f32[32,640]{1,0:T(8,128)S(1)}, u32[]{:S(2)}, u32[]{:S(2)}) collective-permute-start(f32[32,640]{1,0:T(8,128)S(1)} %get-tuple-element.34), channel_id=1, source_target_pairs={{0,8},{4,12},{8,0},{12,4},{1,9},{5,13},{9,1},{13,5},{2,10},{6,14},... | collective-permute-start | bytes 245768 | tf_op jit(solution)/shard_map/ppermute | solution.py:23
  26.0 17.0 %collective-permute-start.7 = (f32[32,640]{1,0:T(8,128)S(1)}, f32[32,640]{1,0:T(8,128)S(1)}, u32[]{:S(2)}, u32[]{:S(2)}) collective-permute-start(f32[32,640]{1,0:T(8,128)S(1)} %get-tuple-element.35), channel_id=1, source_target_pairs={{0,12},{4,8},{8,4},{12,0},{1,13},{5,9},{9,5},{13,1},{2,14},{6,10},... | collective-permute-start | bytes 245768 | tf_op jit(solution)/shard_map/ppermute | solution.py:23
  26.0 6.5 %collective-permute-start.4 = (f32[32,128]{1,0:T(8,128)S(1)}, f32[32,128]{1,0:T(8,128)S(1)}, u32[]{:S(2)}, u32[]{:S(2)}) collective-permute-start(f32[32,128]{1,0:T(8,128)S(1)} %get-tuple-element.28.refs_0_), channel_id=1, source_target_pairs={{0,12},{4,8},{8,4},{12,0},{1,13},{5,9},{9,5},{13,1},{2,14},{6,10},... | collective-permute-start | bytes 49160 | tf_op jit(solution)/shard_map/ppermute | solution.py:23
  29.9 4.9 %collective-permute-start.3 = (f32[32,128]{1,0:T(8,128)S(1)}, f32[32,128]{1,0:T(8,128)S(1)}, u32[]{:S(2)}, u32[]{:S(2)}) collective-permute-start(f32[32,128]{1,0:T(8,128)S(1)} %get-tuple-element.28.refs_0_), channel_id=1, source_target_pairs={{0,8},{4,12},{8,0},{12,4},{1,9},{5,13},{9,1},{13,5},{2,10},{6,14},... | collective-permute-start | bytes 49160 | tf_op jit(solution)/shard_map/ppermute | solution.py:23
  32.6 3.9 %collective-permute-start.2 = (f32[32,128]{1,0:T(8,128)S(1)}, f32[32,128]{1,0:T(8,128)S(1)}, u32[]{:S(2)}, u32[]{:S(2)}) collective-permute-start(f32[32,128]{1,0:T(8,128)S(1)} %get-tuple-element.28.refs_0_), channel_id=1, source_target_pairs={{0,4},{4,0},{8,12},{12,8},{1,5},{5,1},{9,13},{13,9},{2,6},{6,2},{1... | collective-permute-start | bytes 49160 | tf_op jit(solution)/shard_map/ppermute | solution.py:23
  34.8 8.3 %collective-permute-start.9 = (f32[64,128]{1,0:T(8,128)S(1)}, f32[64,128]{1,0:T(8,128)S(1)}, u32[]{:S(2)}, u32[]{:S(2)}) collective-permute-start(f32[64,128]{1,0:T(8,128)S(1)} %get-tuple-element.38), channel_id=1, source_target_pairs={{0,8},{4,12},{8,0},{12,4},{1,9},{5,13},{9,1},{13,5},{2,10},{6,14},... | collective-permute-start | bytes 98312 | tf_op jit(solution)/shard_map/ppermute | solution.py:23
  36.5 6.6 %collective-permute-start.10 = (f32[64,128]{1,0:T(8,128)S(1)}, f32[64,128]{1,0:T(8,128)S(1)}, u32[]{:S(2)}, u32[]{:S(2)}) collective-permute-start(f32[64,128]{1,0:T(8,128)S(1)} %get-tuple-element.39), channel_id=1, source_target_pairs={{0,12},{4,8},{8,4},{12,0},{1,13},{5,9},{9,5},{13,1},{2,14},{6,10},... | collective-permute-start | bytes 98312 | tf_op jit(solution)/shard_map/ppermute | solution.py:23

commit v3 on v0

v3 whole, which is shorter than its diff:
```python
import functools
import math

import jax
import jax.numpy as jnp
from jax import lax
from jax.experimental import pallas as pl
from jax.experimental.pallas import tpu as pltpu
from jax.sharding import PartitionSpec as P

LANES = 128
PER_WORD = 4
GROUP = LANES * PER_WORD
VMEM_LIMIT = 40 * 1024 * 1024
HIGHEST = lax.Precision.HIGHEST
IN_VMEM = pl.BlockSpec(memory_space=pltpu.VMEM)


def from_partner(block, axis, apart):
    count = lax.axis_size(axis)
    route = [(low, low ^ apart) for low in range(count)]
    return lax.ppermute(block, axis, route)


def split2(value):
    high = value.astype(jnp.bfloat16)
    low = (value - high.astype(jnp.float32)).astype(jnp.bfloat16)
    return high, low


def split3(value):
    high, rest = value.astype(jnp.bfloat16), None
    rest = value - high.astype(jnp.float32)
    middle, low = split2(rest)
    return high, middle, low


def digits(words):
    out = []
    for j in range(PER_WORD):
        one = jnp.bitwise_and(jnp.right_shift(words, 2 * j), 3)
        out.append(one.astype(jnp.bfloat16))
    return out


def natural_of_column(shape):
    column = lax.broadcasted_iota(jnp.int32, shape, len(shape) - 1)
    return PER_WORD * jnp.bitwise_and(column, LANES - 1) + jnp.right_shift(column, 7)


def to_digit_order():
    row = lax.broadcasted_iota(jnp.int32, (GROUP, GROUP), 0)
    column = natural_of_column((1, GROUP))
    return jnp.where(row == column, 1.0, 0.0).astype(jnp.bfloat16)


def to_natural_order():
    row = lax.broadcasted_iota(jnp.int32, (GROUP, GROUP), 0)
    natural = PER_WORD * jnp.bitwise_and(row, LANES - 1) + jnp.right_shift(row, 7)
    column = lax.broadcasted_iota(jnp.int32, (GROUP, GROUP), 1)
    return jnp.where(natural == column, 1.0, 0.0).astype(jnp.bfloat16)


def dot32(a, b):
    return jnp.dot(a, b, preferred_element_type=jnp.float32)


def group_of(slot, direct):
    return jnp.bitwise_xor(lax.axis_index("people"), slot) if direct else slot


def sketch_kernel(chunk, scaled_ref, shifted_ref, *refs):
    planes_refs, out_ref = refs[:-1], refs[-1]
    k, markers = scaled_ref.shape
    people = out_ref.shape[1]
    offset = jnp.sum(shifted_ref[...], axis=1, keepdims=True)
    order = to_digit_order()
    stacked = jnp.concatenate(split2(scaled_ref[...]), axis=0)
    pieces = [[] for _ in range(PER_WORD)]
    for group in range(markers // GROUP):
        moved = dot32(stacked[:, group * GROUP:(group + 1) * GROUP], order).astype(jnp.bfloat16)
        for j in range(PER_WORD):
            pieces[j].append(moved[:, j * LANES:(j + 1) * LANES])
    arranged = [jnp.concatenate(pieces[j], axis=1) for j in range(PER_WORD)]
    for at in range(0, people, chunk):
        total = None
        for j in range(PER_WORD):
            term = lax.dot_general(
                arranged[j], planes_refs[j][at:at + chunk, :], (((1,), (1,)), ((), ())),
                preferred_element_type=jnp.float32,
            )
            total = term if total is None else total + term
        out_ref[:, at:at + chunk] = total[:k] + total[k:] - offset


def sketch_partial(scaled, shifted, planes, chunk):
    return pl.pallas_call(
        functools.partial(sketch_kernel, chunk),
        out_shape=jax.ShapeDtypeStruct((scaled.shape[0], planes[0].shape[0]), jnp.float32),
        in_specs=[IN_VMEM] * (2 + len(planes)),
        out_specs=IN_VMEM,
        compiler_params=pltpu.CompilerParams(vmem_limit_bytes=VMEM_LIMIT),
        name="sketch",
    )(scaled, shifted, *planes)


def standard(rows, planes_refs, freq, group):
    n_rows = rows.shape[0]
    row_sum = jnp.sum(rows, axis=1, keepdims=True)
    at = group * LANES
    planes = jnp.concatenate([ref[:, at:at + LANES] for ref in planes_refs], axis=1)
    raw = dot32(jnp.concatenate(split2(rows), axis=0), planes)
    return (raw[:n_rows] + raw[n_rows:] - row_sum * (2.0 * freq)) * lax.rsqrt(2.0 * freq * (1.0 - freq))


def trait_kernel(direct, freq_ref, residual_ref, weight_ref, chosen_ref, *refs):
    planes_refs, outs = refs[:PER_WORD], refs[PER_WORD:-3]
    order_ref, pick_ref, total = refs[-3:]
    markers, n_chosen = pick_ref.shape
    chosen = chosen_ref[...].reshape(1, n_chosen) - lax.axis_index("markers") * markers
    rows = residual_ref[...].astype(jnp.float32) * weight_ref[...].reshape(1, -1)
    freq = jnp.broadcast_to(freq_ref[...].reshape(1, markers), (8, markers))
    freq = jnp.concatenate(split3(freq), axis=0)
    order = to_digit_order()
    score = None
    for group in range(markers // GROUP):
        span = slice(group * GROUP, (group + 1) * GROUP)
        row = lax.broadcasted_iota(jnp.int32, (GROUP, 1), 0)
        natural = PER_WORD * jnp.bitwise_and(row, LANES - 1) + jnp.right_shift(row, 7) + group * GROUP
        pick = jnp.where(natural == chosen, 1.0, 0.0).astype(jnp.bfloat16)
        pick_ref[span, :] = pick
        moved = dot32(freq[:, span], order)
        moved = moved[:8] + moved[8:16] + moved[16:]
        order_ref[:, span] = moved
        high, low = split2(standard(rows, planes_refs, moved[0:1], group))
        term = dot32(high, pick) + dot32(low, pick)
        score = term if score is None else score + term
    total[...] = score
    width = n_chosen // len(outs)
    for slot, out in enumerate(outs):
        at = pl.multiple_of(group_of(slot, direct) * width, width)
        out[...] = total[:, pl.ds(at, width)]


def trait_scores(planes, freq, residuals, weight, chosen, direct):
    people, words = planes[0].shape
    markers = words * PER_WORD
    r = residuals.shape[0]
    groups = markers // GROUP
    n_chosen = chosen.shape[0]
    out = pl.pallas_call(
        functools.partial(trait_kernel, direct),
        out_shape=tuple(
            jax.ShapeDtypeStruct((r, n_chosen // groups), jnp.float32) for _ in range(groups)
        ) + (
            jax.ShapeDtypeStruct((8, markers), jnp.float32),
            jax.ShapeDtypeStruct((markers, n_chosen), jnp.bfloat16),
        ),
        in_specs=[IN_VMEM] * (4 + len(planes)),
        out_specs=(IN_VMEM,) * (groups + 2),
        scratch_shapes=[pltpu.VMEM((r, n_chosen), jnp.float32)],
        compiler_params=pltpu.CompilerParams(vmem_limit_bytes=VMEM_LIMIT),
        cost_estimate=pl.CostEstimate(flops=2 * 2 * r * people * markers, bytes_accessed=2 * people * markers, transcendentals=0),
        name="traits",
    )(freq, residuals, weight, chosen, *planes)
    return out[:-2], out[-2], out[-1]


def product_kernel(direct, first_ref, second_ref, order_ref, pick_ref, residual_ref, weight_ref, *refs):
    planes_refs, refs = refs[:PER_WORD], refs[PER_WORD:]
    sketch_ref, value, score = refs[-3:]
    groups = (len(refs) - 3) // 2
    trait_refs, outs = refs[:groups], refs[groups:2 * groups]
    weight = weight_ref[...].reshape(1, -1)
    sketch = (first_ref[...] + second_ref[...]) * weight
    sketch_ref[...] = sketch
    k = sketch.shape[0]
    rows = sketch * weight
    total = None
    for group in range(groups):
        span = slice(group * GROUP, (group + 1) * GROUP)
        piece = standard(rows, planes_refs, order_ref[0:1, span], group)
        value[:, span] = piece
        both = dot32(jnp.concatenate(split2(piece), axis=0), pick_ref[span, :])
        term = both[:k] + both[k:]
        total = term if total is None else total + term
    score[...] = total
    rows = jnp.concatenate([sketch, residual_ref[...].astype(jnp.float32)], axis=0)
    gram = lax.dot_general(
        sketch, rows, (((1,), (1,)), ((), ())), precision=HIGHEST, preferred_element_type=jnp.float32
    )
    width = total.shape[1] // groups
    for slot, out in enumerate(outs):
        group = group_of(slot, direct)
        at = GROUP
        out[:, :at] = value[:, pl.ds(pl.multiple_of(group * GROUP, GROUP), GROUP)]
        out[:, at:at + width] = score[:, pl.ds(pl.multiple_of(group * width, width), width)]
        at += width
        for first in range(0, trait_refs[slot].shape[0], k):
            out[:, at:at + width] = trait_refs[slot][first:first + k, :]
            at += width
        out[:, at:at + gram.shape[1]] = gram
        if at + gram.shape[1] < out.shape[1]:
            out[:, at + gram.shape[1]:] = jnp.zeros((k, out.shape[1] - at - gram.shape[1]), jnp.float32)


def products(first, second, order, pick, residuals, weight, planes, traits, direct):
    k, people = first.shape
    markers, n_chosen = pick.shape
    groups = markers // GROUP
    r, width = traits[0].shape
    gram_room = -(-(k + r) // LANES) * LANES
    out = pl.pallas_call(
        functools.partial(product_kernel, direct),
        out_shape=tuple(
            jax.ShapeDtypeStruct((k, GROUP + width + r // k * width + gram_room), jnp.float32)
            for _ in range(groups)
        ) + (jax.ShapeDtypeStruct((k, people), jnp.float32),),
        in_specs=[IN_VMEM] * (6 + len(planes) + groups),
        out_specs=(IN_VMEM,) * (groups + 1),
        scratch_shapes=[
            pltpu.VMEM((k, markers), jnp.float32),
            pltpu.VMEM((k, n_chosen), jnp.float32),
        ],
        compiler_params=pltpu.CompilerParams(vmem_limit_bytes=VMEM_LIMIT),
        name="products",
    )(first, second, order, pick, residuals, weight, *planes, *traits)
    return list(out[:-1]), out[-1]


def eliminate(system, k):
    row_at = lax.broadcasted_iota(jnp.int32, (k, 1), 0)
    shape = system.shape
    block = 8
    for start in range(0, k, block):
        columns = [
            jnp.broadcast_to(system[:, j:j + 1], shape) for j in range(start, start + block)
        ]
        for t in range(block):
            j = start + t
            inverse = lax.rsqrt(columns[t][j:j + 1, :])
            factor = columns[t] * inverse
            for s in range(t + 1, block):
                columns[s] = columns[s] - factor * factor[start + s:start + s + 1, :]
            scaled = system[j:j + 1, :] * inverse
            updated = system - factor * scaled
            system = jnp.where(row_at == j, scaled, jnp.where(row_at > j, updated, system))
    return system


def finish_kernel(root_people, k, r, width, score_width, digit_order, sketch_ref, *refs):
    parts, (components_ref, coefficients_ref, next_ref, out_ref) = refs[:-4], refs[-4:]
    row_at = lax.broadcasted_iota(jnp.int32, (k, k), 0)
    column_at = lax.broadcasted_iota(jnp.int32, (k, k), 1)
    identity = jnp.where(row_at == column_at, 1.0, 0.0)
    totals = [ref[...] for ref in parts]
    while len(totals) > 1:
        totals = [a + b for a, b in zip(totals[::2], totals[1::2])]
    total = totals[0]
    traits_at = width + score_width
    gram_at = traits_at + r // k * score_width
    system = eliminate(jnp.concatenate([total[:, gram_at:gram_at + k + r], identity], axis=1), k)
    coefficients = system[:, k:k + r]
    inverse = system[:, k + r:]
    coefficients_ref[...] = coefficients
    components_ref[...] = root_people * jnp.dot(
        inverse, sketch_ref[...], precision=HIGHEST, preferred_element_type=jnp.float32
    )
    solved = jnp.dot(
        inverse, total[:, :traits_at], precision=HIGHEST, preferred_element_type=jnp.float32
    )
    basis = solved[:, :width]
    if digit_order:
        both = dot32(jnp.concatenate(split2(basis), axis=0), to_natural_order())
        basis = both[:k] + both[k:]
    next_ref[...] = basis
    removed = lax.dot_general(
        coefficients, solved[:, width:], (((0,), (0,)), ((), ())),
        precision=HIGHEST, preferred_element_type=jnp.float32,
    )
    for i in range(r // k):
        at = traits_at + i * score_width
        out_ref[i * k:(i + 1) * k, :] = (
            total[:, at:at + score_width] - removed[i * k:(i + 1) * k]
        ) * (1.0 / root_people)


def finish(root_people, r, width, score_width, digit_order, sketch, parts):
    k = sketch.shape[0]
    return pl.pallas_call(
        functools.partial(finish_kernel, root_people, k, r, width, score_width, digit_order),
        out_shape=(
            jax.ShapeDtypeStruct(sketch.shape, jnp.float32),
            jax.ShapeDtypeStruct((k, r), jnp.float32),
            jax.ShapeDtypeStruct((k, width), jnp.float32),
            jax.ShapeDtypeStruct((r, score_width), jnp.float32),
        ),
        in_specs=[IN_VMEM] * (1 + len(parts)),
        out_specs=(IN_VMEM,) * 4,
        compiler_params=pltpu.CompilerParams(vmem_limit_bytes=VMEM_LIMIT),
        name="finish",
    )(sketch, *parts)


def shards(genotype, allele_freq, person_weight, basis, residuals, block_markers):
    people, words = genotype.shape
    markers = words * PER_WORD
    k, r = basis.shape[0], residuals.shape[0]
    marker_count = lax.axis_size("markers")
    people_count = lax.axis_size("people")
    groups = markers // GROUP
    direct = people_count == groups and groups == 4
    score_width = block_markers.shape[0] // people_count
    planes = digits(genotype)
    scaled = basis.astype(jnp.float32) * lax.rsqrt(2.0 * allele_freq * (1.0 - allele_freq))[None, :]
    shifted = scaled * (2.0 * allele_freq)[None, :]
    sketch = sketch_partial(scaled, shifted, planes, people // 4)
    apart = 1
    while apart * 2 < marker_count:
        sketch = sketch + from_partner(sketch, "markers", apart)
        apart *= 2
    other = from_partner(sketch, "markers", apart)
    traits, order, pick = trait_scores(
        planes, allele_freq, residuals, person_weight, block_markers, direct
    )
    parts, sketch = products(
        sketch, other, order, pick, residuals, person_weight, planes, traits, direct
    )
    if direct:
        parts = parts[:1] + [from_partner(parts[i], "people", i) for i in range(1, groups)]
    else:
        part_width = block_markers.shape[0] // groups
        whole = jnp.stack(parts, axis=1)
        value = whole[:, :, :GROUP].reshape(k, groups, PER_WORD, LANES)
        value = value.swapaxes(2, 3).reshape(k, markers)
        ends = [GROUP + i * part_width for i in range(r // k + 2)]
        scores = [whole[:, :, at:at + part_width].reshape(k, -1) for at in ends[:-1]]
        total = lax.psum((value, scores, parts[0][:, ends[-1]:]), "people")
        index = lax.axis_index("people")

        def own(array):
            width = array.shape[1] // people_count
            return lax.dynamic_slice_in_dim(array, index * width, width, 1)
        parts = [jnp.concatenate([own(total[0])] + [own(one) for one in total[1]] + [total[2]], axis=1)]
    components, coefficients, basis_own, score_own = finish(
        math.sqrt(people * people_count), r, markers // people_count, score_width, direct, sketch, parts
    )
    return components, coefficients, basis_own[None], score_own[None]


def solution(mesh):
    placed = (
        P(("cohort", "people"), "markers"),
        P(("cohort", "markers")),
        P(("cohort", "people")),
        P("cohort", "markers"),
        P("cohort", "people"),
        P("markers"),
    )
    return jax.shard_map(
        shards,
        mesh=mesh,
        in_specs=placed,
        out_specs=(
            P("cohort", "people"),
            P("cohort", None),
            P("markers", "cohort", "people"),
            P("markers", "cohort", "people"),
        ),
        check_vma=False,
    )
```

time: 227 us -> 36.5 us (0.16)
  blocking collectives: 57.6 us -> 0 us
  waiting for transfers between devices: 67.5 us -> 13.3 us
  local copies, waits for them, and re-layouts: 35.2 us -> 0.03 us
  other arithmetic: 31.6 us -> 4.19 us
  matrix products: 16 us -> 0 us
  between operations: 14.3 us -> 0.72 us
  Pallas kernels: 0 us -> 10.2 us
  starting transfers between devices: 4.36 us -> 7.9 us
    psum x2 -> x0, waiting for transfers between devices: 61.4 us -> none  [the longest x1 34.2 us: shards(): lax.psum((basis_partial, score_partial), 'people')]
    psum x1 -> x0, blocking collectives: 57.6 us -> none  [shards(): lax.psum(jnp.dot(ortho_share, own_residual.T, precision=lax.Precision.HIG...]
    shift_right_arithmetic x4 -> x0, local copies, waits for them, and re-layouts: 21.1 us -> none  [decode(): jnp.right_shift(packed[:, :, None], shifts[None, None, :])]
    another operation x17 -> x0, other arithmetic: 21.1 us -> none  [the longest x12 14.4 us: shards(): factor_up = jnp.linalg.cholesky(combined).T]
    dot_general x14 -> x0, matrix products: 14.1 us -> none  [the longest x1 5.42 us: shards(): jnp.dot(ortho_half, weighted, preferred_element_type=jnp.float32)]
    pallas_call x0 -> x4, Pallas kernels: none -> 10.2 us  [the longest x1 3.12 us: products(): pl.pallas_call(functools.partial(product_kernel, direct), out_shape=tuple...]
    ppermute x4 -> x5, waiting for transfers between devices: 6.08 us -> 13.3 us  [from_partner(): return lax.ppermute(block, axis, route)]
    gather x1 -> x0, local copies, waits for them, and re-layouts: 7.19 us -> none  [shards(): chosen = jnp.take(weighted, columns, axis=1)]
  transfers between devices with their start and end apart: 6 -> 5, of which waited for: 6 -> 4; matrix products, arithmetic and copies ran while one was open for 5% -> 0% of each run, Pallas kernels for 0% -> 8%
where the time goes in v3:
time: 36.5 us; the launch traced here: 36.3 us
  waiting for transfers between devices  13.3 us (36%)
  Pallas kernels  10.2 us (28%)
  starting transfers between devices  7.9 us (22%)
  other arithmetic  4.19 us (11%)
  between operations  0.72 us (2%)
    ppermute x5, waiting for transfers between devices, from_partner(): return lax.ppermute(block, axis, route)  13.3 us
    ppermute x5, starting transfers between devices, from_partner(): return lax.ppermute(block, axis, route)  7.9 us
    convert_element_type x1, other arithmetic, digits(): out.append(one.astype(jnp.bfloat16))  3.41 us
    pallas_call x1, Pallas kernels, products(): pl.pallas_call(functools.partial(product_kernel, direct), out_shape=tuple...  3.12 us
    pallas_call x1, Pallas kernels, trait_scores(): pl.pallas_call(functools.partial(trait_kernel, direct), out_shape=tuple((...  2.77 us
    pallas_call x1, Pallas kernels, sketch_partial(): pl.pallas_call(functools.partial(sketch_kernel, chunk), out_shape=jax.Sha...  2.24 us
    pallas_call x1, Pallas kernels, finish(): pl.pallas_call(functools.partial(finish_kernel, root_people, k, r, width,...  2.06 us
  transfers between devices with their start and end apart: 5, of which 4 were waited for; matrix products, arithmetic and copies ran while one was open for 0% of the time, Pallas kernels for 8%

profile of v3, /device:TPU:0, one launch (start us, length us, event | category | flops | bytes accessed | tf_op | source)
XLA Modules:
  0.0 36.3 jit_solution(15229143846099633800)
XLA Ops:
  0.6 0.7 %broadcast_multiply_fusion.1 = (f32[2048]{0:T(1024)S(1)}, f32[2048]{0:T(1024)S(1)}) fusion(f32[2048]{0:T(1024)} %freq_ref.1), kind=kLoop, calls=%fused_computation.7 | loop fusion | flops 6144 | bytes 24576 | tf_op jit(solution)/shard_map/mul | solution.py:315
  1.3 0.0 copy-start.4
  1.3 3.4 %and_convert_fusion = (bf16[1536,512]{1,0:T(8,128)(2,1)S(1)}, bf16[1536,512]{1,0:T(8,128)(2,1)S(1)}, bf16[1536,512]{1,0:T(8,128)(2,1)S(1)}, bf16[1536,512]{1,0:T(8,128)(2,1)S(1)}) fusion(s32[1536,512]{1,0:T(8,128)} %param.6), kind=kLoop, calls=%fused_computation | loop fusion | flops 9437184 | bytes 9437184 | tf_op jit(solution)/shard_map/convert_element_type | solution.py:42
  4.8 0.0 copy-done.4
  4.8 0.0 copy-start
  4.8 0.0 copy-start.1
  4.8 0.0 copy-start.2
  4.8 0.0 copy-start.3
  4.9 2.2 %sketch.1 = f32[32,1536]{1,0:T(8,128)S(1)} custom-call(f32[32,2048]{1,0:T(8,128)S(1)} %get-tuple-element.39.scaled_ref, f32[32,2048]{1,0:T(8,128)S(1)} %get-tuple-element.38.shifted_ref, bf16[1536,512]{1,0:T(8,128)(2,1)S(1)} %get-tuple-element.36.refs_0_, bf16[1536,512]{1,0:T(8,128)(2,1)S(1)} %get-tuple-element.35.refs_1_, ...), custom_call_target="tpu_custom_call" | custom-call | tf_op jit(solution)/shard_map/sketch/pallas_call | solution.py:97
  7.1 0.5 %collective-permute-start = (f32[32,1536]{1,0:T(8,128)S(1)}, f32[32,1536]{1,0:T(8,128)S(1)}, u32[]{:S(2)}, u32[]{:S(2)}) collective-permute-start(f32[32,1536]{1,0:T(8,128)S(1)} %sketch.1), channel_id=1, source_target_pairs={{0,1},{1,0},{2,3},{3,2},{4,5},{5,4},{6,7},{7,6},{8,9},{9,8},{10,11... | collective-permute-start | bytes 589832 | tf_op jit(solution)/shard_map/ppermute | solution.py:22
  7.6 1.1 %collective-permute-done = f32[32,1536]{1,0:T(8,128)S(1)} collective-permute-done((f32[32,1536]{1,0:T(8,128)S(1)}, f32[32,1536]{1,0:T(8,128)S(1)}, u32[]{:S(2)}, u32[]{:S(2)}) %collective-permute-start) | collective-permute-done | bytes 196640 | tf_op jit(solution)/shard_map/ppermute | solution.py:22
  8.7 2.9 %collective-permute-start.1 = (f32[32,1536]{1,0:T(8,128)S(1)}, f32[32,1536]{1,0:T(8,128)S(1)}, u32[]{:S(2)}, u32[]{:S(2)}) collective-permute-start(f32[32,1536]{1,0:T(8,128)S(1)} %add.3.first_ref), channel_id=1, source_target_pairs={{0,2},{1,3},{2,0},{3,1},{4,6},{5,7},{6,4},{7,5},{8,10},{9,11},{10,... | collective-permute-start | bytes 589832 | tf_op jit(solution)/shard_map/ppermute | solution.py:22
  11.6 0.0 copy-done
  11.6 0.0 copy-done.1
  11.6 0.0 copy-done.2
  11.6 0.0 copy-done.3
  11.6 2.8 %traits.1 = (f32[64,128]{1,0:T(8,128)S(1)}, f32[64,128]{1,0:T(8,128)S(1)}, f32[64,128]{1,0:T(8,128)S(1)}, f32[64,128]{1,0:T(8,128)S(1)}, f32[8,2048]{1,0:T(8,128)S(1)}, /*index=5*/bf16[2048,512]{1,0:T(8,128)(2,1)S(1)}) custom-call(f32[2048]{0:T(1024)S(1)} %copy-done.1, bf16[64,1536]{1,0:T(8,128)(2,1)S(1)} %copy-done, f32[1536]{0:T(1024)S(1)} %copy-done.2, ...), custom_call_target="tpu_custom_call" | custom-call | flops 805306368 | bytes 6291456 | tf_op jit(solution)/shard_map/traits/pallas_call | solution.py:151
  14.4 2.4 %collective-permute-done.1.second_ref = f32[32,1536]{1,0:T(8,128)S(1)} collective-permute-done((f32[32,1536]{1,0:T(8,128)S(1)}, f32[32,1536]{1,0:T(8,128)S(1)}, u32[]{:S(2)}, u32[]{:S(2)}) %collective-permute-start.1) | collective-permute-done | bytes 196640 | tf_op jit(solution)/shard_map/ppermute | solution.py:22
  16.8 3.1 %products.1 = (f32[32,1024]{1,0:T(8,128)S(1)}, f32[32,1024]{1,0:T(8,128)S(1)}, f32[32,1024]{1,0:T(8,128)S(1)}, f32[32,1024]{1,0:T(8,128)S(1)}, f32[32,1536]{1,0:T(8,128)S(1)}) custom-call(f32[32,1536]{1,0:T(8,128)S(1)} %add.3.first_ref, f32[32,1536]{1,0:T(8,128)S(1)} %collective-permute-done.1.second_ref, f32[8,2048]{1,0:T(8,128)S(1)} %get-tuple-element.19.order_ref, ...), custom_call_target="tpu_custom_call" | custom-call | tf_op jit(solution)/shard_map/products/pallas_call | solution.py:213
  20.0 1.9 %collective-permute-start.2 = (f32[32,1024]{1,0:T(8,128)S(1)}, f32[32,1024]{1,0:T(8,128)S(1)}, u32[]{:S(2)}, u32[]{:S(2)}) collective-permute-start(f32[32,1024]{1,0:T(8,128)S(1)} %get-tuple-element.27), channel_id=1, source_target_pairs={{0,4},{4,0},{8,12},{12,8},{1,5},{5,1},{9,13},{13,9},{2,6},{6,2},{1... | collective-permute-start | bytes 393224 | tf_op jit(solution)/shard_map/ppermute | solution.py:22
  21.8 2.6 %collective-permute-start.3 = (f32[32,1024]{1,0:T(8,128)S(1)}, f32[32,1024]{1,0:T(8,128)S(1)}, u32[]{:S(2)}, u32[]{:S(2)}) collective-permute-start(f32[32,1024]{1,0:T(8,128)S(1)} %get-tuple-element.28), channel_id=1, source_target_pairs={{0,8},{4,12},{8,0},{12,4},{1,9},{5,13},{9,1},{13,5},{2,10},{6,14},... | collective-permute-start | bytes 393224 | tf_op jit(solution)/shard_map/ppermute | solution.py:22
  24.4 0.0 collective-permute-start.4
  24.4 2.0 %collective-permute-done.2.refs_1_ = f32[32,1024]{1,0:T(8,128)S(1)} collective-permute-done((f32[32,1024]{1,0:T(8,128)S(1)}, f32[32,1024]{1,0:T(8,128)S(1)}, u32[]{:S(2)}, u32[]{:S(2)}) %collective-permute-start.2) | collective-permute-done | bytes 131104 | tf_op jit(solution)/shard_map/ppermute | solution.py:22
  26.5 7.8 %collective-permute-done.3.refs_2_ = f32[32,1024]{1,0:T(8,128)S(1)} collective-permute-done((f32[32,1024]{1,0:T(8,128)S(1)}, f32[32,1024]{1,0:T(8,128)S(1)}, u32[]{:S(2)}, u32[]{:S(2)}) %collective-permute-start.3) | collective-permute-done | bytes 131104 | tf_op jit(solution)/shard_map/ppermute | solution.py:22
  34.2 0.0 collective-permute-done.4.refs_3_
  34.2 2.1 %finish.1 = (f32[32,1536]{1,0:T(8,128)}, f32[32,64]{1,0:T(8,128)}, f32[32,512]{1,0:T(8,128)}, f32[64,128]{1,0:T(8,128)}) custom-call(f32[32,1536]{1,0:T(8,128)S(1)} %get-tuple-element.25.sketch_ref, f32[32,1024]{1,0:T(8,128)S(1)} %get-tuple-element.26.refs_0_, f32[32,1024]{1,0:T(8,128)S(1)} %collective-permute-done.2.refs_1_, ...), custom_call_target="tpu_custom_call" | custom-call | tf_op jit(solution)/shard_map/finish/pallas_call | solution.py:290
  (2 shorter events, 0.1 us)
Async XLA Ops:
  1.3 3.4 %copy-start.4 = (bf16[32,2048]{1,0:T(8,128)(2,1)S(1)}, bf16[32,2048]{1,0:T(8,128)(2,1)}, u32[]{:S(2)}) copy-start(bf16[32,2048]{1,0:T(8,128)(2,1)} %param.9) | copy-start | bytes 393220
  4.8 6.8 %copy-start = (bf16[64,1536]{1,0:T(8,128)(2,1)S(1)}, bf16[64,1536]{1,0:T(8,128)(2,1)}, u32[]{:S(2)}) copy-start(bf16[64,1536]{1,0:T(8,128)(2,1)} %residual_ref.3) | copy-start | bytes 589828
  4.8 6.8 %copy-start.1 = (f32[2048]{0:T(1024)S(1)}, f32[2048]{0:T(1024)}, u32[]{:S(2)}) copy-start(f32[2048]{0:T(1024)} %freq_ref.1) | copy-start | bytes 24580
  4.8 6.8 %copy-start.2 = (f32[1536]{0:T(1024)S(1)}, f32[1536]{0:T(1024)}, u32[]{:S(2)}) copy-start(f32[1536]{0:T(1024)} %weight_ref.3) | copy-start | bytes 18436
  4.8 6.8 %copy-start.3 = (s32[512]{0:T(512)S(1)}, s32[512]{0:T(512)}, u32[]{:S(2)}) copy-start(s32[512]{0:T(512)} %chosen_ref.1) | copy-start | bytes 6148
  7.1 1.6 %collective-permute-start = (f32[32,1536]{1,0:T(8,128)S(1)}, f32[32,1536]{1,0:T(8,128)S(1)}, u32[]{:S(2)}, u32[]{:S(2)}) collective-permute-start(f32[32,1536]{1,0:T(8,128)S(1)} %sketch.1), channel_id=1, source_target_pairs={{0,1},{1,0},{2,3},{3,2},{4,5},{5,4},{6,7},{7,6},{8,9},{9,8},{10,11... | collective-permute-start | bytes 589832 | tf_op jit(solution)/shard_map/ppermute | solution.py:22
  8.7 8.1 %collective-permute-start.1 = (f32[32,1536]{1,0:T(8,128)S(1)}, f32[32,1536]{1,0:T(8,128)S(1)}, u32[]{:S(2)}, u32[]{:S(2)}) collective-permute-start(f32[32,1536]{1,0:T(8,128)S(1)} %add.3.first_ref), channel_id=1, source_target_pairs={{0,2},{1,3},{2,0},{3,1},{4,6},{5,7},{6,4},{7,5},{8,10},{9,11},{10,... | collective-permute-start | bytes 589832 | tf_op jit(solution)/shard_map/ppermute | solution.py:22
  20.0 6.5 %collective-permute-start.2 = (f32[32,1024]{1,0:T(8,128)S(1)}, f32[32,1024]{1,0:T(8,128)S(1)}, u32[]{:S(2)}, u32[]{:S(2)}) collective-permute-start(f32[32,1024]{1,0:T(8,128)S(1)} %get-tuple-element.27), channel_id=1, source_target_pairs={{0,4},{4,0},{8,12},{12,8},{1,5},{5,1},{9,13},{13,9},{2,6},{6,2},{1... | collective-permute-start | bytes 393224 | tf_op jit(solution)/shard_map/ppermute | solution.py:22
  21.8 12.4 %collective-permute-start.3 = (f32[32,1024]{1,0:T(8,128)S(1)}, f32[32,1024]{1,0:T(8,128)S(1)}, u32[]{:S(2)}, u32[]{:S(2)}) collective-permute-start(f32[32,1024]{1,0:T(8,128)S(1)} %get-tuple-element.28), channel_id=1, source_target_pairs={{0,8},{4,12},{8,0},{12,4},{1,9},{5,13},{9,1},{13,5},{2,10},{6,14},... | collective-permute-start | bytes 393224 | tf_op jit(solution)/shard_map/ppermute | solution.py:22
  24.4 9.8 %collective-permute-start.4 = (f32[32,1024]{1,0:T(8,128)S(1)}, f32[32,1024]{1,0:T(8,128)S(1)}, u32[]{:S(2)}, u32[]{:S(2)}) collective-permute-start(f32[32,1024]{1,0:T(8,128)S(1)} %get-tuple-element.29), channel_id=1, source_target_pairs={{0,12},{4,8},{8,4},{12,0},{1,13},{5,9},{9,5},{13,1},{2,14},{6,10},... | collective-permute-start | bytes 393224 | tf_op jit(solution)/shard_map/ppermute | solution.py:22

commit v4 on v3

--- a/solution.py
+++ b/solution.py
@@ -104,25 +104,23 @@
     )(scaled, shifted, *planes)
 
 
-def standard(rows, planes_refs, freq, group):
+def standard(rows, planes, freq):
     n_rows = rows.shape[0]
     row_sum = jnp.sum(rows, axis=1, keepdims=True)
-    at = group * LANES
-    planes = jnp.concatenate([ref[:, at:at + LANES] for ref in planes_refs], axis=1)
     raw = dot32(jnp.concatenate(split2(rows), axis=0), planes)
     return (raw[:n_rows] + raw[n_rows:] - row_sum * (2.0 * freq)) * lax.rsqrt(2.0 * freq * (1.0 - freq))
 
 
 def trait_kernel(direct, freq_ref, residual_ref, weight_ref, chosen_ref, *refs):
-    planes_refs, outs = refs[:PER_WORD], refs[PER_WORD:-3]
-    order_ref, pick_ref, total = refs[-3:]
+    planes_refs, outs = refs[:PER_WORD], refs[PER_WORD:-5]
+    order_ref, chosen_freq_ref, gathered_ref, pick_ref, total = refs[-5:]
+    people = gathered_ref.shape[0]
     markers, n_chosen = pick_ref.shape
     chosen = chosen_ref[...].reshape(1, n_chosen) - lax.axis_index("markers") * markers
-    rows = residual_ref[...].astype(jnp.float32) * weight_ref[...].reshape(1, -1)
     freq = jnp.broadcast_to(freq_ref[...].reshape(1, markers), (8, markers))
     freq = jnp.concatenate(split3(freq), axis=0)
     order = to_digit_order()
-    score = None
+    chosen_freq = None
     for group in range(markers // GROUP):
         span = slice(group * GROUP, (group + 1) * GROUP)
         row = lax.broadcasted_iota(jnp.int32, (GROUP, 1), 0)
@@ -130,12 +128,21 @@
         pick = jnp.where(natural == chosen, 1.0, 0.0).astype(jnp.bfloat16)
         pick_ref[span, :] = pick
         moved = dot32(freq[:, span], order)
-        moved = moved[:8] + moved[8:16] + moved[16:]
-        order_ref[:, span] = moved
-        high, low = split2(standard(rows, planes_refs, moved[0:1], group))
-        term = dot32(high, pick) + dot32(low, pick)
-        score = term if score is None else score + term
-    total[...] = score
+        order_ref[:, span] = moved[:8] + moved[8:16] + moved[16:]
+        term = dot32(moved.astype(jnp.bfloat16), pick)
+        chosen_freq = term if chosen_freq is None else chosen_freq + term
+    chosen_freq = chosen_freq[:8] + chosen_freq[8:16] + chosen_freq[16:]
+    chosen_freq_ref[...] = chosen_freq
+    half = people // 2
+    for at in range(0, people, half):
+        rows = slice(at, at + half)
+        planes = jnp.concatenate([
+            ref[rows, group * LANES:(group + 1) * LANES]
+            for group in range(markers // GROUP) for ref in planes_refs
+        ], axis=1)
+        gathered_ref[rows, :] = dot32(planes, pick_ref[...]).astype(jnp.bfloat16)
+    rows = residual_ref[...].astype(jnp.float32) * weight_ref[...].reshape(1, -1)
+    total[...] = standard(rows, gathered_ref[...], chosen_freq[0:1])
     width = n_chosen // len(outs)
     for slot, out in enumerate(outs):
         at = pl.multiple_of(group_of(slot, direct) * width, width)
@@ -154,78 +161,117 @@
             jax.ShapeDtypeStruct((r, n_chosen // groups), jnp.float32) for _ in range(groups)
         ) + (
             jax.ShapeDtypeStruct((8, markers), jnp.float32),
-            jax.ShapeDtypeStruct((markers, n_chosen), jnp.bfloat16),
+            jax.ShapeDtypeStruct((8, n_chosen), jnp.float32),
+            jax.ShapeDtypeStruct((people, n_chosen), jnp.bfloat16),
         ),
         in_specs=[IN_VMEM] * (4 + len(planes)),
-        out_specs=(IN_VMEM,) * (groups + 2),
-        scratch_shapes=[pltpu.VMEM((r, n_chosen), jnp.float32)],
+        out_specs=(IN_VMEM,) * (groups + 3),
+        scratch_shapes=[
+            pltpu.VMEM((markers, n_chosen), jnp.bfloat16),
+            pltpu.VMEM((r, n_chosen), jnp.float32),
+        ],
         compiler_params=pltpu.CompilerParams(vmem_limit_bytes=VMEM_LIMIT),
-        cost_estimate=pl.CostEstimate(flops=2 * 2 * r * people * markers, bytes_accessed=2 * people * markers, transcendentals=0),
+        cost_estimate=pl.CostEstimate(flops=2 * n_chosen * people * markers, bytes_accessed=2 * people * markers, transcendentals=0),
         name="traits",
     )(freq, residuals, weight, chosen, *planes)
-    return out[:-2], out[-2], out[-1]
-
-
-def product_kernel(direct, first_ref, second_ref, order_ref, pick_ref, residual_ref, weight_ref, *refs):
-    planes_refs, refs = refs[:PER_WORD], refs[PER_WORD:]
-    sketch_ref, value, score = refs[-3:]
-    groups = (len(refs) - 3) // 2
-    trait_refs, outs = refs[:groups], refs[groups:2 * groups]
-    weight = weight_ref[...].reshape(1, -1)
-    sketch = (first_ref[...] + second_ref[...]) * weight
-    sketch_ref[...] = sketch
+    return out[:-3], out[-3], out[-2], out[-1]
+
+
+def gram_of(sketch, residual):
     k = sketch.shape[0]
-    rows = sketch * weight
-    total = None
-    for group in range(groups):
-        span = slice(group * GROUP, (group + 1) * GROUP)
-        piece = standard(rows, planes_refs, order_ref[0:1, span], group)
-        value[:, span] = piece
-        both = dot32(jnp.concatenate(split2(piece), axis=0), pick_ref[span, :])
-        term = both[:k] + both[k:]
-        total = term if total is None else total + term
-    score[...] = total
-    rows = jnp.concatenate([sketch, residual_ref[...].astype(jnp.float32)], axis=0)
-    gram = lax.dot_general(
-        sketch, rows, (((1,), (1,)), ((), ())), precision=HIGHEST, preferred_element_type=jnp.float32
-    )
-    width = total.shape[1] // groups
-    for slot, out in enumerate(outs):
+    parts = jnp.concatenate(split3(sketch), axis=0)
+    raw = lax.dot_general(
+        parts, jnp.concatenate([parts, residual], axis=0), (((1,), (1,)), ((), ())),
+        preferred_element_type=jnp.float32,
+    )
+    block = [[raw[i * k:(i + 1) * k, j * k:(j + 1) * k] for j in range(3)] for i in range(3)]
+    small = (block[0][2] + block[2][0]) + block[1][1]
+    own = block[0][0] + ((block[0][1] + block[1][0]) + small)
+    cross = raw[:k, 3 * k:] + (raw[k:2 * k, 3 * k:] + raw[2 * k:, 3 * k:])
+    return jnp.concatenate([own, cross], axis=1)
+
+
+def write_messages(direct, slots, outs, rows, order_ref, chosen_freq_ref, gathered_ref, planes_refs, trait_refs, gram):
+    groups = order_ref.shape[1] // GROUP
+    width = gathered_ref.shape[1] // groups
+    k = rows.shape[0]
+    for slot, out, traits in zip(slots, outs, trait_refs):
         group = group_of(slot, direct)
-        at = GROUP
-        out[:, :at] = value[:, pl.ds(pl.multiple_of(group * GROUP, GROUP), GROUP)]
-        out[:, at:at + width] = score[:, pl.ds(pl.multiple_of(group * width, width), width)]
-        at += width
-        for first in range(0, trait_refs[slot].shape[0], k):
-            out[:, at:at + width] = trait_refs[slot][first:first + k, :]
+        words_at = pl.ds(pl.multiple_of(group * LANES, LANES), LANES)
+        markers_at = pl.ds(pl.multiple_of(group * GROUP, GROUP), GROUP)
+        scores_at = pl.ds(pl.multiple_of(group * width, width), width)
+        planes = jnp.concatenate(
+            [ref[:, words_at] for ref in planes_refs] + [gathered_ref[:, scores_at]], axis=1
+        )
+        freq = jnp.concatenate([order_ref[0:1, markers_at], chosen_freq_ref[0:1, scores_at]], axis=1)
+        at = GROUP + width
+        out[:, :at] = standard(rows, planes, freq)
+        for first in range(0, traits.shape[0], k):
+            out[:, at:at + width] = traits[first:first + k, :]
             at += width
         out[:, at:at + gram.shape[1]] = gram
         if at + gram.shape[1] < out.shape[1]:
             out[:, at + gram.shape[1]:] = jnp.zeros((k, out.shape[1] - at - gram.shape[1]), jnp.float32)
 
 
-def products(first, second, order, pick, residuals, weight, planes, traits, direct):
-    k, people = first.shape
-    markers, n_chosen = pick.shape
-    groups = markers // GROUP
+def far_kernel(direct, slots, first_ref, second_ref, residual_ref, weight_ref, order_ref, chosen_freq_ref, gathered_ref, *refs):
+    planes_refs, refs = refs[:PER_WORD], refs[PER_WORD:]
+    n = len(slots)
+    trait_refs, outs, (sketch_ref, gram_ref) = refs[:n], refs[n:2 * n], refs[2 * n:]
+    weight = weight_ref[...].reshape(1, -1)
+    sketch = (first_ref[...] + second_ref[...]) * weight
+    sketch_ref[...] = sketch
+    gram = gram_of(sketch, residual_ref[...])
+    gram_ref[...] = gram
+    write_messages(
+        direct, slots, outs, sketch * weight, order_ref, chosen_freq_ref, gathered_ref, planes_refs, trait_refs, gram
+    )
+
+
+def near_kernel(direct, slots, sketch_ref, gram_ref, weight_ref, order_ref, chosen_freq_ref, gathered_ref, *refs):
+    planes_refs, refs = refs[:PER_WORD], refs[PER_WORD:]
+    n = len(slots)
+    write_messages(
+        direct, slots, refs[n:], sketch_ref[...] * weight_ref[...].reshape(1, -1),
+        order_ref, chosen_freq_ref, gathered_ref, planes_refs, refs[:n], gram_ref[...],
+    )
+
+
+def product_call(kernel, name, slots, inputs, common, planes, traits, more, direct):
+    order, chosen_freq, gathered = common
+    people, n_chosen = gathered.shape
+    groups = order.shape[1] // GROUP
+    k = inputs[0].shape[0]
     r, width = traits[0].shape
     gram_room = -(-(k + r) // LANES) * LANES
-    out = pl.pallas_call(
-        functools.partial(product_kernel, direct),
-        out_shape=tuple(
-            jax.ShapeDtypeStruct((k, GROUP + width + r // k * width + gram_room), jnp.float32)
-            for _ in range(groups)
-        ) + (jax.ShapeDtypeStruct((k, people), jnp.float32),),
-        in_specs=[IN_VMEM] * (6 + len(planes) + groups),
-        out_specs=(IN_VMEM,) * (groups + 1),
-        scratch_shapes=[
-            pltpu.VMEM((k, markers), jnp.float32),
-            pltpu.VMEM((k, n_chosen), jnp.float32),
-        ],
+    message = jax.ShapeDtypeStruct((k, GROUP + width + r // k * width + gram_room), jnp.float32)
+    operands = (*inputs, *common, *planes, *[traits[slot] for slot in slots])
+    out_shape = (message,) * len(slots) + more
+    columns = len(slots) * (GROUP + width)
+    return pl.pallas_call(
+        functools.partial(kernel, direct, slots),
+        out_shape=out_shape,
+        in_specs=[IN_VMEM] * len(operands),
+        out_specs=(IN_VMEM,) * len(out_shape),
         compiler_params=pltpu.CompilerParams(vmem_limit_bytes=VMEM_LIMIT),
-        name="products",
-    )(first, second, order, pick, residuals, weight, *planes, *traits)
-    return list(out[:-1]), out[-1]
+        cost_estimate=pl.CostEstimate(flops=4 * k * people * columns, bytes_accessed=2 * people * columns, transcendentals=0),
+        name=name,
+    )(*operands)
+
+
+def products(first, second, residuals, weight, common, planes, traits, direct):
+    k, people = first.shape
+    gram = jax.ShapeDtypeStruct((k, k + residuals.shape[0]), jnp.float32)
+    slots = tuple(range(len(traits)))
+    near, far = slots[:2], slots[2:]
+    out = product_call(
+        far_kernel, "far", far, (first, second, residuals, weight), common, planes, traits,
+        (jax.ShapeDtypeStruct((k, people), jnp.float32), gram), direct,
+    )
+    parts, sketch, gram = out[:-2], out[-2], out[-1]
+    return [*product_call(
+        near_kernel, "near", near, (sketch, gram, weight), common, planes, traits, (), direct
+    ), *parts], sketch
 
 
 def eliminate(system, k):
@@ -320,14 +366,15 @@
         sketch = sketch + from_partner(sketch, "markers", apart)
         apart *= 2
     other = from_partner(sketch, "markers", apart)
-    traits, order, pick = trait_scores(
+    traits, *common = trait_scores(
         planes, allele_freq, residuals, person_weight, block_markers, direct
     )
     parts, sketch = products(
-        sketch, other, order, pick, residuals, person_weight, planes, traits, direct
+        sketch, other, residuals, person_weight, common, planes, traits, direct
     )
     if direct:
-        parts = parts[:1] + [from_partner(parts[i], "people", i) for i in range(1, groups)]
+        moved = {i: from_partner(parts[i], "people", i) for i in range(groups - 1, 0, -1)}
+        parts = [moved[2], moved[3], moved[1], parts[0]]
     else:
         part_width = block_markers.shape[0] // groups
         whole = jnp.stack(parts, axis=1)

time: 36.5 us -> 33.6 us (0.921)
  waiting for transfers between devices: 13.3 us -> 9.8 us
  Pallas kernels: 10.2 us -> 10.7 us
    ppermute x5, waiting for transfers between devices: 13.3 us -> 9.8 us  [from_partner(): return lax.ppermute(block, axis, route)]
    pallas_call x1, Pallas kernels: 2.77 us -> 4.67 us  [trait_scores(): pl.pallas_call(functools.partial(trait_kernel, direct), out_shape=tuple((...]
    pallas_call x1 -> x2, Pallas kernels: 3.12 us -> 1.73 us  [product_call(): pl.pallas_call(functools.partial(kernel, direct, slots), out_shape=out_sh...]
  transfers between devices with their start and end apart: 5 -> 5, of which waited for: 4 -> 4; matrix products, arithmetic and copies ran while one was open for 0% -> 0% of each run, Pallas kernels for 8% -> 16%
where the time goes in v4:
time: 33.6 us; the launch traced here: 33.4 us
  Pallas kernels  10.7 us (32%)
  waiting for transfers between devices  9.8 us (29%)
  starting transfers between devices  7.94 us (24%)
  other arithmetic  4.19 us (12%)
  between operations  0.71 us (2%)
    ppermute x5, waiting for transfers between devices, from_partner(): return lax.ppermute(block, axis, route)  9.8 us
    ppermute x5, starting transfers between devices, from_partner(): return lax.ppermute(block, axis, route)  7.94 us
    pallas_call x1, Pallas kernels, trait_scores(): pl.pallas_call(functools.partial(trait_kernel, direct), out_shape=tuple((...  4.67 us
    convert_element_type x1, other arithmetic, digits(): out.append(one.astype(jnp.bfloat16))  3.41 us
    pallas_call x1, Pallas kernels, sketch_partial(): pl.pallas_call(functools.partial(sketch_kernel, chunk), out_shape=jax.Sha...  2.24 us
    pallas_call x1, Pallas kernels, finish(): pl.pallas_call(functools.partial(finish_kernel, root_people, k, r, width,...  2.06 us
    pallas_call x2, Pallas kernels, product_call(): pl.pallas_call(functools.partial(kernel, direct, slots), out_shape=out_sh...  1.73 us
    mul x1, other arithmetic, shards(): 2.0 * allele_freq * (1.0 - allele_freq)  0.71 us
  transfers between devices with their start and end apart: 5, of which 4 were waited for; matrix products, arithmetic and copies ran while one was open for 0% of the time, Pallas kernels for 16%

profile of v4, /device:TPU:0, one launch (start us, length us, event | category | flops | bytes accessed | tf_op | source)
XLA Modules:
  0.0 33.4 jit_solution(14962155537076372646)
XLA Ops:
  0.6 0.7 %broadcast_multiply_fusion.1 = (f32[2048]{0:T(1024)S(1)}, f32[2048]{0:T(1024)S(1)}) fusion(f32[2048]{0:T(1024)} %freq_ref.1), kind=kLoop, calls=%fused_computation.7 | loop fusion | flops 6144 | bytes 24576 | tf_op jit(solution)/shard_map/mul | solution.py:361
  1.3 0.0 copy-start.4
  1.3 3.4 %and_convert_fusion = (bf16[1536,512]{1,0:T(8,128)(2,1)S(1)}, bf16[1536,512]{1,0:T(8,128)(2,1)S(1)}, bf16[1536,512]{1,0:T(8,128)(2,1)S(1)}, bf16[1536,512]{1,0:T(8,128)(2,1)S(1)}) fusion(s32[1536,512]{1,0:T(8,128)} %param.6), kind=kLoop, calls=%fused_computation | loop fusion | flops 9437184 | bytes 9437184 | tf_op jit(solution)/shard_map/convert_element_type | solution.py:42
  4.8 0.0 copy-done.4
  4.8 0.0 copy-start
  4.8 0.0 copy-start.1
  4.8 0.0 copy-start.2
  4.8 0.0 copy-start.3
  4.9 2.2 %sketch.1 = f32[32,1536]{1,0:T(8,128)S(1)} custom-call(f32[32,2048]{1,0:T(8,128)S(1)} %get-tuple-element.43.scaled_ref, f32[32,2048]{1,0:T(8,128)S(1)} %get-tuple-element.42.shifted_ref, bf16[1536,512]{1,0:T(8,128)(2,1)S(1)} %get-tuple-element.40.refs_0_, bf16[1536,512]{1,0:T(8,128)(2,1)S(1)} %get-tuple-element.39.refs_1_, ...), custom_call_target="tpu_custom_call" | custom-call | tf_op jit(solution)/shard_map/sketch/pallas_call | solution.py:97
  7.1 0.5 %collective-permute-start = (f32[32,1536]{1,0:T(8,128)S(1)}, f32[32,1536]{1,0:T(8,128)S(1)}, u32[]{:S(2)}, u32[]{:S(2)}) collective-permute-start(f32[32,1536]{1,0:T(8,128)S(1)} %sketch.1), channel_id=1, source_target_pairs={{0,1},{1,0},{2,3},{3,2},{4,5},{5,4},{6,7},{7,6},{8,9},{9,8},{10,11... | collective-permute-start | bytes 589832 | tf_op jit(solution)/shard_map/ppermute | solution.py:22
  7.6 1.1 %collective-permute-done = f32[32,1536]{1,0:T(8,128)S(1)} collective-permute-done((f32[32,1536]{1,0:T(8,128)S(1)}, f32[32,1536]{1,0:T(8,128)S(1)}, u32[]{:S(2)}, u32[]{:S(2)}) %collective-permute-start) | collective-permute-done | bytes 196640 | tf_op jit(solution)/shard_map/ppermute | solution.py:22
  8.7 2.9 %collective-permute-start.1 = (f32[32,1536]{1,0:T(8,128)S(1)}, f32[32,1536]{1,0:T(8,128)S(1)}, u32[]{:S(2)}, u32[]{:S(2)}) collective-permute-start(f32[32,1536]{1,0:T(8,128)S(1)} %add.3.first_ref), channel_id=1, source_target_pairs={{0,2},{1,3},{2,0},{3,1},{4,6},{5,7},{6,4},{7,5},{8,10},{9,11},{10,... | collective-permute-start | bytes 589832 | tf_op jit(solution)/shard_map/ppermute | solution.py:22
  11.6 0.0 copy-done
  11.6 0.0 copy-done.1
  11.6 0.0 copy-done.2
  11.6 0.0 copy-done.3
  11.6 4.7 %traits.1 = (f32[64,128]{1,0:T(8,128)S(1)}, f32[64,128]{1,0:T(8,128)S(1)}, f32[64,128]{1,0:T(8,128)S(1)}, f32[64,128]{1,0:T(8,128)S(1)}, f32[8,2048]{1,0:T(8,128...) custom-call(f32[2048]{0:T(1024)S(1)} %copy-done.2, bf16[64,1536]{1,0:T(8,128)(2,1)S(1)} %copy-done, ...), custom_call_target="tpu_custom_call" | custom-call | flops 3221225472 | bytes 6291456 | tf_op jit(solution)/shard_map/traits/pallas_call | solution.py:158
  16.3 0.5 %collective-permute-done.1.second_ref = f32[32,1536]{1,0:T(8,128)S(1)} collective-permute-done((f32[32,1536]{1,0:T(8,128)S(1)}, f32[32,1536]{1,0:T(8,128)S(1)}, u32[]{:S(2)}, u32[]{:S(2)}) %collective-permute-start.1) | collective-permute-done | bytes 196640 | tf_op jit(solution)/shard_map/ppermute | solution.py:22
  16.8 0.9 %far.1 = (f32[32,1024]{1,0:T(8,128)S(1)}, f32[32,1024]{1,0:T(8,128)S(1)}, f32[32,1536]{1,0:T(8,128)S(1)}, f32[32,96]{1,0:T(8,128)S(1)}) custom-call(f32[32,1536]{1,0:T(8,128)S(1)} %add.3.first_ref, f32[32,1536]{1,0:T(8,128)S(1)} %collective-permute-done.1.second_ref, bf16[64,1536]{1,0:T(8,128)(2,1)S(1)} %copy-done, f32[1536]{0:T(1024)S(1)} %copy-done.1, ...), custom_call_target="tpu_custom_call" | custom-call | flops 251658240 | bytes 3932160 | tf_op jit(solution)/shard_map/far/pallas_call | solution.py:251
  17.7 2.9 %collective-permute-start.2 = (f32[32,1024]{1,0:T(8,128)S(1)}, f32[32,1024]{1,0:T(8,128)S(1)}, u32[]{:S(2)}, u32[]{:S(2)}) collective-permute-start(f32[32,1024]{1,0:T(8,128)S(1)} %get-tuple-element.27), channel_id=1, source_target_pairs={{0,8},{4,12},{8,0},{12,4},{1,9},{5,13},{9,1},{13,5},{2,10},{6,14},... | collective-permute-start | bytes 393224 | tf_op jit(solution)/shard_map/ppermute | solution.py:22
  20.6 1.4 %collective-permute-start.3 = (f32[32,1024]{1,0:T(8,128)S(1)}, f32[32,1024]{1,0:T(8,128)S(1)}, u32[]{:S(2)}, u32[]{:S(2)}) collective-permute-start(f32[32,1024]{1,0:T(8,128)S(1)} %get-tuple-element.28), channel_id=1, source_target_pairs={{0,12},{4,8},{8,4},{12,0},{1,13},{5,9},{9,5},{13,1},{2,14},{6,10},... | collective-permute-start | bytes 393224 | tf_op jit(solution)/shard_map/ppermute | solution.py:22
  22.0 0.8 %near.1 = (f32[32,1024]{1,0:T(8,128)S(1)}, f32[32,1024]{1,0:T(8,128)S(1)}) custom-call(f32[32,1536]{1,0:T(8,128)S(1)} %get-tuple-element.26.sketch_ref, f32[32,96]{1,0:T(8,128)S(1)} %get-tuple-element.29.gram_ref, f32[1536]{0:T(1024)S(1)} %copy-done.1, f32[8,2048]{1,0:T(8,128)S(1)} %get-tuple-element.21.order_ref, ...), custom_call_target="tpu_custom_call" | custom-call | flops 251658240 | bytes 3932160 | tf_op jit(solution)/shard_map/near/pallas_call | solution.py:251
  22.8 0.3 collective-permute-start.4
  23.1 7.4 %collective-permute-done.2.refs_0_ = f32[32,1024]{1,0:T(8,128)S(1)} collective-permute-done((f32[32,1024]{1,0:T(8,128)S(1)}, f32[32,1024]{1,0:T(8,128)S(1)}, u32[]{:S(2)}, u32[]{:S(2)}) %collective-permute-start.2) | collective-permute-done | bytes 131104 | tf_op jit(solution)/shard_map/ppermute | solution.py:22
  30.5 0.0 collective-permute-done.3.refs_1_
  30.5 0.8 %collective-permute-done.4.refs_2_ = f32[32,1024]{1,0:T(8,128)S(1)} collective-permute-done((f32[32,1024]{1,0:T(8,128)S(1)}, f32[32,1024]{1,0:T(8,128)S(1)}, u32[]{:S(2)}, u32[]{:S(2)}) %collective-permute-start.4) | collective-permute-done | bytes 131104 | tf_op jit(solution)/shard_map/ppermute | solution.py:22
  31.3 2.1 %finish.1 = (f32[32,1536]{1,0:T(8,128)}, f32[32,64]{1,0:T(8,128)}, f32[32,512]{1,0:T(8,128)}, f32[64,128]{1,0:T(8,128)}) custom-call(f32[32,1536]{1,0:T(8,128)S(1)} %get-tuple-element.26.sketch_ref, f32[32,1024]{1,0:T(8,128)S(1)} %collective-permute-done.2.refs_0_, f32[32,1024]{1,0:T(8,128)S(1)} %collective-permute-done.3.refs_1_, ...), custom_call_target="tpu_custom_call" | custom-call | tf_op jit(solution)/shard_map/finish/pallas_call | solution.py:336
  (2 shorter events, 0.1 us)
Async XLA Ops:
  1.3 3.4 %copy-start.4 = (bf16[32,2048]{1,0:T(8,128)(2,1)S(1)}, bf16[32,2048]{1,0:T(8,128)(2,1)}, u32[]{:S(2)}) copy-start(bf16[32,2048]{1,0:T(8,128)(2,1)} %param.9) | copy-start | bytes 393220
  4.8 6.8 %copy-start = (bf16[64,1536]{1,0:T(8,128)(2,1)S(1)}, bf16[64,1536]{1,0:T(8,128)(2,1)}, u32[]{:S(2)}) copy-start(bf16[64,1536]{1,0:T(8,128)(2,1)} %residual_ref.3) | copy-start | bytes 589828
  4.8 6.8 %copy-start.1 = (f32[1536]{0:T(1024)S(1)}, f32[1536]{0:T(1024)}, u32[]{:S(2)}) copy-start(f32[1536]{0:T(1024)} %weight_ref.5) | copy-start | bytes 18436
  4.8 6.8 %copy-start.2 = (f32[2048]{0:T(1024)S(1)}, f32[2048]{0:T(1024)}, u32[]{:S(2)}) copy-start(f32[2048]{0:T(1024)} %freq_ref.1) | copy-start | bytes 24580
  4.8 6.8 %copy-start.3 = (s32[512]{0:T(512)S(1)}, s32[512]{0:T(512)}, u32[]{:S(2)}) copy-start(s32[512]{0:T(512)} %chosen_ref.1) | copy-start | bytes 6148
  7.1 1.6 %collective-permute-start = (f32[32,1536]{1,0:T(8,128)S(1)}, f32[32,1536]{1,0:T(8,128)S(1)}, u32[]{:S(2)}, u32[]{:S(2)}) collective-permute-start(f32[32,1536]{1,0:T(8,128)S(1)} %sketch.1), channel_id=1, source_target_pairs={{0,1},{1,0},{2,3},{3,2},{4,5},{5,4},{6,7},{7,6},{8,9},{9,8},{10,11... | collective-permute-start | bytes 589832 | tf_op jit(solution)/shard_map/ppermute | solution.py:22
  8.7 8.1 %collective-permute-start.1 = (f32[32,1536]{1,0:T(8,128)S(1)}, f32[32,1536]{1,0:T(8,128)S(1)}, u32[]{:S(2)}, u32[]{:S(2)}) collective-permute-start(f32[32,1536]{1,0:T(8,128)S(1)} %add.3.first_ref), channel_id=1, source_target_pairs={{0,2},{1,3},{2,0},{3,1},{4,6},{5,7},{6,4},{7,5},{8,10},{9,11},{10,... | collective-permute-start | bytes 589832 | tf_op jit(solution)/shard_map/ppermute | solution.py:22
  17.7 12.7 %collective-permute-start.2 = (f32[32,1024]{1,0:T(8,128)S(1)}, f32[32,1024]{1,0:T(8,128)S(1)}, u32[]{:S(2)}, u32[]{:S(2)}) collective-permute-start(f32[32,1024]{1,0:T(8,128)S(1)} %get-tuple-element.27), channel_id=1, source_target_pairs={{0,8},{4,12},{8,0},{12,4},{1,9},{5,13},{9,1},{13,5},{2,10},{6,14},... | collective-permute-start | bytes 393224 | tf_op jit(solution)/shard_map/ppermute | solution.py:22
  20.6 9.9 %collective-permute-start.3 = (f32[32,1024]{1,0:T(8,128)S(1)}, f32[32,1024]{1,0:T(8,128)S(1)}, u32[]{:S(2)}, u32[]{:S(2)}) collective-permute-start(f32[32,1024]{1,0:T(8,128)S(1)} %get-tuple-element.28), channel_id=1, source_target_pairs={{0,12},{4,8},{8,4},{12,0},{1,13},{5,9},{9,5},{13,1},{2,14},{6,10},... | collective-permute-start | bytes 393224 | tf_op jit(solution)/shard_map/ppermute | solution.py:22
  22.8 8.5 %collective-permute-start.4 = (f32[32,1024]{1,0:T(8,128)S(1)}, f32[32,1024]{1,0:T(8,128)S(1)}, u32[]{:S(2)}, u32[]{:S(2)}) collective-permute-start(f32[32,1024]{1,0:T(8,128)S(1)} %get-tuple-element.32), channel_id=1, source_target_pairs={{0,4},{4,0},{8,12},{12,8},{1,5},{5,1},{9,13},{13,9},{2,6},{6,2},{1... | collective-permute-start | bytes 393224 | tf_op jit(solution)/shard_map/ppermute | solution.py:22

commit v5 on v4

v5 whole, which is shorter than its diff:
```python
import functools
import math

import jax
import jax.numpy as jnp
from jax import lax
from jax.experimental import pallas as pl
from jax.experimental.pallas import tpu as pltpu
from jax.sharding import PartitionSpec as P

LANES = 128
PER_WORD = 4
GROUP = LANES * PER_WORD
VMEM_LIMIT = 40 * 1024 * 1024
VMEM_SKETCH = 51 * 1024 * 1024
HIGHEST = lax.Precision.HIGHEST
IN_VMEM = pl.BlockSpec(memory_space=pltpu.VMEM)
IN_HBM = pl.BlockSpec(memory_space=pltpu.HBM)


def from_partner(block, axis, apart):
    count = lax.axis_size(axis)
    route = [(low, low ^ apart) for low in range(count)]
    return lax.ppermute(block, axis, route)


def split2(value):
    high = value.astype(jnp.bfloat16)
    low = (value - high.astype(jnp.float32)).astype(jnp.bfloat16)
    return high, low


def split3(value):
    high, rest = value.astype(jnp.bfloat16), None
    rest = value - high.astype(jnp.float32)
    middle, low = split2(rest)
    return high, middle, low


def digits(words):
    out = []
    for j in range(PER_WORD):
        one = words if j == 0 else jnp.right_shift(words, 2 * j)
        one = one if j == PER_WORD - 1 else jnp.bitwise_and(one, 3)
        out.append(one.astype(jnp.float32).astype(jnp.bfloat16))
    return out


def natural_of_column(shape):
    column = lax.broadcasted_iota(jnp.int32, shape, len(shape) - 1)
    return PER_WORD * jnp.bitwise_and(column, LANES - 1) + jnp.right_shift(column, 7)


def to_digit_order():
    row = lax.broadcasted_iota(jnp.int32, (GROUP, GROUP), 0)
    column = natural_of_column((1, GROUP))
    return jnp.where(row == column, 1.0, 0.0).astype(jnp.bfloat16)


def to_natural_order():
    row = lax.broadcasted_iota(jnp.int32, (GROUP, GROUP), 0)
    natural = PER_WORD * jnp.bitwise_and(row, LANES - 1) + jnp.right_shift(row, 7)
    column = lax.broadcasted_iota(jnp.int32, (GROUP, GROUP), 1)
    return jnp.where(natural == column, 1.0, 0.0).astype(jnp.bfloat16)


def dot32(a, b):
    return jnp.dot(a, b, preferred_element_type=jnp.float32)


def group_of(slot, direct):
    return jnp.bitwise_xor(lax.axis_index("people"), slot) if direct else slot


def sketch_kernel(cuts, words_ref, basis_ref, freq_ref, out_ref, half_ref, held, sems):
    copies = [
        pltpu.make_async_copy(
            words_ref.at[pl.ds(low, high - low), :], held.at[pl.ds(low, high - low), :], sems.at[i]
        )
        for i, (low, high) in enumerate(zip(cuts, cuts[1:]))
    ]
    for copy in copies:
        copy.start()
    k, markers = basis_ref.shape
    freq = freq_ref[...].reshape(1, markers)
    scaled = basis_ref[...].astype(jnp.float32) * lax.rsqrt(2.0 * freq * (1.0 - freq))
    offset = jnp.sum(scaled * (2.0 * freq), axis=1, keepdims=True)
    order = to_digit_order()
    stacked = jnp.concatenate(split2(scaled), axis=0)
    pieces = [[] for _ in range(PER_WORD)]
    for group in range(markers // GROUP):
        moved = dot32(stacked[:, group * GROUP:(group + 1) * GROUP], order).astype(jnp.bfloat16)
        for j in range(PER_WORD):
            pieces[j].append(moved[:, j * LANES:(j + 1) * LANES])
    arranged = jnp.concatenate([piece for one in pieces for piece in one], axis=1)
    for copy, low, high in zip(copies, cuts, cuts[1:]):
        copy.wait()
        words = held[low:high, :]
        half_ref[low:high, :] = words.astype(jnp.float32).astype(jnp.bfloat16)
        total = lax.dot_general(
            arranged, jnp.concatenate(digits(words), axis=1), (((1,), (1,)), ((), ())),
            preferred_element_type=jnp.float32,
        )
        out_ref[:, low:high] = total[:k] + total[k:] - offset


def sketch_partial(genotype, basis, freq):
    people = genotype.shape[0]
    cuts = (0, people // 3, people)
    return pl.pallas_call(
        functools.partial(sketch_kernel, cuts),
        out_shape=(
            jax.ShapeDtypeStruct((basis.shape[0], people), jnp.float32),
            jax.ShapeDtypeStruct(genotype.shape, jnp.bfloat16),
        ),
        in_specs=[IN_HBM, IN_VMEM, IN_VMEM],
        out_specs=(IN_VMEM,) * 2,
        scratch_shapes=[
            pltpu.VMEM(genotype.shape, genotype.dtype),
            pltpu.SemaphoreType.DMA((len(cuts) - 1,)),
        ],
        compiler_params=pltpu.CompilerParams(vmem_limit_bytes=VMEM_SKETCH),
        name="sketch",
    )(genotype, basis, freq)


def standard(rows, planes, freq):
    n_rows = rows.shape[0]
    row_sum = jnp.sum(rows, axis=1, keepdims=True)
    raw = dot32(jnp.concatenate(split2(rows), axis=0), planes)
    return (raw[:n_rows] + raw[n_rows:] - row_sum * (2.0 * freq)) * lax.rsqrt(2.0 * freq * (1.0 - freq))


def moved_freq(freq_ref, group, order):
    markers = freq_ref.shape[0]
    freq = jnp.broadcast_to(freq_ref[...].reshape(1, markers), (8, markers))
    return dot32(jnp.concatenate(split3(freq[:, group * GROUP:(group + 1) * GROUP]), axis=0), order)


def trait_kernel(direct, half_ref, freq_ref, residual_ref, weight_ref, chosen_ref, *refs):
    outs, (chosen_freq_ref, gathered_ref, total) = refs[:-3], refs[-3:]
    people, words = half_ref.shape
    markers, n_chosen = PER_WORD * words, gathered_ref.shape[1]
    chosen = chosen_ref[...].reshape(1, n_chosen) - lax.axis_index("markers") * markers
    digit = jnp.bitwise_and(chosen, PER_WORD - 1)
    row = lax.broadcasted_iota(jnp.int32, (words, 1), 0)
    pick = jnp.where(row == jnp.right_shift(chosen, 2), 1.0, 0.0).astype(jnp.bfloat16)
    word = dot32(half_ref[...], pick).astype(jnp.int32)
    word = jnp.bitwise_and(jnp.right_shift(word, 2 * digit), 3)
    gathered = word.astype(jnp.float32).astype(jnp.bfloat16)
    gathered_ref[...] = gathered
    order = to_digit_order()
    moved = [moved_freq(freq_ref, group, order) for group in range(markers // GROUP)]
    moved = jnp.concatenate([
        jnp.concatenate([one[:, j * LANES:(j + 1) * LANES] for one in moved], axis=1)
        for j in range(PER_WORD)
    ], axis=0)
    moved = dot32(moved.astype(jnp.bfloat16), pick)
    chosen_freq = jnp.zeros((8, n_chosen), jnp.float32)
    for j in range(PER_WORD):
        one = moved[24 * j:24 * (j + 1)]
        chosen_freq = jnp.where(digit == j, one[:8] + one[8:16] + one[16:], chosen_freq)
    chosen_freq_ref[...] = chosen_freq
    rows = residual_ref[...].astype(jnp.float32) * weight_ref[...].reshape(1, -1)
    total[...] = standard(rows, gathered, chosen_freq[0:1])
    width = n_chosen // 4 if direct else n_chosen

    def chunk(slot):
        at = pl.multiple_of(group_of(slot, direct) * width, width)
        return total[:, pl.ds(at, width)]
    if direct:
        sent, kept_own, kept_far = outs
        sent[:, :width] = chunk(1)
        sent[:, width:] = chunk(2)
        kept_own[...] = chunk(0)
        kept_far[...] = chunk(3)
    else:
        outs[0][...] = total[...]


def trait_scores(half, freq, residuals, weight, chosen, direct):
    people, words = half.shape
    r, n_chosen = residuals.shape[0], chosen.shape[0]
    width = n_chosen // 4
    widths = (2 * width, width, width) if direct else (n_chosen,)
    out = pl.pallas_call(
        functools.partial(trait_kernel, direct),
        out_shape=tuple(jax.ShapeDtypeStruct((r, one), jnp.float32) for one in widths) + (
            jax.ShapeDtypeStruct((8, n_chosen), jnp.float32),
            jax.ShapeDtypeStruct((people, n_chosen), jnp.bfloat16),
        ),
        in_specs=[IN_VMEM] * 5,
        out_specs=(IN_VMEM,) * (len(widths) + 2),
        scratch_shapes=[pltpu.VMEM((r, n_chosen), jnp.float32)],
        compiler_params=pltpu.CompilerParams(vmem_limit_bytes=VMEM_LIMIT),
        cost_estimate=pl.CostEstimate(flops=2 * n_chosen * people * (words + 2 * r), bytes_accessed=2 * people * (words + n_chosen), transcendentals=0),
        name="traits",
    )(half, freq, residuals, weight, chosen)
    return out[:-2], out[-2:]


def decode_kernel(half_ref, freq_ref, planes_ref, order_ref):
    order = to_digit_order()
    for group in range(order_ref.shape[1] // GROUP):
        span = slice(group * GROUP, (group + 1) * GROUP)
        word = half_ref[:, group * LANES:(group + 1) * LANES].astype(jnp.float32).astype(jnp.int32)
        planes_ref[:, span] = jnp.concatenate(digits(word), axis=1)
        moved = moved_freq(freq_ref, group, order)
        order_ref[:, span] = moved[:8] + moved[8:16] + moved[16:]


def decode(half, freq):
    people, words = half.shape
    markers = words * PER_WORD
    return pl.pallas_call(
        decode_kernel,
        out_shape=(
            jax.ShapeDtypeStruct((people, markers), jnp.bfloat16),
            jax.ShapeDtypeStruct((8, markers), jnp.float32),
        ),
        in_specs=[IN_VMEM] * 2,
        out_specs=(IN_VMEM,) * 2,
        compiler_params=pltpu.CompilerParams(vmem_limit_bytes=VMEM_LIMIT),
        cost_estimate=pl.CostEstimate(flops=people * markers * 16, bytes_accessed=4 * people * markers, transcendentals=0),
        name="decode",
    )(half, freq)


def gram_of(sketch, residual):
    k = sketch.shape[0]
    parts = jnp.concatenate(split3(sketch), axis=0)
    raw = lax.dot_general(
        parts, jnp.concatenate([parts, residual], axis=0), (((1,), (1,)), ((), ())),
        preferred_element_type=jnp.float32,
    )
    block = [[raw[i * k:(i + 1) * k, j * k:(j + 1) * k] for j in range(3)] for i in range(3)]
    small = (block[0][2] + block[2][0]) + block[1][1]
    own = block[0][0] + ((block[0][1] + block[1][0]) + small)
    cross = raw[:k, 3 * k:] + (raw[k:2 * k, 3 * k:] + raw[2 * k:, 3 * k:])
    return jnp.concatenate([own, cross], axis=1)


def write_messages(direct, slots, outs, rows, planes_ref, order_ref, chosen_freq_ref, gathered_ref, gram):
    groups = order_ref.shape[1] // GROUP
    width = gathered_ref.shape[1] // groups
    k = rows.shape[0]
    for slot, out in zip(slots, outs):
        group = group_of(slot, direct)
        markers_at = pl.ds(pl.multiple_of(group * GROUP, GROUP), GROUP)
        scores_at = pl.ds(pl.multiple_of(group * width, width), width)
        planes = jnp.concatenate([planes_ref[:, markers_at], gathered_ref[:, scores_at]], axis=1)
        freq = jnp.concatenate([order_ref[0:1, markers_at], chosen_freq_ref[0:1, scores_at]], axis=1)
        at = GROUP + width
        out[:, :at] = standard(rows, planes, freq)
        out[:, at:at + gram.shape[1]] = gram
        end = at + padded(gram.shape[1])
        if at + gram.shape[1] < end:
            out[:, at + gram.shape[1]:end] = jnp.zeros((k, end - at - gram.shape[1]), jnp.float32)


def write_traits(out, mine, other, k):
    r, width = mine.shape
    at = out.shape[1] - r // k * width
    for i in range(r // k):
        out[:, at + i * width:at + (i + 1) * width] = mine[i * k:(i + 1) * k] + other[i * k:(i + 1) * k]


def far_kernel(direct, first_ref, second_ref, residual_ref, weight_ref, planes_ref, order_ref, chosen_freq_ref, gathered_ref, *refs):
    trait_refs, (out_a, out_b, sketch_ref, gram_ref) = refs[:-4], refs[-4:]
    weight = weight_ref[...].reshape(1, -1)
    sketch = (first_ref[...] + second_ref[...]) * weight
    sketch_ref[...] = sketch
    gram = gram_of(sketch, residual_ref[...])
    gram_ref[...] = gram
    write_messages(
        direct, (2, 3), (out_a, out_b), sketch * weight, planes_ref, order_ref, chosen_freq_ref, gathered_ref, gram
    )
    if direct:
        width = trait_refs[0].shape[1]
        write_traits(out_b, trait_refs[0][...], trait_refs[1][:, width:], sketch.shape[0])


def near_kernel(direct, sketch_ref, gram_ref, weight_ref, planes_ref, order_ref, chosen_freq_ref, gathered_ref, *refs):
    trait_refs, (out_a, out_b) = refs[:-2], refs[-2:]
    write_messages(
        direct, (0, 1), (out_a, out_b), sketch_ref[...] * weight_ref[...].reshape(1, -1),
        planes_ref, order_ref, chosen_freq_ref, gathered_ref, gram_ref[...],
    )
    if direct:
        width = trait_refs[0].shape[1]
        write_traits(out_a, trait_refs[0][...], trait_refs[1][:, :width], sketch_ref.shape[0])


def padded(width):
    return -(-width // LANES) * LANES


def product_call(kernel, name, inputs, common, traits, widths, more, direct):
    _, order, _, gathered = common
    people = gathered.shape[0]
    k = inputs[0].shape[0]
    operands = (*inputs, *common, *traits)
    out_shape = tuple(jax.ShapeDtypeStruct((k, width), jnp.float32) for width in widths) + more
    return pl.pallas_call(
        functools.partial(kernel, direct),
        out_shape=out_shape,
        in_specs=[IN_VMEM] * len(operands),
        out_specs=(IN_VMEM,) * len(out_shape),
        compiler_params=pltpu.CompilerParams(vmem_limit_bytes=VMEM_LIMIT),
        cost_estimate=pl.CostEstimate(flops=4 * k * people * sum(widths), bytes_accessed=2 * people * sum(widths), transcendentals=0),
        name=name,
    )(*operands)


def products(first, second, residuals, weight, common, traits, swapped, direct):
    k, people = first.shape
    r = traits[0].shape[0]
    width = common[-1].shape[1] // 4
    plain = GROUP + width + padded(k + r)
    longer = plain + (r // k * width if direct else 0)
    out_a, out_b, sketch, gram = product_call(
        far_kernel, "far", (first, second, residuals, weight), common,
        (traits[2], swapped) if direct else (), (plain, longer),
        (jax.ShapeDtypeStruct((k, people), jnp.float32), jax.ShapeDtypeStruct((k, k + r), jnp.float32)), direct,
    )
    own, near = product_call(
        near_kernel, "near", (sketch, gram, weight), common,
        (traits[1], swapped) if direct else (), (longer, plain), (), direct,
    )
    return [own, near, out_a, out_b], sketch


def eliminate(system, k):
    row_at = lax.broadcasted_iota(jnp.int32, (k, 1), 0)
    shape = system.shape
    block = 8
    for start in range(0, k, block):
        columns = [
            jnp.broadcast_to(system[:, j:j + 1], shape) for j in range(start, start + block)
        ]
        for t in range(block):
            j = start + t
            inverse = lax.rsqrt(columns[t][j:j + 1, :])
            factor = columns[t] * inverse
            for s in range(t + 1, block):
                columns[s] = columns[s] - factor * factor[start + s:start + s + 1, :]
            scaled = system[j:j + 1, :] * inverse
            updated = system - factor * scaled
            system = jnp.where(row_at == j, scaled, jnp.where(row_at > j, updated, system))
    return system


def finish_kernel(root_people, k, r, width, score_width, digit_order, sketch_ref, tail_ref, *refs):
    parts, (components_ref, coefficients_ref, next_ref, out_ref) = refs[:-4], refs[-4:]
    row_at = lax.broadcasted_iota(jnp.int32, (k, k), 0)
    column_at = lax.broadcasted_iota(jnp.int32, (k, k), 1)
    identity = jnp.where(row_at == column_at, 1.0, 0.0)
    gram_at = width + score_width
    trait_at = gram_at + padded(k + r)
    total = parts[0][:, :trait_at]
    traits = parts[0][:, trait_at:]
    for ref in parts[1:]:
        total = total + ref[...]
    if len(parts) > 1:
        traits = traits + tail_ref[:, trait_at:]
    system = eliminate(jnp.concatenate([total[:, gram_at:gram_at + k + r], identity], axis=1), k)
    coefficients = system[:, k:k + r]
    inverse = system[:, k + r:]
    coefficients_ref[...] = coefficients
    components_ref[...] = root_people * jnp.dot(
        inverse, sketch_ref[...], precision=HIGHEST, preferred_element_type=jnp.float32
    )
    solved = jnp.dot(
        inverse, total[:, :gram_at], precision=HIGHEST, preferred_element_type=jnp.float32
    )
    basis = solved[:, :width]
    if digit_order:
        both = dot32(jnp.concatenate(split2(basis), axis=0), to_natural_order())
        basis = both[:k] + both[k:]
    next_ref[...] = basis
    removed = lax.dot_general(
        coefficients, solved[:, width:], (((0,), (0,)), ((), ())),
        precision=HIGHEST, preferred_element_type=jnp.float32,
    )
    for i in range(r // k):
        out_ref[i * k:(i + 1) * k, :] = (
            traits[:, i * score_width:(i + 1) * score_width] - removed[i * k:(i + 1) * k]
        ) * (1.0 / root_people)


def finish(root_people, r, width, score_width, digit_order, sketch, tail, parts):
    k = sketch.shape[0]
    return pl.pallas_call(
        functools.partial(finish_kernel, root_people, k, r, width, score_width, digit_order),
        out_shape=(
            jax.ShapeDtypeStruct(sketch.shape, jnp.float32),
            jax.ShapeDtypeStruct((k, r), jnp.float32),
            jax.ShapeDtypeStruct((k, width), jnp.float32),
            jax.ShapeDtypeStruct((r, score_width), jnp.float32),
        ),
        in_specs=[IN_VMEM] * (2 + len(parts)),
        out_specs=(IN_VMEM,) * 4,
        compiler_params=pltpu.CompilerParams(vmem_limit_bytes=VMEM_LIMIT),
        name="finish",
    )(sketch, tail, *parts)


def shards(genotype, allele_freq, person_weight, basis, residuals, block_markers):
    people, words = genotype.shape
    markers = words * PER_WORD
    k, r = basis.shape[0], residuals.shape[0]
    marker_count = lax.axis_size("markers")
    people_count = lax.axis_size("people")
    groups = markers // GROUP
    direct = people_count == groups and groups == 4
    score_width = block_markers.shape[0] // people_count
    sketch, half = sketch_partial(genotype, basis, allele_freq)
    apart = 1
    while apart * 2 < marker_count:
        sketch = sketch + from_partner(sketch, "markers", apart)
        apart *= 2
    other = from_partner(sketch, "markers", apart)
    traits, (chosen_freq, gathered) = trait_scores(
        half, allele_freq, residuals, person_weight, block_markers, direct
    )
    swapped = from_partner(traits[0], "people", 1) if direct else None
    planes, order = decode(half, allele_freq)
    parts, sketch = products(
        sketch, other, residuals, person_weight, (planes, order, chosen_freq, gathered), traits, swapped, direct
    )
    if direct:
        near, far, tail = [from_partner(parts[i], "people", i) for i in range(1, groups)]
        parts = [parts[0], near, far + tail[:, :far.shape[1]]]
    else:
        whole = jnp.stack(parts, axis=1)
        part_width = block_markers.shape[0] // groups
        value = whole[:, :, :GROUP].reshape(k, groups, PER_WORD, LANES)
        value = value.swapaxes(2, 3).reshape(k, markers)
        projected = whole[:, :, GROUP:GROUP + part_width].reshape(k, -1)
        gram = parts[0][:, GROUP + part_width:]
        value, projected, traits, gram = lax.psum((value, projected, traits[0], gram), "people")
        index = lax.axis_index("people")

        def own(array):
            width = array.shape[1] // people_count
            return lax.dynamic_slice_in_dim(array, index * width, width, 1)
        traits = own(traits)
        tail = jnp.concatenate(
            [own(value), own(projected), gram] + [traits[i * k:(i + 1) * k] for i in range(r // k)], axis=1
        )
        parts = [tail]
    components, coefficients, basis_own, score_own = finish(
        math.sqrt(people * people_count), r, markers // people_count, score_width, direct, sketch, tail, parts
    )
    return components, coefficients, basis_own[None], score_own[None]


def solution(mesh):
    placed = (
        P(("cohort", "people"), "markers"),
        P(("cohort", "markers")),
        P(("cohort", "people")),
        P("cohort", "markers"),
        P("cohort", "people"),
        P("markers"),
    )
    return jax.shard_map(
        shards,
        mesh=mesh,
        in_specs=placed,
        out_specs=(
            P("cohort", "people"),
            P("cohort", None),
            P("markers", "cohort", "people"),
            P("markers", "cohort", "people"),
        ),
        check_vma=False,
    )
```

time: 33.6 us -> 33.2 us (0.988)
  other arithmetic: 4.19 us -> 0.05 us
  starting transfers between devices: 7.94 us -> 9.6 us
  local copies, waits for them, and re-layouts: 0.03 us -> 1.65 us
  Pallas kernels: 10.7 us -> 12.3 us
  waiting for transfers between devices: 9.8 us -> 8.69 us
    pallas_call x3 -> x4, Pallas kernels: 3.98 us -> 8.18 us  [the longest x1 3.75 us: sketch_partial(): pl.pallas_call(functools.partial(sketch_kernel, cuts), out_shape=(jax.Sha...]
    convert_element_type x1 -> x0, other arithmetic: 3.41 us -> none  [digits(): out.append(one.astype(jnp.bfloat16))]
    pallas_call x1, Pallas kernels: 4.67 us -> 2.04 us  [trait_scores(): pl.pallas_call(functools.partial(trait_kernel, direct), out_shape=tuple((...]
    ppermute x5 -> x6, starting transfers between devices: 7.94 us -> 9.6 us  [from_partner(): return lax.ppermute(block, axis, route)]
    unnamed x10 -> x12, local copies, waits for them, and re-layouts: 0.03 us -> 1.65 us
    ppermute x5 -> x6, waiting for transfers between devices: 9.8 us -> 8.69 us  [from_partner(): return lax.ppermute(block, axis, route)]
    mul x2 -> x0, other arithmetic: 0.75 us -> none  [the longest x1 0.71 us: shards(): 2.0 * allele_freq * (1.0 - allele_freq)]
  transfers between devices with their start and end apart: 5 -> 6, of which waited for: 4 -> 2; matrix products, arithmetic and copies ran while one was open for 0% -> 0% of each run, Pallas kernels for 16% -> 17%
where the time goes in v5:
time: 33.2 us; the launch traced here: 33 us
  Pallas kernels  12.3 us (37%)
  starting transfers between devices  9.6 us (29%)
  waiting for transfers between devices  8.69 us (26%)
  local copies, waits for them, and re-layouts  1.65 us (5%)
  between operations  0.72 us (2%)
    ppermute x6, starting transfers between devices, from_partner(): return lax.ppermute(block, axis, route)  9.6 us
    ppermute x6, waiting for transfers between devices, from_partner(): return lax.ppermute(block, axis, route)  8.69 us
    pallas_call x1, Pallas kernels, sketch_partial(): pl.pallas_call(functools.partial(sketch_kernel, cuts), out_shape=(jax.Sha...  3.75 us
    pallas_call x1, Pallas kernels, decode(): pl.pallas_call(decode_kernel, out_shape=(jax.ShapeDtypeStruct((people, ma...  2.74 us
    pallas_call x1, Pallas kernels, finish(): pl.pallas_call(functools.partial(finish_kernel, root_people, k, r, width,...  2.07 us
    pallas_call x1, Pallas kernels, trait_scores(): pl.pallas_call(functools.partial(trait_kernel, direct), out_shape=tuple((...  2.04 us
    pallas_call x2, Pallas kernels, product_call(): pl.pallas_call(functools.partial(kernel, direct), out_shape=out_shape, in...  1.69 us
    unnamed x12, local copies, waits for them, and re-layouts  1.65 us
  transfers between devices with their start and end apart: 6, of which 2 were waited for; matrix products, arithmetic and copies ran while one was open for 0% of the time, Pallas kernels for 17%

profile of v5, /device:TPU:0, one launch (start us, length us, event | category | flops | bytes accessed | tf_op | source)
XLA Modules:
  0.0 33.0 jit_solution(17927090556121632388)
XLA Ops:
  0.6 0.0 copy-start
  0.6 0.0 copy-start.1
  0.7 0.9 %copy-done.1 = bf16[32,2048]{1,0:T(8,128)(2,1)S(1)} copy-done((bf16[32,2048]{1,0:T(8,128)(2,1)S(1)}, bf16[32,2048]{1,0:T(8,128)(2,1)}, u32[]{:S(2)}) %copy-start.1) | copy-done | bytes 131096
  1.6 0.0 copy-start.2
  1.6 0.7 %copy-done.2 = f32[2048]{0:T(1024)S(1)} copy-done((f32[2048]{0:T(1024)S(1)}, f32[2048]{0:T(1024)}, u32[]{:S(2)}) %copy-start.2) | copy-done | bytes 8216
  2.3 0.0 copy-start.4
  2.3 0.0 copy-start.5
  2.3 0.0 copy-start.3
  2.3 3.8 %sketch.1 = (f32[32,1536]{1,0:T(8,128)S(1)}, bf16[1536,512]{1,0:T(8,128)(2,1)S(1)}) custom-call(s32[1536,512]{1,0:T(8,128)} %words_ref.1, bf16[32,2048]{1,0:T(8,128)(2,1)S(1)} %copy-done.1, f32[2048]{0:T(1024)S(1)} %copy-done.2), custom_call_target="tpu_custom_call" | custom-call | tf_op jit(solution)/shard_map/sketch/pallas_call | solution.py:110
  6.1 0.5 %collective-permute-start = (f32[32,1536]{1,0:T(8,128)S(1)}, f32[32,1536]{1,0:T(8,128)S(1)}, u32[]{:S(2)}, u32[]{:S(2)}) collective-permute-start(f32[32,1536]{1,0:T(8,128)S(1)} %get-tuple-element.23), channel_id=1, source_target_pairs={{0,1},{1,0},{2,3},{3,2},{4,5},{5,4},{6,7},{7,6},{8,9},{9,8},{10,11... | collective-permute-start | bytes 589832 | tf_op jit(solution)/shard_map/ppermute | solution.py:24
  6.6 1.1 %collective-permute-done = f32[32,1536]{1,0:T(8,128)S(1)} collective-permute-done((f32[32,1536]{1,0:T(8,128)S(1)}, f32[32,1536]{1,0:T(8,128)S(1)}, u32[]{:S(2)}, u32[]{:S(2)}) %collective-permute-start) | collective-permute-done | bytes 196640 | tf_op jit(solution)/shard_map/ppermute | solution.py:24
  7.7 2.9 %collective-permute-start.1 = (f32[32,1536]{1,0:T(8,128)S(1)}, f32[32,1536]{1,0:T(8,128)S(1)}, u32[]{:S(2)}, u32[]{:S(2)}) collective-permute-start(f32[32,1536]{1,0:T(8,128)S(1)} %add.6.first_ref), channel_id=1, source_target_pairs={{0,2},{1,3},{2,0},{3,1},{4,6},{5,7},{6,4},{7,5},{8,10},{9,11},{10,... | collective-permute-start | bytes 589832 | tf_op jit(solution)/shard_map/ppermute | solution.py:24
  10.6 0.0 copy-done
  10.6 0.0 copy-done.4
  10.6 0.0 copy-done.5
  10.6 2.0 %traits.1 = (f32[64,256]{1,0:T(8,128)S(1)}, f32[64,128]{1,0:T(8,128)S(1)}, f32[64,128]{1,0:T(8,128)S(1)}, f32[8,512]{1,0:T(8,128)S(1)}, bf16[1536,512]{1,0:T(8,128)(2,1)S(1)}) custom-call(bf16[1536,512]{1,0:T(8,128)(2,1)S(1)} %get-tuple-element.24.half_ref, f32[2048]{0:T(1024)S(1)} %copy-done.2, bf16[64,1536]{1,0:T(8,128)(2,1)S(1)} %copy-done, ...), custom_call_target="tpu_custom_call" | custom-call | flops 1006632960 | bytes 3145728 | tf_op jit(solution)/shard_map/traits/pallas_call | solution.py:186
  12.7 1.6 %collective-permute-start.2 = (f32[64,256]{1,0:T(8,128)S(1)}, f32[64,256]{1,0:T(8,128)S(1)}, u32[]{:S(2)}, u32[]{:S(2)}) collective-permute-start(f32[64,256]{1,0:T(8,128)S(1)} %get-tuple-element.30), channel_id=1, source_target_pairs={{0,4},{4,0},{8,12},{12,8},{1,5},{5,1},{9,13},{13,9},{2,6},{6,2},{1... | collective-permute-start | bytes 196616 | tf_op jit(solution)/shard_map/ppermute | solution.py:24
  14.3 0.0 copy-done.3
  14.3 2.7 %decode.1 = (bf16[1536,2048]{1,0:T(8,128)(2,1)S(1)}, f32[8,2048]{1,0:T(8,128)S(1)}) custom-call(bf16[1536,512]{1,0:T(8,128)(2,1)S(1)} %get-tuple-element.24.half_ref, f32[2048]{0:T(1024)S(1)} %copy-done.3), custom_call_target="tpu_custom_call" | custom-call | flops 50331648 | bytes 12582912 | tf_op jit(solution)/shard_map/decode/pallas_call | solution.py:215
  17.0 0.0 collective-permute-done.2.refs_1_
  17.0 0.0 collective-permute-done.1.second_ref
  17.1 0.9 %far.1 = (f32[32,768]{1,0:T(8,128)S(1)}, f32[32,1024]{1,0:T(8,128)S(1)}, f32[32,1536]{1,0:T(8,128)S(1)}, f32[32,96]{1,0:T(8,128)S(1)}) custom-call(f32[32,1536]{1,0:T(8,128)S(1)} %add.6.first_ref, f32[32,1536]{1,0:T(8,128)S(1)} %collective-permute-done.1.second_ref, bf16[64,1536]{1,0:T(8,128)(2,1)S(1)} %copy-done, f32[1536]{0:T(1024)S(1)} %copy-done.4, ...), custom_call_target="tpu_custom_call" | custom-call | flops 352321536 | bytes 5505024 | tf_op jit(solution)/shard_map/far/pallas_call | solution.py:304
  17.9 3.6 %collective-permute-start.3 = (f32[32,1024]{1,0:T(8,128)S(1)}, f32[32,1024]{1,0:T(8,128)S(1)}, u32[]{:S(2)}, u32[]{:S(2)}) collective-permute-start(f32[32,1024]{1,0:T(8,128)S(1)} %get-tuple-element.32), channel_id=1, source_target_pairs={{0,12},{4,8},{8,4},{12,0},{1,13},{5,9},{9,5},{13,1},{2,14},{6,10},... | collective-permute-start | bytes 393224 | tf_op jit(solution)/shard_map/ppermute | solution.py:24
  21.6 0.0 collective-permute-start.5
  21.6 0.8 %near.1 = (f32[32,1024]{1,0:T(8,128)S(1)}, f32[32,768]{1,0:T(8,128)S(1)}) custom-call(f32[32,1536]{1,0:T(8,128)S(1)} %get-tuple-element.31.sketch_ref, f32[32,96]{1,0:T(8,128)S(1)} %get-tuple-element.33.gram_ref, f32[1536]{0:T(1024)S(1)} %copy-done.4, bf16[1536,2048]{1,0:T(8,128)(2,1)S(1)} %get-tuple-element.25.planes_ref, ...), custom_call_target="tpu_custom_call" | custom-call | flops 352321536 | bytes 5505024 | tf_op jit(solution)/shard_map/near/pallas_call | solution.py:304
  22.4 0.9 %collective-permute-start.4 = (f32[32,768]{1,0:T(8,128)S(1)}, f32[32,768]{1,0:T(8,128)S(1)}, u32[]{:S(2)}, u32[]{:S(2)}) collective-permute-start(f32[32,768]{1,0:T(8,128)S(1)} %get-tuple-element.36), channel_id=1, source_target_pairs={{0,4},{4,0},{8,12},{12,8},{1,5},{5,1},{9,13},{13,9},{2,6},{6,2},{1... | collective-permute-start | bytes 294920 | tf_op jit(solution)/shard_map/ppermute | solution.py:24
  23.3 7.6 %collective-permute-done.5 = f32[32,768]{1,0:T(8,128)S(1)} collective-permute-done((f32[32,768]{1,0:T(8,128)S(1)}, f32[32,768]{1,0:T(8,128)S(1)}, u32[]{:S(2)}, u32[]{:S(2)}) %collective-permute-start.5) | collective-permute-done | bytes 98336 | tf_op jit(solution)/shard_map/ppermute | solution.py:24
  30.9 0.0 collective-permute-done.3.tail_ref
  30.9 0.0 collective-permute-done.4.refs_1_
  30.9 2.1 %finish.1 = (f32[32,1536]{1,0:T(8,128)}, f32[32,64]{1,0:T(8,128)}, f32[32,512]{1,0:T(8,128)}, f32[64,128]{1,0:T(8,128)}) custom-call(f32[32,1536]{1,0:T(8,128)S(1)} %get-tuple-element.31.sketch_ref, f32[32,1024]{1,0:T(8,128)S(1)} %collective-permute-done.3.tail_ref, f32[32,1024]{1,0:T(8,128)S(1)} %get-tuple-element.35.refs_0_, ...), custom_call_target="tpu_custom_call" | custom-call | tf_op jit(solution)/shard_map/finish/pallas_call | solution.py:393
  (2 shorter events, 0.1 us)
Async XLA Ops:
  0.6 10.0 %copy-start = (bf16[64,1536]{1,0:T(8,128)(2,1)S(1)}, bf16[64,1536]{1,0:T(8,128)(2,1)}, u32[]{:S(2)}) copy-start(bf16[64,1536]{1,0:T(8,128)(2,1)} %residual_ref.3) | copy-start | bytes 589828
  0.6 0.9 %copy-start.1 = (bf16[32,2048]{1,0:T(8,128)(2,1)S(1)}, bf16[32,2048]{1,0:T(8,128)(2,1)}, u32[]{:S(2)}) copy-start(bf16[32,2048]{1,0:T(8,128)(2,1)} %basis_ref.1) | copy-start | bytes 393220
  1.6 0.7 %copy-start.2 = (f32[2048]{0:T(1024)S(1)}, f32[2048]{0:T(1024)}, u32[]{:S(2)}) copy-start(f32[2048]{0:T(1024)} %freq_ref.5) | copy-start | bytes 24580
  2.3 8.3 %copy-start.4 = (f32[1536]{0:T(1024)S(1)}, f32[1536]{0:T(1024)}, u32[]{:S(2)}) copy-start(f32[1536]{0:T(1024)} %weight_ref.5) | copy-start | bytes 18436
  2.3 8.3 %copy-start.5 = (s32[512]{0:T(512)S(1)}, s32[512]{0:T(512)}, u32[]{:S(2)}) copy-start(s32[512]{0:T(512)} %chosen_ref.1) | copy-start | bytes 6148
  2.3 12.0 %copy-start.3 = (f32[2048]{0:T(1024)S(1)}, f32[2048]{0:T(1024)}, u32[]{:S(2)}) copy-start(f32[2048]{0:T(1024)} %freq_ref.5) | copy-start | bytes 24580
  6.1 1.6 %collective-permute-start = (f32[32,1536]{1,0:T(8,128)S(1)}, f32[32,1536]{1,0:T(8,128)S(1)}, u32[]{:S(2)}, u32[]{:S(2)}) collective-permute-start(f32[32,1536]{1,0:T(8,128)S(1)} %get-tuple-element.23), channel_id=1, source_target_pairs={{0,1},{1,0},{2,3},{3,2},{4,5},{5,4},{6,7},{7,6},{8,9},{9,8},{10,11... | collective-permute-start | bytes 589832 | tf_op jit(solution)/shard_map/ppermute | solution.py:24
  7.7 9.4 %collective-permute-start.1 = (f32[32,1536]{1,0:T(8,128)S(1)}, f32[32,1536]{1,0:T(8,128)S(1)}, u32[]{:S(2)}, u32[]{:S(2)}) collective-permute-start(f32[32,1536]{1,0:T(8,128)S(1)} %add.6.first_ref), channel_id=1, source_target_pairs={{0,2},{1,3},{2,0},{3,1},{4,6},{5,7},{6,4},{7,5},{8,10},{9,11},{10,... | collective-permute-start | bytes 589832 | tf_op jit(solution)/shard_map/ppermute | solution.py:24
  12.7 4.4 %collective-permute-start.2 = (f32[64,256]{1,0:T(8,128)S(1)}, f32[64,256]{1,0:T(8,128)S(1)}, u32[]{:S(2)}, u32[]{:S(2)}) collective-permute-start(f32[64,256]{1,0:T(8,128)S(1)} %get-tuple-element.30), channel_id=1, source_target_pairs={{0,4},{4,0},{8,12},{12,8},{1,5},{5,1},{9,13},{13,9},{2,6},{6,2},{1... | collective-permute-start | bytes 196616 | tf_op jit(solution)/shard_map/ppermute | solution.py:24
  17.9 13.0 %collective-permute-start.3 = (f32[32,1024]{1,0:T(8,128)S(1)}, f32[32,1024]{1,0:T(8,128)S(1)}, u32[]{:S(2)}, u32[]{:S(2)}) collective-permute-start(f32[32,1024]{1,0:T(8,128)S(1)} %get-tuple-element.32), channel_id=1, source_target_pairs={{0,12},{4,8},{8,4},{12,0},{1,13},{5,9},{9,5},{13,1},{2,14},{6,10},... | collective-permute-start | bytes 393224 | tf_op jit(solution)/shard_map/ppermute | solution.py:24
  21.6 9.3 %collective-permute-start.5 = (f32[32,768]{1,0:T(8,128)S(1)}, f32[32,768]{1,0:T(8,128)S(1)}, u32[]{:S(2)}, u32[]{:S(2)}) collective-permute-start(f32[32,768]{1,0:T(8,128)S(1)} %get-tuple-element.37), channel_id=1, source_target_pairs={{0,8},{4,12},{8,0},{12,4},{1,9},{5,13},{9,1},{13,5},{2,10},{6,14},... | collective-permute-start | bytes 294920 | tf_op jit(solution)/shard_map/ppermute | solution.py:24
  22.4 8.5 %collective-permute-start.4 = (f32[32,768]{1,0:T(8,128)S(1)}, f32[32,768]{1,0:T(8,128)S(1)}, u32[]{:S(2)}, u32[]{:S(2)}) collective-permute-start(f32[32,768]{1,0:T(8,128)S(1)} %get-tuple-element.36), channel_id=1, source_target_pairs={{0,4},{4,0},{8,12},{12,8},{1,5},{5,1},{9,13},{13,9},{2,6},{6,2},{1... | collective-permute-start | bytes 294920 | tf_op jit(solution)/shard_map/ppermute | solution.py:24

commit v6 on v5

--- a/solution.py
+++ b/solution.py
@@ -11,6 +11,7 @@
 LANES = 128
 PER_WORD = 4
 GROUP = LANES * PER_WORD
+CUT = 128
 VMEM_LIMIT = 40 * 1024 * 1024
 VMEM_SKETCH = 51 * 1024 * 1024
 HIGHEST = lax.Precision.HIGHEST
@@ -72,15 +73,35 @@
     return jnp.bitwise_xor(lax.axis_index("people"), slot) if direct else slot
 
 
-def sketch_kernel(cuts, words_ref, basis_ref, freq_ref, out_ref, half_ref, held, sems):
-    copies = [
-        pltpu.make_async_copy(
-            words_ref.at[pl.ds(low, high - low), :], held.at[pl.ds(low, high - low), :], sems.at[i]
-        )
-        for i, (low, high) in enumerate(zip(cuts, cuts[1:]))
-    ]
-    for copy in copies:
-        copy.start()
+def load_kernel(words_ref, half_ref, held, sems):
+    parts = sems.shape[0]
+    rows = held.shape[0] // parts
+    copies = []
+    for part in range(parts):
+        at = pl.ds(part * rows, rows)
+        copies.append(pltpu.make_async_copy(words_ref.at[at, :], held.at[at, :], sems.at[part]))
+        copies[-1].start()
+    for part, copy in enumerate(copies):
+        copy.wait()
+        at = slice(part * rows, (part + 1) * rows)
+        half_ref[at, :] = held[at, :].astype(jnp.float32).astype(jnp.bfloat16)
+
+
+def load_words(genotype):
+    parts = 3
+    return pl.pallas_call(
+        load_kernel,
+        out_shape=jax.ShapeDtypeStruct(genotype.shape, jnp.bfloat16),
+        in_specs=[IN_HBM],
+        out_specs=IN_VMEM,
+        scratch_shapes=[pltpu.VMEM(genotype.shape, genotype.dtype), pltpu.SemaphoreType.DMA((parts,))],
+        compiler_params=pltpu.CompilerParams(vmem_limit_bytes=VMEM_SKETCH),
+        cost_estimate=pl.CostEstimate(flops=0, bytes_accessed=6 * genotype.size, transcendentals=0),
+        name="load",
+    )(genotype)
+
+
+def sketch_kernel(half_ref, basis_ref, freq_ref, out_ref):
     k, markers = basis_ref.shape
     freq = freq_ref[...].reshape(1, markers)
     scaled = basis_ref[...].astype(jnp.float32) * lax.rsqrt(2.0 * freq * (1.0 - freq))
@@ -93,35 +114,23 @@
         for j in range(PER_WORD):
             pieces[j].append(moved[:, j * LANES:(j + 1) * LANES])
     arranged = jnp.concatenate([piece for one in pieces for piece in one], axis=1)
-    for copy, low, high in zip(copies, cuts, cuts[1:]):
-        copy.wait()
-        words = held[low:high, :]
-        half_ref[low:high, :] = words.astype(jnp.float32).astype(jnp.bfloat16)
-        total = lax.dot_general(
-            arranged, jnp.concatenate(digits(words), axis=1), (((1,), (1,)), ((), ())),
-            preferred_element_type=jnp.float32,
-        )
-        out_ref[:, low:high] = total[:k] + total[k:] - offset
-
-
-def sketch_partial(genotype, basis, freq):
-    people = genotype.shape[0]
-    cuts = (0, people // 3, people)
+    words = half_ref[...].astype(jnp.float32).astype(jnp.int32)
+    total = lax.dot_general(
+        arranged, jnp.concatenate(digits(words), axis=1), (((1,), (1,)), ((), ())),
+        preferred_element_type=jnp.float32,
+    )
+    out_ref[...] = total[:k] + total[k:] - offset
+
+
+def sketch_partial(half, basis, freq):
     return pl.pallas_call(
-        functools.partial(sketch_kernel, cuts),
-        out_shape=(
-            jax.ShapeDtypeStruct((basis.shape[0], people), jnp.float32),
-            jax.ShapeDtypeStruct(genotype.shape, jnp.bfloat16),
-        ),
-        in_specs=[IN_HBM, IN_VMEM, IN_VMEM],
-        out_specs=(IN_VMEM,) * 2,
-        scratch_shapes=[
-            pltpu.VMEM(genotype.shape, genotype.dtype),
-            pltpu.SemaphoreType.DMA((len(cuts) - 1,)),
-        ],
-        compiler_params=pltpu.CompilerParams(vmem_limit_bytes=VMEM_SKETCH),
+        sketch_kernel,
+        out_shape=jax.ShapeDtypeStruct((basis.shape[0], half.shape[0]), jnp.float32),
+        in_specs=[IN_VMEM] * 3,
+        out_specs=IN_VMEM,
+        compiler_params=pltpu.CompilerParams(vmem_limit_bytes=VMEM_LIMIT),
         name="sketch",
-    )(genotype, basis, freq)
+    )(half, basis, freq)
 
 
 def standard(rows, planes, freq):
@@ -240,94 +249,71 @@
     return jnp.concatenate([own, cross], axis=1)
 
 
-def write_messages(direct, slots, outs, rows, planes_ref, order_ref, chosen_freq_ref, gathered_ref, gram):
-    groups = order_ref.shape[1] // GROUP
-    width = gathered_ref.shape[1] // groups
-    k = rows.shape[0]
-    for slot, out in zip(slots, outs):
-        group = group_of(slot, direct)
-        markers_at = pl.ds(pl.multiple_of(group * GROUP, GROUP), GROUP)
-        scores_at = pl.ds(pl.multiple_of(group * width, width), width)
-        planes = jnp.concatenate([planes_ref[:, markers_at], gathered_ref[:, scores_at]], axis=1)
-        freq = jnp.concatenate([order_ref[0:1, markers_at], chosen_freq_ref[0:1, scores_at]], axis=1)
-        at = GROUP + width
-        out[:, :at] = standard(rows, planes, freq)
-        out[:, at:at + gram.shape[1]] = gram
-        end = at + padded(gram.shape[1])
-        if at + gram.shape[1] < end:
-            out[:, at + gram.shape[1]:end] = jnp.zeros((k, end - at - gram.shape[1]), jnp.float32)
-
-
-def write_traits(out, mine, other, k):
-    r, width = mine.shape
-    at = out.shape[1] - r // k * width
-    for i in range(r // k):
-        out[:, at + i * width:at + (i + 1) * width] = mine[i * k:(i + 1) * k] + other[i * k:(i + 1) * k]
-
-
-def far_kernel(direct, first_ref, second_ref, residual_ref, weight_ref, planes_ref, order_ref, chosen_freq_ref, gathered_ref, *refs):
-    trait_refs, (out_a, out_b, sketch_ref, gram_ref) = refs[:-4], refs[-4:]
+def padded(width):
+    return -(-width // LANES) * LANES
+
+
+def chunk_of(slot, direct, rows, planes_ref, order_ref, chosen_freq_ref, gathered_ref):
+    width = gathered_ref.shape[1] // (order_ref.shape[1] // GROUP)
+    group = group_of(slot, direct)
+    markers_at = pl.ds(pl.multiple_of(group * GROUP, GROUP), GROUP)
+    scores_at = pl.ds(pl.multiple_of(group * width, width), width)
+    planes = jnp.concatenate([planes_ref[:, markers_at], gathered_ref[:, scores_at]], axis=1)
+    freq = jnp.concatenate([order_ref[0:1, markers_at], chosen_freq_ref[0:1, scores_at]], axis=1)
+    return standard(rows, planes, freq)
+
+
+def far_kernel(direct, first_ref, second_ref, residual_ref, weight_ref, *refs):
+    common, refs = refs[:4], refs[4:]
+    trait_refs, refs = (refs[:2], refs[2:]) if direct else ((), refs)
+    relay_ref, straight_ref, kept_ref, across_ref, sketch_ref, gram_ref = refs[:6]
     weight = weight_ref[...].reshape(1, -1)
     sketch = (first_ref[...] + second_ref[...]) * weight
     sketch_ref[...] = sketch
     gram = gram_of(sketch, residual_ref[...])
+    k, room = gram.shape[0], gram_ref.shape[1] - gram.shape[1]
+    if room:
+        gram = jnp.concatenate([gram, jnp.zeros((k, room), jnp.float32)], axis=1)
     gram_ref[...] = gram
-    write_messages(
-        direct, (2, 3), (out_a, out_b), sketch * weight, planes_ref, order_ref, chosen_freq_ref, gathered_ref, gram
-    )
+    cut = relay_ref.shape[1] - gram.shape[1]
+    rows = sketch * weight
+    for slot, low_ref, high_ref in ((2, relay_ref, straight_ref), (3, kept_ref, across_ref)):
+        chunk = chunk_of(slot, direct, rows, *common)
+        low_ref[:, :cut] = chunk[:, :cut]
+        low_ref[:, cut:] = gram
+        high_ref[...] = chunk[:, cut:]
     if direct:
-        width = trait_refs[0].shape[1]
-        write_traits(out_b, trait_refs[0][...], trait_refs[1][:, width:], sketch.shape[0])
-
-
-def near_kernel(direct, sketch_ref, gram_ref, weight_ref, planes_ref, order_ref, chosen_freq_ref, gathered_ref, *refs):
-    trait_refs, (out_a, out_b) = refs[:-2], refs[-2:]
-    write_messages(
-        direct, (0, 1), (out_a, out_b), sketch_ref[...] * weight_ref[...].reshape(1, -1),
-        planes_ref, order_ref, chosen_freq_ref, gathered_ref, gram_ref[...],
-    )
-    if direct:
-        width = trait_refs[0].shape[1]
-        write_traits(out_a, trait_refs[0][...], trait_refs[1][:, :width], sketch_ref.shape[0])
-
-
-def padded(width):
-    return -(-width // LANES) * LANES
-
-
-def product_call(kernel, name, inputs, common, traits, widths, more, direct):
-    _, order, _, gathered = common
-    people = gathered.shape[0]
+        add_pairs(refs[6], *trait_refs)
+
+
+def add_pairs(out, mine, other):
+    k, (r, width) = out.shape[0], mine.shape
+    pair = mine[...] + other[:, width:]
+    for i in range(r // k):
+        out[:, i * width:(i + 1) * width] = pair[i * k:(i + 1) * k]
+
+
+def chunk_kernel(direct, slots, sketch_ref, weight_ref, gram_ref, *refs):
+    common, outs = refs[:4], refs[4:]
+    rows = sketch_ref[...] * weight_ref[...].reshape(1, -1)
+    for slot, out in zip(slots, outs):
+        chunk = chunk_of(slot, direct, rows, *common)
+        out[:, :chunk.shape[1]] = chunk
+        out[:, chunk.shape[1]:] = gram_ref[...]
+
+
+def product_call(kernel, name, inputs, common, widths, people):
     k = inputs[0].shape[0]
-    operands = (*inputs, *common, *traits)
-    out_shape = tuple(jax.ShapeDtypeStruct((k, width), jnp.float32) for width in widths) + more
+    operands = (*inputs, *common)
     return pl.pallas_call(
-        functools.partial(kernel, direct),
-        out_shape=out_shape,
+        kernel,
+        out_shape=tuple(jax.ShapeDtypeStruct((k, width), jnp.float32) for width in widths),
         in_specs=[IN_VMEM] * len(operands),
-        out_specs=(IN_VMEM,) * len(out_shape),
+        out_specs=(IN_VMEM,) * len(widths),
         compiler_params=pltpu.CompilerParams(vmem_limit_bytes=VMEM_LIMIT),
         cost_estimate=pl.CostEstimate(flops=4 * k * people * sum(widths), bytes_accessed=2 * people * sum(widths), transcendentals=0),
         name=name,
     )(*operands)
-
-
-def products(first, second, residuals, weight, common, traits, swapped, direct):
-    k, people = first.shape
-    r = traits[0].shape[0]
-    width = common[-1].shape[1] // 4
-    plain = GROUP + width + padded(k + r)
-    longer = plain + (r // k * width if direct else 0)
-    out_a, out_b, sketch, gram = product_call(
-        far_kernel, "far", (first, second, residuals, weight), common,
-        (traits[2], swapped) if direct else (), (plain, longer),
-        (jax.ShapeDtypeStruct((k, people), jnp.float32), jax.ShapeDtypeStruct((k, k + r), jnp.float32)), direct,
-    )
-    own, near = product_call(
-        near_kernel, "near", (sketch, gram, weight), common,
-        (traits[1], swapped) if direct else (), (longer, plain), (), direct,
-    )
-    return [own, near, out_a, out_b], sketch
 
 
 def eliminate(system, k):
@@ -350,19 +336,31 @@
     return system
 
 
-def finish_kernel(root_people, k, r, width, score_width, digit_order, sketch_ref, tail_ref, *refs):
-    parts, (components_ref, coefficients_ref, next_ref, out_ref) = refs[:-4], refs[-4:]
+def finish_kernel(root_people, r, width, digit_order, sketch_ref, own_ref, kept_ref, *refs):
+    more, (components_ref, coefficients_ref, next_ref, out_ref) = refs[:-4], refs[-4:]
+    k = sketch_ref.shape[0]
+    score_width = out_ref.shape[1]
+    total = own_ref[...]
+    traits = [kept_ref[i * k:(i + 1) * k, :] for i in range(r // k)]
+    gram_at = width + score_width
+    if more:
+        swapped_ref, near_ref, relayed_ref, straight_ref, across_ref = more
+        total = total + near_ref[...]
+        cut = gram_at - straight_ref.shape[1]
+        at = cut + total.shape[1] - gram_at
+        total = jnp.concatenate([
+            total[:, :cut] + relayed_ref[:, :cut],
+            total[:, cut:gram_at] + (straight_ref[...] + across_ref[...]),
+            total[:, gram_at:] + relayed_ref[:, cut:at],
+        ], axis=1)
+        traits = [
+            one + swapped_ref[i * k:(i + 1) * k, :score_width]
+            + relayed_ref[:, at + i * score_width:at + (i + 1) * score_width]
+            for i, one in enumerate(traits)
+        ]
     row_at = lax.broadcasted_iota(jnp.int32, (k, k), 0)
     column_at = lax.broadcasted_iota(jnp.int32, (k, k), 1)
     identity = jnp.where(row_at == column_at, 1.0, 0.0)
-    gram_at = width + score_width
-    trait_at = gram_at + padded(k + r)
-    total = parts[0][:, :trait_at]
-    traits = parts[0][:, trait_at:]
-    for ref in parts[1:]:
-        total = total + ref[...]
-    if len(parts) > 1:
-        traits = traits + tail_ref[:, trait_at:]
     system = eliminate(jnp.concatenate([total[:, gram_at:gram_at + k + r], identity], axis=1), k)
     coefficients = system[:, k:k + r]
     inverse = system[:, k + r:]
@@ -370,9 +368,7 @@
     components_ref[...] = root_people * jnp.dot(
         inverse, sketch_ref[...], precision=HIGHEST, preferred_element_type=jnp.float32
     )
-    solved = jnp.dot(
-        inverse, total[:, :gram_at], precision=HIGHEST, preferred_element_type=jnp.float32
-    )
+    solved = jnp.dot(inverse, total[:, :gram_at], precision=HIGHEST, preferred_element_type=jnp.float32)
     basis = solved[:, :width]
     if digit_order:
         both = dot32(jnp.concatenate(split2(basis), axis=0), to_natural_order())
@@ -382,27 +378,26 @@
         coefficients, solved[:, width:], (((0,), (0,)), ((), ())),
         precision=HIGHEST, preferred_element_type=jnp.float32,
     )
-    for i in range(r // k):
-        out_ref[i * k:(i + 1) * k, :] = (
-            traits[:, i * score_width:(i + 1) * score_width] - removed[i * k:(i + 1) * k]
-        ) * (1.0 / root_people)
-
-
-def finish(root_people, r, width, score_width, digit_order, sketch, tail, parts):
+    for i, one in enumerate(traits):
+        out_ref[i * k:(i + 1) * k, :] = (one - removed[i * k:(i + 1) * k]) * (1.0 / root_people)
+
+
+def finish(root_people, width, digit_order, sketch, own, kept, more):
     k = sketch.shape[0]
+    r = kept.shape[0]
     return pl.pallas_call(
-        functools.partial(finish_kernel, root_people, k, r, width, score_width, digit_order),
+        functools.partial(finish_kernel, root_people, r, width, digit_order),
         out_shape=(
             jax.ShapeDtypeStruct(sketch.shape, jnp.float32),
             jax.ShapeDtypeStruct((k, r), jnp.float32),
             jax.ShapeDtypeStruct((k, width), jnp.float32),
-            jax.ShapeDtypeStruct((r, score_width), jnp.float32),
+            jax.ShapeDtypeStruct(kept.shape, jnp.float32),
         ),
-        in_specs=[IN_VMEM] * (2 + len(parts)),
+        in_specs=[IN_VMEM] * (3 + len(more)),
         out_specs=(IN_VMEM,) * 4,
         compiler_params=pltpu.CompilerParams(vmem_limit_bytes=VMEM_LIMIT),
         name="finish",
-    )(sketch, tail, *parts)
+    )(sketch, own, kept, *more)
 
 
 def shards(genotype, allele_freq, person_weight, basis, residuals, block_markers):
@@ -413,8 +408,8 @@
     people_count = lax.axis_size("people")
     groups = markers // GROUP
     direct = people_count == groups and groups == 4
-    score_width = block_markers.shape[0] // people_count
-    sketch, half = sketch_partial(genotype, basis, allele_freq)
+    half = load_words(genotype)
+    sketch = sketch_partial(half, basis, allele_freq)
     apart = 1
     while apart * 2 < marker_count:
         sketch = sketch + from_partner(sketch, "markers", apart)
@@ -425,32 +420,51 @@
     )
     swapped = from_partner(traits[0], "people", 1) if direct else None
     planes, order = decode(half, allele_freq)
-    parts, sketch = products(
-        sketch, other, residuals, person_weight, (planes, order, chosen_freq, gathered), traits, swapped, direct
-    )
+    common = planes, order, chosen_freq, gathered
+    width = GROUP + gathered.shape[1] // groups
+    room = padded(k + r)
+    relay, straight, kept, across, sketch, gram, *pair = product_call(
+        functools.partial(far_kernel, direct), "far", (sketch, other, residuals, person_weight),
+        common + ((traits[2], swapped) if direct else ()),
+        (CUT + room, width - CUT, CUT + room, width - CUT, people, room) + ((r // k * (width - GROUP),) if direct else ()),
+        people,
+    )
+
+    def chunks(name, *slots):
+        return product_call(
+            functools.partial(chunk_kernel, direct, slots), name, (sketch, person_weight, gram), common,
+            (width + room,) * len(slots), people,
+        )
     if direct:
-        near, far, tail = [from_partner(parts[i], "people", i) for i in range(1, groups)]
-        parts = [parts[0], near, far + tail[:, :far.shape[1]]]
+        relay = from_partner(relay, "people", 1)
+        straight = from_partner(straight, "people", 2)
+        across = from_partner(across, "people", 3)
+        near, = chunks("near", 1)
+        near = from_partner(near, "people", 1)
+        relayed = jnp.concatenate([kept + relay] + pair, axis=1)
+        relayed = from_partner(relayed, "people", 3)
+        own, = chunks("own", 0)
+        kept, more = traits[1], (swapped, near, relayed, straight, across)
     else:
-        whole = jnp.stack(parts, axis=1)
-        part_width = block_markers.shape[0] // groups
+        first, second = chunks("near", 0, 1)
+        gram = lax.psum(gram, "people")
+        whole = jnp.stack([
+            first[:, :width], second[:, :width], jnp.concatenate([relay[:, :CUT], straight], axis=1),
+            jnp.concatenate([kept[:, :CUT], across], axis=1),
+        ], axis=1)
         value = whole[:, :, :GROUP].reshape(k, groups, PER_WORD, LANES)
         value = value.swapaxes(2, 3).reshape(k, markers)
-        projected = whole[:, :, GROUP:GROUP + part_width].reshape(k, -1)
-        gram = parts[0][:, GROUP + part_width:]
-        value, projected, traits, gram = lax.psum((value, projected, traits[0], gram), "people")
+        projected = whole[:, :, GROUP:].reshape(k, -1)
+        value, projected, kept = lax.psum((value, projected, traits[0]), "people")
         index = lax.axis_index("people")
 
-        def own(array):
-            width = array.shape[1] // people_count
-            return lax.dynamic_slice_in_dim(array, index * width, width, 1)
-        traits = own(traits)
-        tail = jnp.concatenate(
-            [own(value), own(projected), gram] + [traits[i * k:(i + 1) * k] for i in range(r // k)], axis=1
-        )
-        parts = [tail]
+        def own_part(array):
+            part = array.shape[1] // people_count
+            return lax.dynamic_slice_in_dim(array, index * part, part, 1)
+        own = jnp.concatenate([own_part(value), own_part(projected), gram], axis=1)
+        kept, more = own_part(kept), ()
     components, coefficients, basis_own, score_own = finish(
-        math.sqrt(people * people_count), r, markers // people_count, score_width, direct, sketch, tail, parts
+        math.sqrt(people * people_count), markers // people_count, direct, sketch, own, kept, more
     )
     return components, coefficients, basis_own[None], score_own[None]
 

time: 33.2 us -> 31.3 us (0.943)
  waiting for transfers between devices: 8.69 us -> 4.04 us
  starting transfers between devices: 9.6 us -> 13.2 us
  local copies, waits for them, and re-layouts: 1.65 us -> 0.02 us
  Pallas kernels: 12.3 us -> 13.1 us
    ppermute x6 -> x8, waiting for transfers between devices: 8.69 us -> 4.04 us  [from_partner(): return lax.ppermute(block, axis, route)]
    ppermute x6 -> x8, starting transfers between devices: 9.6 us -> 13.2 us  [from_partner(): return lax.ppermute(block, axis, route)]
    unnamed x12 -> x10, local copies, waits for them, and re-layouts: 1.65 us -> 0.02 us
    pallas_call x4 -> x6, Pallas kernels: 7.51 us -> 8.36 us  [the longest x1 2.46 us: sketch_partial(): pl.pallas_call(sketch_kernel, out_shape=jax.ShapeDtypeStruct((basis.shape...]
  transfers between devices with their start and end apart: 6 -> 8, of which waited for: 2 -> 3; matrix products, arithmetic and copies ran while one was open for 0% -> 0% of each run, Pallas kernels for 17% -> 18%
where the time goes in v6:
time: 31.3 us; the launch traced here: 31.2 us
  starting transfers between devices  13.2 us (42%)
  Pallas kernels  13.1 us (42%)
  waiting for transfers between devices  4.04 us (13%)
  between operations  0.77 us (2%)
    ppermute x8, starting transfers between devices, from_partner(): return lax.ppermute(block, axis, route)  13.2 us
    ppermute x8, waiting for transfers between devices, from_partner(): return lax.ppermute(block, axis, route)  4.04 us
    pallas_call x1, Pallas kernels, decode(): pl.pallas_call(decode_kernel, out_shape=(jax.ShapeDtypeStruct((people, ma...  2.74 us
    pallas_call x1, Pallas kernels, sketch_partial(): pl.pallas_call(sketch_kernel, out_shape=jax.ShapeDtypeStruct((basis.shape...  2.46 us
    pallas_call x1, Pallas kernels, finish(): pl.pallas_call(functools.partial(finish_kernel, root_people, r, width, di...  2.06 us
    pallas_call x1, Pallas kernels, trait_scores(): pl.pallas_call(functools.partial(trait_kernel, direct), out_shape=tuple((...  2.04 us
    pallas_call x1, Pallas kernels, load_words(): pl.pallas_call(load_kernel, out_shape=jax.ShapeDtypeStruct(genotype.shape...  2.01 us
    pallas_call x3, Pallas kernels, product_call(): pl.pallas_call(kernel, out_shape=tuple((jax.ShapeDtypeStruct((k, width),...  1.83 us
  transfers between devices with their start and end apart: 8, of which 3 were waited for; matrix products, arithmetic and copies ran while one was open for 0% of the time, Pallas kernels for 18%

profile of v6, /device:TPU:0, one launch (start us, length us, event | category | flops | bytes accessed | tf_op | source)
XLA Modules:
  0.0 31.2 jit_solution(11728659511121248169)
XLA Ops:
  0.6 0.0 copy-start.3
  0.6 0.0 copy-start.1
  0.7 0.0 copy-start.2
  0.7 0.0 copy-start
  0.7 0.0 copy-start.4
  0.7 2.0 %load.1.half_ref = bf16[1536,512]{1,0:T(8,128)(2,1)S(1)} custom-call(s32[1536,512]{1,0:T(8,128)} %words_ref.1), custom_call_target="tpu_custom_call" | custom-call | bytes 4718592 | tf_op jit(solution)/shard_map/load/pallas_call | solution.py:92
  2.7 0.0 copy-done.3
  2.7 0.0 copy-done.1
  2.7 2.5 %sketch.1 = f32[32,1536]{1,0:T(8,128)S(1)} custom-call(bf16[1536,512]{1,0:T(8,128)(2,1)S(1)} %load.1.half_ref, bf16[32,2048]{1,0:T(8,128)(2,1)S(1)} %copy-done.1, f32[2048]{0:T(1024)S(1)} %copy-done.3), custom_call_target="tpu_custom_call" | custom-call | tf_op jit(solution)/shard_map/sketch/pallas_call | solution.py:126
  5.2 0.5 %collective-permute-start = (f32[32,1536]{1,0:T(8,128)S(1)}, f32[32,1536]{1,0:T(8,128)S(1)}, u32[]{:S(2)}, u32[]{:S(2)}) collective-permute-start(f32[32,1536]{1,0:T(8,128)S(1)} %sketch.1), channel_id=1, source_target_pairs={{0,1},{1,0},{2,3},{3,2},{4,5},{5,4},{6,7},{7,6},{8,9},{9,8},{10,11... | collective-permute-start | bytes 589832 | tf_op jit(solution)/shard_map/ppermute | solution.py:25
  5.7 1.1 %collective-permute-done = f32[32,1536]{1,0:T(8,128)S(1)} collective-permute-done((f32[32,1536]{1,0:T(8,128)S(1)}, f32[32,1536]{1,0:T(8,128)S(1)}, u32[]{:S(2)}, u32[]{:S(2)}) %collective-permute-start) | collective-permute-done | bytes 196640 | tf_op jit(solution)/shard_map/ppermute | solution.py:25
  6.8 2.9 %collective-permute-start.1 = (f32[32,1536]{1,0:T(8,128)S(1)}, f32[32,1536]{1,0:T(8,128)S(1)}, u32[]{:S(2)}, u32[]{:S(2)}) collective-permute-start(f32[32,1536]{1,0:T(8,128)S(1)} %add.6.first_ref), channel_id=1, source_target_pairs={{0,2},{1,3},{2,0},{3,1},{4,6},{5,7},{6,4},{7,5},{8,10},{9,11},{10,... | collective-permute-start | bytes 589832 | tf_op jit(solution)/shard_map/ppermute | solution.py:25
  9.7 0.0 copy-done.2
  9.7 0.0 copy-done
  9.7 0.0 copy-done.4
  9.7 2.0 %traits.1 = (f32[64,256]{1,0:T(8,128)S(1)}, f32[64,128]{1,0:T(8,128)S(1)}, f32[64,128]{1,0:T(8,128)S(1)}, f32[8,512]{1,0:T(8,128)S(1)}, bf16[1536,512]{1,0:T(8,128)(2,1)S(1)}) custom-call(bf16[1536,512]{1,0:T(8,128)(2,1)S(1)} %load.1.half_ref, f32[2048]{0:T(1024)S(1)} %copy-done.3, bf16[64,1536]{1,0:T(8,128)(2,1)S(1)} %copy-done, f32[1536]{0:T(1024)S(1)} %copy-done.2, ...), custom_call_target="tpu_custom_call" | custom-call | flops 1006632960 | bytes 3145728 | tf_op jit(solution)/shard_map/traits/pallas_call | solution.py:195
  11.7 1.6 %collective-permute-start.2 = (f32[64,256]{1,0:T(8,128)S(1)}, f32[64,256]{1,0:T(8,128)S(1)}, u32[]{:S(2)}, u32[]{:S(2)}) collective-permute-start(f32[64,256]{1,0:T(8,128)S(1)} %get-tuple-element.27), channel_id=1, source_target_pairs={{0,4},{4,0},{8,12},{12,8},{1,5},{5,1},{9,13},{13,9},{2,6},{6,2},{1... | collective-permute-start | bytes 196616 | tf_op jit(solution)/shard_map/ppermute | solution.py:25
  13.4 2.7 %decode.1 = (bf16[1536,2048]{1,0:T(8,128)(2,1)S(1)}, f32[8,2048]{1,0:T(8,128)S(1)}) custom-call(bf16[1536,512]{1,0:T(8,128)(2,1)S(1)} %load.1.half_ref, f32[2048]{0:T(1024)S(1)} %copy-done.3), custom_call_target="tpu_custom_call" | custom-call | flops 50331648 | bytes 12582912 | tf_op jit(solution)/shard_map/decode/pallas_call | solution.py:224
  16.1 0.0 collective-permute-done.2.refs_5_.refs_0_
  16.1 0.0 collective-permute-done.1.second_ref
  16.2 0.9 %far.1 = (f32[32,256]{1,0:T(8,128)S(1)}, f32[32,512]{1,0:T(8,128)S(1)}, f32[32,256]{1,0:T(8,128)S(1)}, f32[32,512]{1,0:T(8,128)S(1)}, f32[32,1536]{1,0:T(8,128)S...) custom-call(f32[32,1536]{1,0:T(8,128)S(1)} %add.6.first_ref, f32[32,1536]{1,0:T(8,128)S(1)} %collective-permute-done.1.second_ref, ...), custom_call_target="tpu_custom_call" | custom-call | flops 679477248 | bytes 10616832 | tf_op jit(solution)/shard_map/far/pallas_call | solution.py:308
  17.0 1.6 %collective-permute-start.4 = (f32[32,256]{1,0:T(8,128)S(1)}, f32[32,256]{1,0:T(8,128)S(1)}, u32[]{:S(2)}, u32[]{:S(2)}) collective-permute-start(f32[32,256]{1,0:T(8,128)S(1)} %get-tuple-element.32), channel_id=1, source_target_pairs={{0,4},{4,0},{8,12},{12,8},{1,5},{5,1},{9,13},{13,9},{2,6},{6,2},{1... | collective-permute-start | bytes 98312 | tf_op jit(solution)/shard_map/ppermute | solution.py:25
  18.6 2.6 %collective-permute-start.6 = (f32[32,512]{1,0:T(8,128)S(1)}, f32[32,512]{1,0:T(8,128)S(1)}, u32[]{:S(2)}, u32[]{:S(2)}) collective-permute-start(f32[32,512]{1,0:T(8,128)S(1)} %get-tuple-element.34), channel_id=1, source_target_pairs={{0,8},{4,12},{8,0},{12,4},{1,9},{5,13},{9,1},{13,5},{2,10},{6,14},... | collective-permute-start | bytes 196616 | tf_op jit(solution)/shard_map/ppermute | solution.py:25
  21.2 0.3 collective-permute-start.7
  21.5 0.5 %near.1 = f32[32,768]{1,0:T(8,128)S(1)} custom-call(f32[32,1536]{1,0:T(8,128)S(1)} %get-tuple-element.28.sketch_ref, f32[1536]{0:T(1024)S(1)} %copy-done.2, f32[32,128]{1,0:T(8,128)S(1)} %get-tuple-element.29.gram_ref, bf16[1536,2048]{1,0:T(8,128)(2,1)S(1)} %get-tuple-element.22.refs_0_, f32[8,2048]{1,0:T(8,128)S(1)} %get-tuple-element.23.refs_1_, ...), custom_call_target="tpu_custom_call" | custom-call | flops 150994944 | bytes 2359296 | tf_op jit(solution)/shard_map/near/pallas_call | solution.py:308
  22.0 0.7 %collective-permute-start.3 = (f32[32,768]{1,0:T(8,128)S(1)}, f32[32,768]{1,0:T(8,128)S(1)}, u32[]{:S(2)}, u32[]{:S(2)}) collective-permute-start(f32[32,768]{1,0:T(8,128)S(1)} %near.1), channel_id=1, source_target_pairs={{0,4},{4,0},{8,12},{12,8},{1,5},{5,1},{9,13},{13,9},{2,6},{6,2},{1... | collective-permute-start | bytes 294920 | tf_op jit(solution)/shard_map/ppermute | solution.py:25
  22.6 0.0 collective-permute-done.4
  22.7 3.0 %collective-permute-start.5 = (f32[32,512]{1,0:T(8,128)S(1)}, f32[32,512]{1,0:T(8,128)S(1)}, u32[]{:S(2)}, u32[]{:S(2)}) collective-permute-start(f32[32,512]{1,0:T(8,128)S(1)} %pad_maximum_fusion), channel_id=1, source_target_pairs={{0,12},{4,8},{8,4},{12,0},{1,13},{5,9},{9,5},{13,1},{2,14},{6,10},... | collective-permute-start | bytes 196616 | tf_op jit(solution)/shard_map/ppermute | solution.py:25
  25.7 0.5 %own.1.own_ref = f32[32,768]{1,0:T(8,128)S(1)} custom-call(f32[32,1536]{1,0:T(8,128)S(1)} %get-tuple-element.28.sketch_ref, f32[1536]{0:T(1024)S(1)} %copy-done.2, f32[32,128]{1,0:T(8,128)S(1)} %get-tuple-element.29.gram_ref, bf16[1536,2048]{1,0:T(8,128)(2,1)S(1)} %get-tuple-element.22.refs_0_, f32[8,2048]{1,0:T(8,128)S(1)} %get-tuple-element.23.refs_1_, ...), custom_call_target="tpu_custom_call" | custom-call | flops 150994944 | bytes 2359296 | tf_op jit(solution)/shard_map/own/pallas_call | solution.py:308
  26.2 0.0 collective-permute-done.6.refs_3_
  26.2 1.2 %collective-permute-done.7.refs_4_ = f32[32,512]{1,0:T(8,128)S(1)} collective-permute-done((f32[32,512]{1,0:T(8,128)S(1)}, f32[32,512]{1,0:T(8,128)S(1)}, u32[]{:S(2)}, u32[]{:S(2)}) %collective-permute-start.7) | collective-permute-done | bytes 65568 | tf_op jit(solution)/shard_map/ppermute | solution.py:25
  27.4 1.8 %collective-permute-done.5.refs_2_ = f32[32,512]{1,0:T(8,128)S(1)} collective-permute-done((f32[32,512]{1,0:T(8,128)S(1)}, f32[32,512]{1,0:T(8,128)S(1)}, u32[]{:S(2)}, u32[]{:S(2)}) %collective-permute-start.5) | collective-permute-done | bytes 65568 | tf_op jit(solution)/shard_map/ppermute | solution.py:25
  29.1 0.0 collective-permute-done.3.refs_1_
  29.1 2.1 %finish.1 = (f32[32,1536]{1,0:T(8,128)}, f32[32,64]{1,0:T(8,128)}, f32[32,512]{1,0:T(8,128)}, f32[64,128]{1,0:T(8,128)}) custom-call(f32[32,1536]{1,0:T(8,128)S(1)} %get-tuple-element.28.sketch_ref, f32[32,768]{1,0:T(8,128)S(1)} %own.1.own_ref, f32[64,128]{1,0:T(8,128)S(1)} %get-tuple-element.30.kept_ref, ...), custom_call_target="tpu_custom_call" | custom-call | tf_op jit(solution)/shard_map/finish/pallas_call | solution.py:388
  (3 shorter events, 0.0 us)
Async XLA Ops:
  0.6 2.1 %copy-start.3 = (f32[2048]{0:T(1024)S(1)}, f32[2048]{0:T(1024)}, u32[]{:S(2)}) copy-start(f32[2048]{0:T(1024)} %freq_ref.5) | copy-start | bytes 24580
  0.6 2.1 %copy-start.1 = (bf16[32,2048]{1,0:T(8,128)(2,1)S(1)}, bf16[32,2048]{1,0:T(8,128)(2,1)}, u32[]{:S(2)}) copy-start(bf16[32,2048]{1,0:T(8,128)(2,1)} %basis_ref.1) | copy-start | bytes 393220
  0.7 9.0 %copy-start.2 = (f32[1536]{0:T(1024)S(1)}, f32[1536]{0:T(1024)}, u32[]{:S(2)}) copy-start(f32[1536]{0:T(1024)} %weight_ref.7) | copy-start | bytes 18436
  0.7 9.0 %copy-start = (bf16[64,1536]{1,0:T(8,128)(2,1)S(1)}, bf16[64,1536]{1,0:T(8,128)(2,1)}, u32[]{:S(2)}) copy-start(bf16[64,1536]{1,0:T(8,128)(2,1)} %residual_ref.3) | copy-start | bytes 589828
  0.7 9.0 %copy-start.4 = (s32[512]{0:T(512)S(1)}, s32[512]{0:T(512)}, u32[]{:S(2)}) copy-start(s32[512]{0:T(512)} %chosen_ref.1) | copy-start | bytes 6148
  5.2 1.6 %collective-permute-start = (f32[32,1536]{1,0:T(8,128)S(1)}, f32[32,1536]{1,0:T(8,128)S(1)}, u32[]{:S(2)}, u32[]{:S(2)}) collective-permute-start(f32[32,1536]{1,0:T(8,128)S(1)} %sketch.1), channel_id=1, source_target_pairs={{0,1},{1,0},{2,3},{3,2},{4,5},{5,4},{6,7},{7,6},{8,9},{9,8},{10,11... | collective-permute-start | bytes 589832 | tf_op jit(solution)/shard_map/ppermute | solution.py:25
  6.8 9.4 %collective-permute-start.1 = (f32[32,1536]{1,0:T(8,128)S(1)}, f32[32,1536]{1,0:T(8,128)S(1)}, u32[]{:S(2)}, u32[]{:S(2)}) collective-permute-start(f32[32,1536]{1,0:T(8,128)S(1)} %add.6.first_ref), channel_id=1, source_target_pairs={{0,2},{1,3},{2,0},{3,1},{4,6},{5,7},{6,4},{7,5},{8,10},{9,11},{10,... | collective-permute-start | bytes 589832 | tf_op jit(solution)/shard_map/ppermute | solution.py:25
  11.7 4.4 %collective-permute-start.2 = (f32[64,256]{1,0:T(8,128)S(1)}, f32[64,256]{1,0:T(8,128)S(1)}, u32[]{:S(2)}, u32[]{:S(2)}) collective-permute-start(f32[64,256]{1,0:T(8,128)S(1)} %get-tuple-element.27), channel_id=1, source_target_pairs={{0,4},{4,0},{8,12},{12,8},{1,5},{5,1},{9,13},{13,9},{2,6},{6,2},{1... | collective-permute-start | bytes 196616 | tf_op jit(solution)/shard_map/ppermute | solution.py:25
  17.0 5.6 %collective-permute-start.4 = (f32[32,256]{1,0:T(8,128)S(1)}, f32[32,256]{1,0:T(8,128)S(1)}, u32[]{:S(2)}, u32[]{:S(2)}) collective-permute-start(f32[32,256]{1,0:T(8,128)S(1)} %get-tuple-element.32), channel_id=1, source_target_pairs={{0,4},{4,0},{8,12},{12,8},{1,5},{5,1},{9,13},{13,9},{2,6},{6,2},{1... | collective-permute-start | bytes 98312 | tf_op jit(solution)/shard_map/ppermute | solution.py:25
  18.6 7.6 %collective-permute-start.6 = (f32[32,512]{1,0:T(8,128)S(1)}, f32[32,512]{1,0:T(8,128)S(1)}, u32[]{:S(2)}, u32[]{:S(2)}) collective-permute-start(f32[32,512]{1,0:T(8,128)S(1)} %get-tuple-element.34), channel_id=1, source_target_pairs={{0,8},{4,12},{8,0},{12,4},{1,9},{5,13},{9,1},{13,5},{2,10},{6,14},... | collective-permute-start | bytes 196616 | tf_op jit(solution)/shard_map/ppermute | solution.py:25
  21.2 6.2 %collective-permute-start.7 = (f32[32,512]{1,0:T(8,128)S(1)}, f32[32,512]{1,0:T(8,128)S(1)}, u32[]{:S(2)}, u32[]{:S(2)}) collective-permute-start(f32[32,512]{1,0:T(8,128)S(1)} %get-tuple-element.35), channel_id=1, source_target_pairs={{0,12},{4,8},{8,4},{12,0},{1,13},{5,9},{9,5},{13,1},{2,14},{6,10},... | collective-permute-start | bytes 196616 | tf_op jit(solution)/shard_map/ppermute | solution.py:25
  22.0 7.2 %collective-permute-start.3 = (f32[32,768]{1,0:T(8,128)S(1)}, f32[32,768]{1,0:T(8,128)S(1)}, u32[]{:S(2)}, u32[]{:S(2)}) collective-permute-start(f32[32,768]{1,0:T(8,128)S(1)} %near.1), channel_id=1, source_target_pairs={{0,4},{4,0},{8,12},{12,8},{1,5},{5,1},{9,13},{13,9},{2,6},{6,2},{1... | collective-permute-start | bytes 294920 | tf_op jit(solution)/shard_map/ppermute | solution.py:25
  22.7 6.5 %collective-permute-start.5 = (f32[32,512]{1,0:T(8,128)S(1)}, f32[32,512]{1,0:T(8,128)S(1)}, u32[]{:S(2)}, u32[]{:S(2)}) collective-permute-start(f32[32,512]{1,0:T(8,128)S(1)} %pad_maximum_fusion), channel_id=1, source_target_pairs={{0,12},{4,8},{8,4},{12,0},{1,13},{5,9},{9,5},{13,1},{2,14},{6,10},... | collective-permute-start | bytes 196616 | tf_op jit(solution)/shard_map/ppermute | solution.py:25

commit v7 on v6

--- a/solution.py
+++ b/solution.py
@@ -12,6 +12,7 @@
 PER_WORD = 4
 GROUP = LANES * PER_WORD
 CUT = 128
+FAR, ACROSS = 3, 2
 VMEM_LIMIT = 40 * 1024 * 1024
 VMEM_SKETCH = 51 * 1024 * 1024
 HIGHEST = lax.Precision.HIGHEST
@@ -172,34 +173,26 @@
     chosen_freq_ref[...] = chosen_freq
     rows = residual_ref[...].astype(jnp.float32) * weight_ref[...].reshape(1, -1)
     total[...] = standard(rows, gathered, chosen_freq[0:1])
-    width = n_chosen // 4 if direct else n_chosen
-
-    def chunk(slot):
+    k = outs[0].shape[0]
+    r, width = rows.shape[0], n_chosen // len(outs)
+    for slot, out in enumerate(outs):
         at = pl.multiple_of(group_of(slot, direct) * width, width)
-        return total[:, pl.ds(at, width)]
-    if direct:
-        sent, kept_own, kept_far = outs
-        sent[:, :width] = chunk(1)
-        sent[:, width:] = chunk(2)
-        kept_own[...] = chunk(0)
-        kept_far[...] = chunk(3)
-    else:
-        outs[0][...] = total[...]
-
-
-def trait_scores(half, freq, residuals, weight, chosen, direct):
+        for i in range(r // k):
+            out[:, i * width:(i + 1) * width] = total[i * k:(i + 1) * k, pl.ds(at, width)]
+
+
+def trait_scores(half, freq, residuals, weight, chosen, k, direct):
     people, words = half.shape
+    groups = words // LANES
     r, n_chosen = residuals.shape[0], chosen.shape[0]
-    width = n_chosen // 4
-    widths = (2 * width, width, width) if direct else (n_chosen,)
     out = pl.pallas_call(
         functools.partial(trait_kernel, direct),
-        out_shape=tuple(jax.ShapeDtypeStruct((r, one), jnp.float32) for one in widths) + (
+        out_shape=(jax.ShapeDtypeStruct((k, r // k * n_chosen // groups), jnp.float32),) * groups + (
             jax.ShapeDtypeStruct((8, n_chosen), jnp.float32),
             jax.ShapeDtypeStruct((people, n_chosen), jnp.bfloat16),
         ),
         in_specs=[IN_VMEM] * 5,
-        out_specs=(IN_VMEM,) * (len(widths) + 2),
+        out_specs=(IN_VMEM,) * (groups + 2),
         scratch_shapes=[pltpu.VMEM((r, n_chosen), jnp.float32)],
         compiler_params=pltpu.CompilerParams(vmem_limit_bytes=VMEM_LIMIT),
         cost_estimate=pl.CostEstimate(flops=2 * n_chosen * people * (words + 2 * r), bytes_accessed=2 * people * (words + n_chosen), transcendentals=0),
@@ -264,9 +257,8 @@
 
 
 def far_kernel(direct, first_ref, second_ref, residual_ref, weight_ref, *refs):
-    common, refs = refs[:4], refs[4:]
-    trait_refs, refs = (refs[:2], refs[2:]) if direct else ((), refs)
-    relay_ref, straight_ref, kept_ref, across_ref, sketch_ref, gram_ref = refs[:6]
+    common, trait_refs, refs = refs[:4], refs[4:6], refs[6:]
+    relay_ref, straight_ref, kept_ref, across_ref, sketch_ref, gram_ref = refs
     weight = weight_ref[...].reshape(1, -1)
     sketch = (first_ref[...] + second_ref[...]) * weight
     sketch_ref[...] = sketch
@@ -275,31 +267,27 @@
     if room:
         gram = jnp.concatenate([gram, jnp.zeros((k, room), jnp.float32)], axis=1)
     gram_ref[...] = gram
-    cut = relay_ref.shape[1] - gram.shape[1]
     rows = sketch * weight
-    for slot, low_ref, high_ref in ((2, relay_ref, straight_ref), (3, kept_ref, across_ref)):
+    for slot, low_ref, high_ref, trait_ref in (
+        (FAR, relay_ref, straight_ref, trait_refs[0]), (ACROSS, kept_ref, across_ref, trait_refs[1])
+    ):
         chunk = chunk_of(slot, direct, rows, *common)
-        low_ref[:, :cut] = chunk[:, :cut]
-        low_ref[:, cut:] = gram
-        high_ref[...] = chunk[:, cut:]
-    if direct:
-        add_pairs(refs[6], *trait_refs)
-
-
-def add_pairs(out, mine, other):
-    k, (r, width) = out.shape[0], mine.shape
-    pair = mine[...] + other[:, width:]
-    for i in range(r // k):
-        out[:, i * width:(i + 1) * width] = pair[i * k:(i + 1) * k]
+        low_ref[:, :CUT] = chunk[:, :CUT]
+        low_ref[:, CUT:CUT + gram.shape[1]] = gram
+        low_ref[:, CUT + gram.shape[1]:] = trait_ref[...]
+        high_ref[...] = chunk[:, CUT:]
 
 
 def chunk_kernel(direct, slots, sketch_ref, weight_ref, gram_ref, *refs):
-    common, outs = refs[:4], refs[4:]
+    n = len(slots)
+    common, trait_refs, outs = refs[:4], refs[4:4 + n], refs[4 + n:]
     rows = sketch_ref[...] * weight_ref[...].reshape(1, -1)
-    for slot, out in zip(slots, outs):
+    for slot, trait_ref, out in zip(slots, trait_refs, outs):
         chunk = chunk_of(slot, direct, rows, *common)
+        at = chunk.shape[1] + gram_ref.shape[1]
         out[:, :chunk.shape[1]] = chunk
-        out[:, chunk.shape[1]:] = gram_ref[...]
+        out[:, chunk.shape[1]:at] = gram_ref[...]
+        out[:, at:] = trait_ref[...]
 
 
 def product_call(kernel, name, inputs, common, widths, people):
@@ -336,28 +324,21 @@
     return system
 
 
-def finish_kernel(root_people, r, width, digit_order, sketch_ref, own_ref, kept_ref, *refs):
+def finish_kernel(root_people, r, width, digit_order, sketch_ref, own_ref, *refs):
     more, (components_ref, coefficients_ref, next_ref, out_ref) = refs[:-4], refs[-4:]
     k = sketch_ref.shape[0]
     score_width = out_ref.shape[1]
+    gram_at = width + score_width
+    trait_at = own_ref.shape[1] - r // k * score_width
     total = own_ref[...]
-    traits = [kept_ref[i * k:(i + 1) * k, :] for i in range(r // k)]
-    gram_at = width + score_width
     if more:
-        swapped_ref, near_ref, relayed_ref, straight_ref, across_ref = more
-        total = total + near_ref[...]
-        cut = gram_at - straight_ref.shape[1]
-        at = cut + total.shape[1] - gram_at
+        near_ref, relay_ref, relayed_ref, straight_ref, across_ref = more
+        total = total + jnp.concatenate([near_ref[...], relay_ref[:, relayed_ref.shape[1]:]], axis=1)
         total = jnp.concatenate([
-            total[:, :cut] + relayed_ref[:, :cut],
-            total[:, cut:gram_at] + (straight_ref[...] + across_ref[...]),
-            total[:, gram_at:] + relayed_ref[:, cut:at],
+            total[:, :CUT] + relayed_ref[:, :CUT],
+            total[:, CUT:gram_at] + (straight_ref[...] + across_ref[...]),
+            total[:, gram_at:] + relayed_ref[:, CUT:],
         ], axis=1)
-        traits = [
-            one + swapped_ref[i * k:(i + 1) * k, :score_width]
-            + relayed_ref[:, at + i * score_width:at + (i + 1) * score_width]
-            for i, one in enumerate(traits)
-        ]
     row_at = lax.broadcasted_iota(jnp.int32, (k, k), 0)
     column_at = lax.broadcasted_iota(jnp.int32, (k, k), 1)
     identity = jnp.where(row_at == column_at, 1.0, 0.0)
@@ -378,26 +359,28 @@
         coefficients, solved[:, width:], (((0,), (0,)), ((), ())),
         precision=HIGHEST, preferred_element_type=jnp.float32,
     )
-    for i, one in enumerate(traits):
-        out_ref[i * k:(i + 1) * k, :] = (one - removed[i * k:(i + 1) * k]) * (1.0 / root_people)
-
-
-def finish(root_people, width, digit_order, sketch, own, kept, more):
+    for i in range(r // k):
+        at = trait_at + i * score_width
+        out_ref[i * k:(i + 1) * k, :] = (
+            total[:, at:at + score_width] - removed[i * k:(i + 1) * k]
+        ) * (1.0 / root_people)
+
+
+def finish(root_people, r, width, score_width, digit_order, sketch, own, more):
     k = sketch.shape[0]
-    r = kept.shape[0]
     return pl.pallas_call(
         functools.partial(finish_kernel, root_people, r, width, digit_order),
         out_shape=(
             jax.ShapeDtypeStruct(sketch.shape, jnp.float32),
             jax.ShapeDtypeStruct((k, r), jnp.float32),
             jax.ShapeDtypeStruct((k, width), jnp.float32),
-            jax.ShapeDtypeStruct(kept.shape, jnp.float32),
+            jax.ShapeDtypeStruct((r, score_width), jnp.float32),
         ),
-        in_specs=[IN_VMEM] * (3 + len(more)),
+        in_specs=[IN_VMEM] * (2 + len(more)),
         out_specs=(IN_VMEM,) * 4,
         compiler_params=pltpu.CompilerParams(vmem_limit_bytes=VMEM_LIMIT),
         name="finish",
-    )(sketch, own, kept, *more)
+    )(sketch, own, *more)
 
 
 def shards(genotype, allele_freq, person_weight, basis, residuals, block_markers):
@@ -416,55 +399,58 @@
         apart *= 2
     other = from_partner(sketch, "markers", apart)
     traits, (chosen_freq, gathered) = trait_scores(
-        half, allele_freq, residuals, person_weight, block_markers, direct
-    )
-    swapped = from_partner(traits[0], "people", 1) if direct else None
+        half, allele_freq, residuals, person_weight, block_markers, k, direct
+    )
     planes, order = decode(half, allele_freq)
     common = planes, order, chosen_freq, gathered
-    width = GROUP + gathered.shape[1] // groups
+    part_width = gathered.shape[1] // groups
+    width = GROUP + part_width
     room = padded(k + r)
-    relay, straight, kept, across, sketch, gram, *pair = product_call(
+    low, high = CUT + room + traits[0].shape[1], width - CUT
+    relay, straight, kept, across, sketch, gram = product_call(
         functools.partial(far_kernel, direct), "far", (sketch, other, residuals, person_weight),
-        common + ((traits[2], swapped) if direct else ()),
-        (CUT + room, width - CUT, CUT + room, width - CUT, people, room) + ((r // k * (width - GROUP),) if direct else ()),
-        people,
+        common + (traits[FAR], traits[ACROSS]), (low, high, low, high, people, room), people,
     )
 
     def chunks(name, *slots):
         return product_call(
-            functools.partial(chunk_kernel, direct, slots), name, (sketch, person_weight, gram), common,
-            (width + room,) * len(slots), people,
+            functools.partial(chunk_kernel, direct, slots), name, (sketch, person_weight, gram),
+            common + tuple(traits[slot] for slot in slots),
+            (width + room + traits[0].shape[1],) * len(slots), people,
         )
     if direct:
-        relay = from_partner(relay, "people", 1)
-        straight = from_partner(straight, "people", 2)
-        across = from_partner(across, "people", 3)
+        relay = from_partner(jnp.concatenate([relay, traits[1]], axis=1), "people", 1)
+        straight = from_partner(straight, "people", FAR)
+        across = from_partner(across, "people", ACROSS)
         near, = chunks("near", 1)
-        near = from_partner(near, "people", 1)
-        relayed = jnp.concatenate([kept + relay] + pair, axis=1)
-        relayed = from_partner(relayed, "people", 3)
+        near = from_partner(near[:, :width + room], "people", 1)
+        relayed = from_partner(kept + relay[:, :low], "people", ACROSS)
         own, = chunks("own", 0)
-        kept, more = traits[1], (swapped, near, relayed, straight, across)
+        more = near, relay, relayed, straight, across
     else:
         first, second = chunks("near", 0, 1)
-        gram = lax.psum(gram, "people")
-        whole = jnp.stack([
-            first[:, :width], second[:, :width], jnp.concatenate([relay[:, :CUT], straight], axis=1),
-            jnp.concatenate([kept[:, :CUT], across], axis=1),
-        ], axis=1)
+        pieces = {
+            0: first, 1: second,
+            FAR: jnp.concatenate([relay[:, :CUT], straight, relay[:, CUT:]], axis=1),
+            ACROSS: jnp.concatenate([kept[:, :CUT], across, kept[:, CUT:]], axis=1),
+        }
+        whole = jnp.stack([pieces[slot] for slot in range(groups)], axis=1)
         value = whole[:, :, :GROUP].reshape(k, groups, PER_WORD, LANES)
         value = value.swapaxes(2, 3).reshape(k, markers)
-        projected = whole[:, :, GROUP:].reshape(k, -1)
-        value, projected, kept = lax.psum((value, projected, traits[0]), "people")
+        ends = [GROUP] + [width + room + i * part_width for i in range(r // k)]
+        scores = [whole[:, :, at:at + part_width].reshape(k, -1) for at in ends]
+        value, scores, gram = lax.psum((value, scores, gram), "people")
         index = lax.axis_index("people")
 
         def own_part(array):
             part = array.shape[1] // people_count
             return lax.dynamic_slice_in_dim(array, index * part, part, 1)
-        own = jnp.concatenate([own_part(value), own_part(projected), gram], axis=1)
-        kept, more = own_part(kept), ()
+        scores = [own_part(one) for one in scores]
+        own = jnp.concatenate([own_part(value), scores[0], gram] + scores[1:], axis=1)
+        more = ()
     components, coefficients, basis_own, score_own = finish(
-        math.sqrt(people * people_count), markers // people_count, direct, sketch, own, kept, more
+        math.sqrt(people * people_count), r, markers // people_count, block_markers.shape[0] // people_count,
+        direct, sketch, own, more
     )
     return components, coefficients, basis_own[None], score_own[None]
 

time: 31.3 us -> 30.3 us (0.968)
  starting transfers between devices: 13.2 us -> 11.8 us
  waiting for transfers between devices: 4.04 us -> 4.43 us
    ppermute x8 -> x7, starting transfers between devices: 13.2 us -> 11.8 us  [from_partner(): return lax.ppermute(block, axis, route)]
    ppermute x8 -> x7, waiting for transfers between devices: 4.04 us -> 4.43 us  [from_partner(): return lax.ppermute(block, axis, route)]
  transfers between devices with their start and end apart: 8 -> 7, of which waited for: 3 -> 4; matrix products, arithmetic and copies ran while one was open for 0% -> 0% of each run, Pallas kernels for 18% -> 19%
where the time goes in v7:
time: 30.3 us; the launch traced here: 30.2 us
  Pallas kernels  13.1 us (43%)
  starting transfers between devices  11.8 us (39%)
  waiting for transfers between devices  4.43 us (15%)
  between operations  0.76 us (3%)
    ppermute x7, starting transfers between devices, from_partner(): return lax.ppermute(block, axis, route)  11.8 us
    ppermute x7, waiting for transfers between devices, from_partner(): return lax.ppermute(block, axis, route)  4.43 us
    pallas_call x1, Pallas kernels, decode(): pl.pallas_call(decode_kernel, out_shape=(jax.ShapeDtypeStruct((people, ma...  2.74 us
    pallas_call x1, Pallas kernels, sketch_partial(): pl.pallas_call(sketch_kernel, out_shape=jax.ShapeDtypeStruct((basis.shape...  2.46 us
    pallas_call x1, Pallas kernels, finish(): pl.pallas_call(functools.partial(finish_kernel, root_people, r, width, di...  2.06 us
    pallas_call x1, Pallas kernels, trait_scores(): pl.pallas_call(functools.partial(trait_kernel, direct), out_shape=(jax.Sh...  2.04 us
    pallas_call x1, Pallas kernels, load_words(): pl.pallas_call(load_kernel, out_shape=jax.ShapeDtypeStruct(genotype.shape...  1.97 us
    pallas_call x3, Pallas kernels, product_call(): pl.pallas_call(kernel, out_shape=tuple((jax.ShapeDtypeStruct((k, width),...  1.84 us
  transfers between devices with their start and end apart: 7, of which 4 were waited for; matrix products, arithmetic and copies ran while one was open for 0% of the time, Pallas kernels for 19%

profile of v7, /device:TPU:0, one launch (start us, length us, event | category | flops | bytes accessed | tf_op | source)
XLA Modules:
  0.0 30.2 jit_solution(5386733934042799146)
XLA Ops:
  0.6 0.0 copy-start.3
  0.6 0.0 copy-start.1
  0.7 2.0 %load.1.half_ref = bf16[1536,512]{1,0:T(8,128)(2,1)S(1)} custom-call(s32[1536,512]{1,0:T(8,128)} %words_ref.1), custom_call_target="tpu_custom_call" | custom-call | bytes 4718592 | tf_op jit(solution)/shard_map/load/pallas_call | solution.py:93
  2.6 0.0 copy-done.3
  2.6 0.0 copy-done.1
  2.6 0.0 copy-start
  2.7 0.0 copy-start.2
  2.7 0.0 copy-start.4
  2.7 2.5 %sketch.1 = f32[32,1536]{1,0:T(8,128)S(1)} custom-call(bf16[1536,512]{1,0:T(8,128)(2,1)S(1)} %load.1.half_ref, bf16[32,2048]{1,0:T(8,128)(2,1)S(1)} %copy-done.1, f32[2048]{0:T(1024)S(1)} %copy-done.3), custom_call_target="tpu_custom_call" | custom-call | tf_op jit(solution)/shard_map/sketch/pallas_call | solution.py:127
  5.1 0.5 %collective-permute-start = (f32[32,1536]{1,0:T(8,128)S(1)}, f32[32,1536]{1,0:T(8,128)S(1)}, u32[]{:S(2)}, u32[]{:S(2)}) collective-permute-start(f32[32,1536]{1,0:T(8,128)S(1)} %sketch.1), channel_id=1, source_target_pairs={{0,1},{1,0},{2,3},{3,2},{4,5},{5,4},{6,7},{7,6},{8,9},{9,8},{10,11... | collective-permute-start | bytes 589832 | tf_op jit(solution)/shard_map/ppermute | solution.py:26
  5.6 1.1 %collective-permute-done = f32[32,1536]{1,0:T(8,128)S(1)} collective-permute-done((f32[32,1536]{1,0:T(8,128)S(1)}, f32[32,1536]{1,0:T(8,128)S(1)}, u32[]{:S(2)}, u32[]{:S(2)}) %collective-permute-start) | collective-permute-done | bytes 196640 | tf_op jit(solution)/shard_map/ppermute | solution.py:26
  6.7 2.9 %collective-permute-start.1 = (f32[32,1536]{1,0:T(8,128)S(1)}, f32[32,1536]{1,0:T(8,128)S(1)}, u32[]{:S(2)}, u32[]{:S(2)}) collective-permute-start(f32[32,1536]{1,0:T(8,128)S(1)} %add.6.first_ref), channel_id=1, source_target_pairs={{0,2},{1,3},{2,0},{3,1},{4,6},{5,7},{6,4},{7,5},{8,10},{9,11},{10,... | collective-permute-start | bytes 589832 | tf_op jit(solution)/shard_map/ppermute | solution.py:26
  9.7 2.7 %decode.1 = (bf16[1536,2048]{1,0:T(8,128)(2,1)S(1)}, f32[8,2048]{1,0:T(8,128)S(1)}) custom-call(bf16[1536,512]{1,0:T(8,128)(2,1)S(1)} %load.1.half_ref, f32[2048]{0:T(1024)S(1)} %copy-done.3), custom_call_target="tpu_custom_call" | custom-call | flops 50331648 | bytes 12582912 | tf_op jit(solution)/shard_map/decode/pallas_call | solution.py:217
  12.4 0.0 copy-done
  12.4 0.0 copy-done.2
  12.4 0.0 copy-done.4
  12.4 2.0 %traits.1 = (f32[32,256]{1,0:T(8,128)S(1)}, f32[32,256]{1,0:T(8,128)S(1)}, f32[32,256]{1,0:T(8,128)S(1)}, f32[32,256]{1,0:T(8,128)S(1)}, f32[8,512]{1,0:T(8,128)S(1)}, /*index=5*/bf16[1536,512]{1,0:T(8,128)(2,1)S(1)}) custom-call(bf16[1536,512]{1,0:T(8,128)(2,1)S(1)} %load.1.half_ref, f32[2048]{0:T(1024)S(1)} %copy-done.3, bf16[64,1536]{1,0:T(8,128)(2,1)S(1)} %copy-done, ...), custom_call_target="tpu_custom_call" | custom-call | flops 1006632960 | bytes 3145728 | tf_op jit(solution)/shard_map/traits/pallas_call | solution.py:188
  14.5 0.4 %collective-permute-done.1.second_ref = f32[32,1536]{1,0:T(8,128)S(1)} collective-permute-done((f32[32,1536]{1,0:T(8,128)S(1)}, f32[32,1536]{1,0:T(8,128)S(1)}, u32[]{:S(2)}, u32[]{:S(2)}) %collective-permute-start.1) | collective-permute-done | bytes 196640 | tf_op jit(solution)/shard_map/ppermute | solution.py:26
  14.9 0.9 %far.1 = (f32[32,512]{1,0:T(8,128)S(1)}, f32[32,512]{1,0:T(8,128)S(1)}, f32[32,512]{1,0:T(8,128)S(1)}, f32[32,512]{1,0:T(8,128)S(1)}, f32[32,1536]{1,0:T(8,128)S(1)}, /*index=5*/f32[32,128]{1,0:T(8,128)S(1)}) custom-call(f32[32,1536]{1,0:T(8,128)S(1)} %add.6.first_ref, f32[32,1536]{1,0:T(8,128)S(1)} %collective-permute-done.1.second_ref, ...), custom_call_target="tpu_custom_call" | custom-call | flops 729808896 | bytes 11403264 | tf_op jit(solution)/shard_map/far/pallas_call | solution.py:296
  15.8 1.9 %collective-permute-start.3 = (f32[32,768]{1,0:T(8,128)S(1)}, f32[32,768]{1,0:T(8,128)S(1)}, u32[]{:S(2)}, u32[]{:S(2)}) collective-permute-start(f32[32,768]{1,0:T(8,128)S(1)} %pad_maximum_fusion), channel_id=1, source_target_pairs={{0,4},{4,0},{8,12},{12,8},{1,5},{5,1},{9,13},{13,9},{2,6},{6,2},{1... | collective-permute-start | bytes 294920 | tf_op jit(solution)/shard_map/ppermute | solution.py:26
  17.6 2.5 %collective-permute-start.5 = (f32[32,512]{1,0:T(8,128)S(1)}, f32[32,512]{1,0:T(8,128)S(1)}, u32[]{:S(2)}, u32[]{:S(2)}) collective-permute-start(f32[32,512]{1,0:T(8,128)S(1)} %get-tuple-element.34), channel_id=1, source_target_pairs={{0,12},{4,8},{8,4},{12,0},{1,13},{5,9},{9,5},{13,1},{2,14},{6,10},... | collective-permute-start | bytes 196616 | tf_op jit(solution)/shard_map/ppermute | solution.py:26
  20.1 0.1 collective-permute-start.6
  20.2 0.5 %near.1 = f32[32,1024]{1,0:T(8,128)S(1)} custom-call(f32[32,1536]{1,0:T(8,128)S(1)} %get-tuple-element.28.sketch_ref, f32[1536]{0:T(1024)S(1)} %copy-done.2, f32[32,128]{1,0:T(8,128)S(1)} %get-tuple-element.29.gram_ref, bf16[1536,2048]{1,0:T(8,128)(2,1)S(1)} %get-tuple-element.22.refs_0_, f32[8,2048]{1,0:T(8,128)S(1)} %get-tuple-element.23.refs_1_, ...), custom_call_target="tpu_custom_call" | custom-call | flops 201326592 | bytes 3145728 | tf_op jit(solution)/shard_map/near/pallas_call | solution.py:296
  20.7 1.8 %collective-permute-start.2 = (f32[32,768]{1,0:T(8,128)S(1)}, f32[32,768]{1,0:T(8,128)S(1)}, u32[]{:S(2)}, u32[]{:S(2)}) collective-permute-start(f32[32,768]{1,0:T(8,128)S(1)} %slice.8), channel_id=1, source_target_pairs={{0,4},{4,0},{8,12},{12,8},{1,5},{5,1},{9,13},{13,9},{2,6},{6,2},{1... | collective-permute-start | bytes 294920 | tf_op jit(solution)/shard_map/ppermute | solution.py:26
  22.6 0.0 collective-permute-done.3.refs_1_
  22.6 2.0 %collective-permute-start.4 = (f32[32,512]{1,0:T(8,128)S(1)}, f32[32,512]{1,0:T(8,128)S(1)}, u32[]{:S(2)}, u32[]{:S(2)}) collective-permute-start(f32[32,512]{1,0:T(8,128)S(1)} %slice_add_fusion), channel_id=1, source_target_pairs={{0,8},{4,12},{8,0},{12,4},{1,9},{5,13},{9,1},{13,5},{2,10},{6,14},... | collective-permute-start | bytes 196616 | tf_op jit(solution)/shard_map/ppermute | solution.py:26
  24.6 0.5 %own.1.own_ref = f32[32,1024]{1,0:T(8,128)S(1)} custom-call(f32[32,1536]{1,0:T(8,128)S(1)} %get-tuple-element.28.sketch_ref, f32[1536]{0:T(1024)S(1)} %copy-done.2, f32[32,128]{1,0:T(8,128)S(1)} %get-tuple-element.29.gram_ref, bf16[1536,2048]{1,0:T(8,128)(2,1)S(1)} %get-tuple-element.22.refs_0_, f32[8,2048]{1,0:T(8,128)S(1)} %get-tuple-element.23.refs_1_, ...), custom_call_target="tpu_custom_call" | custom-call | flops 201326592 | bytes 3145728 | tf_op jit(solution)/shard_map/own/pallas_call | solution.py:296
  25.1 0.0 collective-permute-done.5.refs_3_
  25.1 2.3 %collective-permute-done.6.refs_4_ = f32[32,512]{1,0:T(8,128)S(1)} collective-permute-done((f32[32,512]{1,0:T(8,128)S(1)}, f32[32,512]{1,0:T(8,128)S(1)}, u32[]{:S(2)}, u32[]{:S(2)}) %collective-permute-start.6) | collective-permute-done | bytes 65568 | tf_op jit(solution)/shard_map/ppermute | solution.py:26
  27.4 0.0 collective-permute-done.2.refs_0_
  27.4 0.7 %collective-permute-done.4.refs_2_ = f32[32,512]{1,0:T(8,128)S(1)} collective-permute-done((f32[32,512]{1,0:T(8,128)S(1)}, f32[32,512]{1,0:T(8,128)S(1)}, u32[]{:S(2)}, u32[]{:S(2)}) %collective-permute-start.4) | collective-permute-done | bytes 65568 | tf_op jit(solution)/shard_map/ppermute | solution.py:26
  28.1 2.1 %finish.1 = (f32[32,1536]{1,0:T(8,128)}, f32[32,64]{1,0:T(8,128)}, f32[32,512]{1,0:T(8,128)}, f32[64,128]{1,0:T(8,128)}) custom-call(f32[32,1536]{1,0:T(8,128)S(1)} %get-tuple-element.28.sketch_ref, f32[32,1024]{1,0:T(8,128)S(1)} %own.1.own_ref, f32[32,768]{1,0:T(8,128)S(1)} %collective-permute-done.2.refs_0_, f32[32,768]{1,0:T(8,128)S(1)} %collective-permute-done.3.refs_1_, ...), custom_call_target="tpu_custom_call" | custom-call | tf_op jit(solution)/shard_map/finish/pallas_call | solution.py:371
  (4 shorter events, 0.1 us)
Async XLA Ops:
  0.6 2.0 %copy-start.3 = (f32[2048]{0:T(1024)S(1)}, f32[2048]{0:T(1024)}, u32[]{:S(2)}) copy-start(f32[2048]{0:T(1024)} %freq_ref.5) | copy-start | bytes 24580
  0.6 2.0 %copy-start.1 = (bf16[32,2048]{1,0:T(8,128)(2,1)S(1)}, bf16[32,2048]{1,0:T(8,128)(2,1)}, u32[]{:S(2)}) copy-start(bf16[32,2048]{1,0:T(8,128)(2,1)} %basis_ref.1) | copy-start | bytes 393220
  2.6 9.7 %copy-start = (bf16[64,1536]{1,0:T(8,128)(2,1)S(1)}, bf16[64,1536]{1,0:T(8,128)(2,1)}, u32[]{:S(2)}) copy-start(bf16[64,1536]{1,0:T(8,128)(2,1)} %residual_ref.3) | copy-start | bytes 589828
  2.7 9.8 %copy-start.2 = (f32[1536]{0:T(1024)S(1)}, f32[1536]{0:T(1024)}, u32[]{:S(2)}) copy-start(f32[1536]{0:T(1024)} %weight_ref.7) | copy-start | bytes 18436
  2.7 9.8 %copy-start.4 = (s32[512]{0:T(512)S(1)}, s32[512]{0:T(512)}, u32[]{:S(2)}) copy-start(s32[512]{0:T(512)} %chosen_ref.1) | copy-start | bytes 6148
  5.1 1.6 %collective-permute-start = (f32[32,1536]{1,0:T(8,128)S(1)}, f32[32,1536]{1,0:T(8,128)S(1)}, u32[]{:S(2)}, u32[]{:S(2)}) collective-permute-start(f32[32,1536]{1,0:T(8,128)S(1)} %sketch.1), channel_id=1, source_target_pairs={{0,1},{1,0},{2,3},{3,2},{4,5},{5,4},{6,7},{7,6},{8,9},{9,8},{10,11... | collective-permute-start | bytes 589832 | tf_op jit(solution)/shard_map/ppermute | solution.py:26
  6.7 8.1 %collective-permute-start.1 = (f32[32,1536]{1,0:T(8,128)S(1)}, f32[32,1536]{1,0:T(8,128)S(1)}, u32[]{:S(2)}, u32[]{:S(2)}) collective-permute-start(f32[32,1536]{1,0:T(8,128)S(1)} %add.6.first_ref), channel_id=1, source_target_pairs={{0,2},{1,3},{2,0},{3,1},{4,6},{5,7},{6,4},{7,5},{8,10},{9,11},{10,... | collective-permute-start | bytes 589832 | tf_op jit(solution)/shard_map/ppermute | solution.py:26
  15.8 6.8 %collective-permute-start.3 = (f32[32,768]{1,0:T(8,128)S(1)}, f32[32,768]{1,0:T(8,128)S(1)}, u32[]{:S(2)}, u32[]{:S(2)}) collective-permute-start(f32[32,768]{1,0:T(8,128)S(1)} %pad_maximum_fusion), channel_id=1, source_target_pairs={{0,4},{4,0},{8,12},{12,8},{1,5},{5,1},{9,13},{13,9},{2,6},{6,2},{1... | collective-permute-start | bytes 294920 | tf_op jit(solution)/shard_map/ppermute | solution.py:26
  17.6 7.5 %collective-permute-start.5 = (f32[32,512]{1,0:T(8,128)S(1)}, f32[32,512]{1,0:T(8,128)S(1)}, u32[]{:S(2)}, u32[]{:S(2)}) collective-permute-start(f32[32,512]{1,0:T(8,128)S(1)} %get-tuple-element.34), channel_id=1, source_target_pairs={{0,12},{4,8},{8,4},{12,0},{1,13},{5,9},{9,5},{13,1},{2,14},{6,10},... | collective-permute-start | bytes 196616 | tf_op jit(solution)/shard_map/ppermute | solution.py:26
  20.1 7.3 %collective-permute-start.6 = (f32[32,512]{1,0:T(8,128)S(1)}, f32[32,512]{1,0:T(8,128)S(1)}, u32[]{:S(2)}, u32[]{:S(2)}) collective-permute-start(f32[32,512]{1,0:T(8,128)S(1)} %get-tuple-element.35), channel_id=1, source_target_pairs={{0,8},{4,12},{8,0},{12,4},{1,9},{5,13},{9,1},{13,5},{2,10},{6,14},... | collective-permute-start | bytes 196616 | tf_op jit(solution)/shard_map/ppermute | solution.py:26
  20.7 6.7 %collective-permute-start.2 = (f32[32,768]{1,0:T(8,128)S(1)}, f32[32,768]{1,0:T(8,128)S(1)}, u32[]{:S(2)}, u32[]{:S(2)}) collective-permute-start(f32[32,768]{1,0:T(8,128)S(1)} %slice.8), channel_id=1, source_target_pairs={{0,4},{4,0},{8,12},{12,8},{1,5},{5,1},{9,13},{13,9},{2,6},{6,2},{1... | collective-permute-start | bytes 294920 | tf_op jit(solution)/shard_map/ppermute | solution.py:26
  22.6 5.5 %collective-permute-start.4 = (f32[32,512]{1,0:T(8,128)S(1)}, f32[32,512]{1,0:T(8,128)S(1)}, u32[]{:S(2)}, u32[]{:S(2)}) collective-permute-start(f32[32,512]{1,0:T(8,128)S(1)} %slice_add_fusion), channel_id=1, source_target_pairs={{0,8},{4,12},{8,0},{12,4},{1,9},{5,13},{9,1},{13,5},{2,10},{6,14},... | collective-permute-start | bytes 196616 | tf_op jit(solution)/shard_map/ppermute | solution.py:26

commit v8 on v7

--- a/solution.py
+++ b/solution.py
@@ -74,7 +74,7 @@
     return jnp.bitwise_xor(lax.axis_index("people"), slot) if direct else slot
 
 
-def load_kernel(words_ref, half_ref, held, sems):
+def load_kernel(words_ref, half_ref, order_ref, back_ref, held, sems):
     parts = sems.shape[0]
     rows = held.shape[0] // parts
     copies = []
@@ -82,6 +82,8 @@
         at = pl.ds(part * rows, rows)
         copies.append(pltpu.make_async_copy(words_ref.at[at, :], held.at[at, :], sems.at[part]))
         copies[-1].start()
+    order_ref[...] = to_digit_order()
+    back_ref[...] = to_natural_order()
     for part, copy in enumerate(copies):
         copy.wait()
         at = slice(part * rows, (part + 1) * rows)
@@ -92,9 +94,13 @@
     parts = 3
     return pl.pallas_call(
         load_kernel,
-        out_shape=jax.ShapeDtypeStruct(genotype.shape, jnp.bfloat16),
+        out_shape=(
+            jax.ShapeDtypeStruct(genotype.shape, jnp.bfloat16),
+            jax.ShapeDtypeStruct((GROUP, GROUP), jnp.bfloat16),
+            jax.ShapeDtypeStruct((GROUP, GROUP), jnp.bfloat16),
+        ),
         in_specs=[IN_HBM],
-        out_specs=IN_VMEM,
+        out_specs=(IN_VMEM,) * 3,
         scratch_shapes=[pltpu.VMEM(genotype.shape, genotype.dtype), pltpu.SemaphoreType.DMA((parts,))],
         compiler_params=pltpu.CompilerParams(vmem_limit_bytes=VMEM_SKETCH),
         cost_estimate=pl.CostEstimate(flops=0, bytes_accessed=6 * genotype.size, transcendentals=0),
@@ -102,12 +108,12 @@
     )(genotype)
 
 
-def sketch_kernel(half_ref, basis_ref, freq_ref, out_ref):
+def sketch_kernel(half_ref, to_digits_ref, basis_ref, freq_ref, out_ref):
     k, markers = basis_ref.shape
     freq = freq_ref[...].reshape(1, markers)
     scaled = basis_ref[...].astype(jnp.float32) * lax.rsqrt(2.0 * freq * (1.0 - freq))
     offset = jnp.sum(scaled * (2.0 * freq), axis=1, keepdims=True)
-    order = to_digit_order()
+    order = to_digits_ref[...]
     stacked = jnp.concatenate(split2(scaled), axis=0)
     pieces = [[] for _ in range(PER_WORD)]
     for group in range(markers // GROUP):
@@ -123,15 +129,15 @@
     out_ref[...] = total[:k] + total[k:] - offset
 
 
-def sketch_partial(half, basis, freq):
+def sketch_partial(half, to_digits, basis, freq):
     return pl.pallas_call(
         sketch_kernel,
         out_shape=jax.ShapeDtypeStruct((basis.shape[0], half.shape[0]), jnp.float32),
-        in_specs=[IN_VMEM] * 3,
+        in_specs=[IN_VMEM] * 4,
         out_specs=IN_VMEM,
         compiler_params=pltpu.CompilerParams(vmem_limit_bytes=VMEM_LIMIT),
         name="sketch",
-    )(half, basis, freq)
+    )(half, to_digits, basis, freq)
 
 
 def standard(rows, planes, freq):
@@ -147,7 +153,7 @@
     return dot32(jnp.concatenate(split3(freq[:, group * GROUP:(group + 1) * GROUP]), axis=0), order)
 
 
-def trait_kernel(direct, half_ref, freq_ref, residual_ref, weight_ref, chosen_ref, *refs):
+def trait_kernel(direct, half_ref, to_digits_ref, freq_ref, residual_ref, weight_ref, chosen_ref, *refs):
     outs, (chosen_freq_ref, gathered_ref, total) = refs[:-3], refs[-3:]
     people, words = half_ref.shape
     markers, n_chosen = PER_WORD * words, gathered_ref.shape[1]
@@ -159,7 +165,7 @@
     word = jnp.bitwise_and(jnp.right_shift(word, 2 * digit), 3)
     gathered = word.astype(jnp.float32).astype(jnp.bfloat16)
     gathered_ref[...] = gathered
-    order = to_digit_order()
+    order = to_digits_ref[...]
     moved = [moved_freq(freq_ref, group, order) for group in range(markers // GROUP)]
     moved = jnp.concatenate([
         jnp.concatenate([one[:, j * LANES:(j + 1) * LANES] for one in moved], axis=1)
@@ -181,7 +187,7 @@
             out[:, i * width:(i + 1) * width] = total[i * k:(i + 1) * k, pl.ds(at, width)]
 
 
-def trait_scores(half, freq, residuals, weight, chosen, k, direct):
+def trait_scores(half, to_digits, freq, residuals, weight, chosen, k, direct):
     people, words = half.shape
     groups = words // LANES
     r, n_chosen = residuals.shape[0], chosen.shape[0]
@@ -191,18 +197,18 @@
             jax.ShapeDtypeStruct((8, n_chosen), jnp.float32),
             jax.ShapeDtypeStruct((people, n_chosen), jnp.bfloat16),
         ),
-        in_specs=[IN_VMEM] * 5,
+        in_specs=[IN_VMEM] * 6,
         out_specs=(IN_VMEM,) * (groups + 2),
         scratch_shapes=[pltpu.VMEM((r, n_chosen), jnp.float32)],
         compiler_params=pltpu.CompilerParams(vmem_limit_bytes=VMEM_LIMIT),
         cost_estimate=pl.CostEstimate(flops=2 * n_chosen * people * (words + 2 * r), bytes_accessed=2 * people * (words + n_chosen), transcendentals=0),
         name="traits",
-    )(half, freq, residuals, weight, chosen)
+    )(half, to_digits, freq, residuals, weight, chosen)
     return out[:-2], out[-2:]
 
 
-def decode_kernel(half_ref, freq_ref, planes_ref, order_ref):
-    order = to_digit_order()
+def decode_kernel(half_ref, to_digits_ref, freq_ref, planes_ref, order_ref):
+    order = to_digits_ref[...]
     for group in range(order_ref.shape[1] // GROUP):
         span = slice(group * GROUP, (group + 1) * GROUP)
         word = half_ref[:, group * LANES:(group + 1) * LANES].astype(jnp.float32).astype(jnp.int32)
@@ -211,7 +217,7 @@
         order_ref[:, span] = moved[:8] + moved[8:16] + moved[16:]
 
 
-def decode(half, freq):
+def decode(half, to_digits, freq):
     people, words = half.shape
     markers = words * PER_WORD
     return pl.pallas_call(
@@ -220,12 +226,12 @@
             jax.ShapeDtypeStruct((people, markers), jnp.bfloat16),
             jax.ShapeDtypeStruct((8, markers), jnp.float32),
         ),
-        in_specs=[IN_VMEM] * 2,
+        in_specs=[IN_VMEM] * 3,
         out_specs=(IN_VMEM,) * 2,
         compiler_params=pltpu.CompilerParams(vmem_limit_bytes=VMEM_LIMIT),
         cost_estimate=pl.CostEstimate(flops=people * markers * 16, bytes_accessed=4 * people * markers, transcendentals=0),
         name="decode",
-    )(half, freq)
+    )(half, to_digits, freq)
 
 
 def gram_of(sketch, residual):
@@ -324,7 +330,7 @@
     return system
 
 
-def finish_kernel(root_people, r, width, digit_order, sketch_ref, own_ref, *refs):
+def finish_kernel(root_people, r, width, digit_order, sketch_ref, to_natural_ref, own_ref, *refs):
     more, (components_ref, coefficients_ref, next_ref, out_ref) = refs[:-4], refs[-4:]
     k = sketch_ref.shape[0]
     score_width = out_ref.shape[1]
@@ -333,7 +339,9 @@
     total = own_ref[...]
     if more:
         near_ref, relay_ref, relayed_ref, straight_ref, across_ref = more
-        total = total + jnp.concatenate([near_ref[...], relay_ref[:, relayed_ref.shape[1]:]], axis=1)
+        end = relayed_ref.shape[1]
+        beside = [near_ref[...], relay_ref[:, CUT:CUT + trait_at - gram_at], relay_ref[:, end:]]
+        total = total + jnp.concatenate(beside, axis=1)
         total = jnp.concatenate([
             total[:, :CUT] + relayed_ref[:, :CUT],
             total[:, CUT:gram_at] + (straight_ref[...] + across_ref[...]),
@@ -352,7 +360,7 @@
     solved = jnp.dot(inverse, total[:, :gram_at], precision=HIGHEST, preferred_element_type=jnp.float32)
     basis = solved[:, :width]
     if digit_order:
-        both = dot32(jnp.concatenate(split2(basis), axis=0), to_natural_order())
+        both = dot32(jnp.concatenate(split2(basis), axis=0), to_natural_ref[...])
         basis = both[:k] + both[k:]
     next_ref[...] = basis
     removed = lax.dot_general(
@@ -366,7 +374,7 @@
         ) * (1.0 / root_people)
 
 
-def finish(root_people, r, width, score_width, digit_order, sketch, own, more):
+def finish(root_people, r, width, score_width, digit_order, sketch, to_natural, own, more):
     k = sketch.shape[0]
     return pl.pallas_call(
         functools.partial(finish_kernel, root_people, r, width, digit_order),
@@ -376,11 +384,11 @@
             jax.ShapeDtypeStruct((k, width), jnp.float32),
             jax.ShapeDtypeStruct((r, score_width), jnp.float32),
         ),
-        in_specs=[IN_VMEM] * (2 + len(more)),
+        in_specs=[IN_VMEM] * (3 + len(more)),
         out_specs=(IN_VMEM,) * 4,
         compiler_params=pltpu.CompilerParams(vmem_limit_bytes=VMEM_LIMIT),
         name="finish",
-    )(sketch, own, *more)
+    )(sketch, to_natural, own, *more)
 
 
 def shards(genotype, allele_freq, person_weight, basis, residuals, block_markers):
@@ -391,17 +399,17 @@
     people_count = lax.axis_size("people")
     groups = markers // GROUP
     direct = people_count == groups and groups == 4
-    half = load_words(genotype)
-    sketch = sketch_partial(half, basis, allele_freq)
+    half, to_digits, to_natural = load_words(genotype)
+    sketch = sketch_partial(half, to_digits, basis, allele_freq)
     apart = 1
     while apart * 2 < marker_count:
         sketch = sketch + from_partner(sketch, "markers", apart)
         apart *= 2
     other = from_partner(sketch, "markers", apart)
     traits, (chosen_freq, gathered) = trait_scores(
-        half, allele_freq, residuals, person_weight, block_markers, k, direct
-    )
-    planes, order = decode(half, allele_freq)
+        half, to_digits, allele_freq, residuals, person_weight, block_markers, k, direct
+    )
+    planes, order = decode(half, to_digits, allele_freq)
     common = planes, order, chosen_freq, gathered
     part_width = gathered.shape[1] // groups
     width = GROUP + part_width
@@ -423,7 +431,7 @@
         straight = from_partner(straight, "people", FAR)
         across = from_partner(across, "people", ACROSS)
         near, = chunks("near", 1)
-        near = from_partner(near[:, :width + room], "people", 1)
+        near = from_partner(near[:, :width], "people", 1)
         relayed = from_partner(kept + relay[:, :low], "people", ACROSS)
         own, = chunks("own", 0)
         more = near, relay, relayed, straight, across
@@ -450,7 +458,7 @@
         more = ()
     components, coefficients, basis_own, score_own = finish(
         math.sqrt(people * people_count), r, markers // people_count, block_markers.shape[0] // people_count,
-        direct, sketch, own, more
+        direct, sketch, to_natural, own, more
     )
     return components, coefficients, basis_own[None], score_own[None]
 

time: 30.3 us -> 30.2 us (level)
  no operation moved by 1% of the time
where the time goes in v8:
time: 30.2 us; the launch traced here: 30.1 us
  Pallas kernels  12.9 us (43%)
  starting transfers between devices  11.8 us (39%)
  waiting for transfers between devices  4.58 us (15%)
  between operations  0.76 us (3%)
    ppermute x7, starting transfers between devices, from_partner(): return lax.ppermute(block, axis, route)  11.8 us
    ppermute x7, waiting for transfers between devices, from_partner(): return lax.ppermute(block, axis, route)  4.58 us
    pallas_call x1, Pallas kernels, decode(): pl.pallas_call(decode_kernel, out_shape=(jax.ShapeDtypeStruct((people, ma...  2.7 us
    pallas_call x1, Pallas kernels, sketch_partial(): pl.pallas_call(sketch_kernel, out_shape=jax.ShapeDtypeStruct((basis.shape...  2.41 us
    pallas_call x1, Pallas kernels, finish(): pl.pallas_call(functools.partial(finish_kernel, root_people, r, width, di...  2.04 us
    pallas_call x1, Pallas kernels, load_words(): pl.pallas_call(load_kernel, out_shape=(jax.ShapeDtypeStruct(genotype.shap...  1.97 us
    pallas_call x1, Pallas kernels, trait_scores(): pl.pallas_call(functools.partial(trait_kernel, direct), out_shape=(jax.Sh...  1.94 us
    pallas_call x3, Pallas kernels, product_call(): pl.pallas_call(kernel, out_shape=tuple((jax.ShapeDtypeStruct((k, width),...  1.84 us
  transfers between devices with their start and end apart: 7, of which 4 were waited for; matrix products, arithmetic and copies ran while one was open for 0% of the time, Pallas kernels for 19%

profile of v8, /device:TPU:0, one launch (start us, length us, event | category | flops | bytes accessed | tf_op | source)
XLA Modules:
  0.0 30.1 jit_solution(1596574100612874709)
XLA Ops:
  0.6 0.0 copy-start.3
  0.6 0.0 copy-start.1
  0.7 2.0 %load.1 = (bf16[1536,512]{1,0:T(8,128)(2,1)S(1)}, bf16[512,512]{1,0:T(8,128)(2,1)S(1)}, bf16[512,512]{1,0:T(8,128)(2,1)S(1)}) custom-call(s32[1536,512]{1,0:T(8,128)} %words_ref.1), custom_call_target="tpu_custom_call" | custom-call | bytes 4718592 | tf_op jit(solution)/shard_map/load/pallas_call | solution.py:95
  2.6 0.0 copy-start
  2.6 0.0 copy-start.2
  2.7 0.0 copy-start.4
  2.7 0.0 copy-done.3
  2.7 0.0 copy-done.1
  2.7 2.4 %sketch.1 = f32[32,1536]{1,0:T(8,128)S(1)} custom-call(bf16[1536,512]{1,0:T(8,128)(2,1)S(1)} %get-tuple-element.25.half_ref, bf16[512,512]{1,0:T(8,128)(2,1)S(1)} %get-tuple-element.26.to_digits_ref, bf16[32,2048]{1,0:T(8,128)(2,1)S(1)} %copy-done.1, f32[2048]{0:T(1024)S(1)} %copy-done.3), custom_call_target="tpu_custom_call" | custom-call | tf_op jit(solution)/shard_map/sketch/pallas_call | solution.py:133
  5.1 0.5 %collective-permute-start = (f32[32,1536]{1,0:T(8,128)S(1)}, f32[32,1536]{1,0:T(8,128)S(1)}, u32[]{:S(2)}, u32[]{:S(2)}) collective-permute-start(f32[32,1536]{1,0:T(8,128)S(1)} %sketch.1), channel_id=1, source_target_pairs={{0,1},{1,0},{2,3},{3,2},{4,5},{5,4},{6,7},{7,6},{8,9},{9,8},{10,11... | collective-permute-start | bytes 589832 | tf_op jit(solution)/shard_map/ppermute | solution.py:26
  5.6 1.1 %collective-permute-done = f32[32,1536]{1,0:T(8,128)S(1)} collective-permute-done((f32[32,1536]{1,0:T(8,128)S(1)}, f32[32,1536]{1,0:T(8,128)S(1)}, u32[]{:S(2)}, u32[]{:S(2)}) %collective-permute-start) | collective-permute-done | bytes 196640 | tf_op jit(solution)/shard_map/ppermute | solution.py:26
  6.7 2.9 %collective-permute-start.1 = (f32[32,1536]{1,0:T(8,128)S(1)}, f32[32,1536]{1,0:T(8,128)S(1)}, u32[]{:S(2)}, u32[]{:S(2)}) collective-permute-start(f32[32,1536]{1,0:T(8,128)S(1)} %add.6.first_ref), channel_id=1, source_target_pairs={{0,2},{1,3},{2,0},{3,1},{4,6},{5,7},{6,4},{7,5},{8,10},{9,11},{10,... | collective-permute-start | bytes 589832 | tf_op jit(solution)/shard_map/ppermute | solution.py:26
  9.6 2.7 %decode.1 = (bf16[1536,2048]{1,0:T(8,128)(2,1)S(1)}, f32[8,2048]{1,0:T(8,128)S(1)}) custom-call(bf16[1536,512]{1,0:T(8,128)(2,1)S(1)} %get-tuple-element.25.half_ref, bf16[512,512]{1,0:T(8,128)(2,1)S(1)} %get-tuple-element.26.to_digits_ref, f32[2048]{0:T(1024)S(1)} %copy-done.3), custom_call_target="tpu_custom_call" | custom-call | flops 50331648 | bytes 12582912 | tf_op jit(solution)/shard_map/decode/pallas_call | solution.py:223
  12.3 0.0 copy-done
  12.3 0.0 copy-done.2
  12.3 0.0 copy-done.4
  12.3 1.9 %traits.1 = (f32[32,256]{1,0:T(8,128)S(1)}, f32[32,256]{1,0:T(8,128)S(1)}, f32[32,256]{1,0:T(8,128)S(1)}, f32[32,256]{1,0:T(8,128)S(1)}, f32[8,512]{1,0:T(8,128)S(1)}, /*index=5*/bf16[1536,512]{1,0:T(8,128)(2,1)S(1)}) custom-call(bf16[1536,512]{1,0:T(8,128)(2,1)S(1)} %get-tuple-element.25.half_ref, bf16[512,512]{1,0:T(8,128)(2,1)S(1)} %get-tuple-element.26.to_digits_ref, ...), custom_call_target="tpu_custom_call" | custom-call | flops 1006632960 | bytes 3145728 | tf_op jit(solution)/shard_map/traits/pallas_call | solution.py:194
  14.3 0.5 %collective-permute-done.1.second_ref = f32[32,1536]{1,0:T(8,128)S(1)} collective-permute-done((f32[32,1536]{1,0:T(8,128)S(1)}, f32[32,1536]{1,0:T(8,128)S(1)}, u32[]{:S(2)}, u32[]{:S(2)}) %collective-permute-start.1) | collective-permute-done | bytes 196640 | tf_op jit(solution)/shard_map/ppermute | solution.py:26
  14.8 0.9 %far.1 = (f32[32,512]{1,0:T(8,128)S(1)}, f32[32,512]{1,0:T(8,128)S(1)}, f32[32,512]{1,0:T(8,128)S(1)}, f32[32,512]{1,0:T(8,128)S(1)}, f32[32,1536]{1,0:T(8,128)S(1)}, /*index=5*/f32[32,128]{1,0:T(8,128)S(1)}) custom-call(f32[32,1536]{1,0:T(8,128)S(1)} %add.6.first_ref, f32[32,1536]{1,0:T(8,128)S(1)} %collective-permute-done.1.second_ref, ...), custom_call_target="tpu_custom_call" | custom-call | flops 729808896 | bytes 11403264 | tf_op jit(solution)/shard_map/far/pallas_call | solution.py:302
  15.7 1.9 %collective-permute-start.3 = (f32[32,768]{1,0:T(8,128)S(1)}, f32[32,768]{1,0:T(8,128)S(1)}, u32[]{:S(2)}, u32[]{:S(2)}) collective-permute-start(f32[32,768]{1,0:T(8,128)S(1)} %pad_maximum_fusion), channel_id=1, source_target_pairs={{0,4},{4,0},{8,12},{12,8},{1,5},{5,1},{9,13},{13,9},{2,6},{6,2},{1... | collective-permute-start | bytes 294920 | tf_op jit(solution)/shard_map/ppermute | solution.py:26
  17.6 2.5 %collective-permute-start.5 = (f32[32,512]{1,0:T(8,128)S(1)}, f32[32,512]{1,0:T(8,128)S(1)}, u32[]{:S(2)}, u32[]{:S(2)}) collective-permute-start(f32[32,512]{1,0:T(8,128)S(1)} %get-tuple-element.40), channel_id=1, source_target_pairs={{0,12},{4,8},{8,4},{12,0},{1,13},{5,9},{9,5},{13,1},{2,14},{6,10},... | collective-permute-start | bytes 196616 | tf_op jit(solution)/shard_map/ppermute | solution.py:26
  20.1 0.1 collective-permute-start.6
  20.2 0.5 %near.1 = f32[32,1024]{1,0:T(8,128)S(1)} custom-call(f32[32,1536]{1,0:T(8,128)S(1)} %get-tuple-element.33.sketch_ref, f32[1536]{0:T(1024)S(1)} %copy-done.2, f32[32,128]{1,0:T(8,128)S(1)} %get-tuple-element.35.gram_ref, bf16[1536,2048]{1,0:T(8,128)(2,1)S(1)} %get-tuple-element.27.refs_0_, f32[8,2048]{1,0:T(8,128)S(1)} %get-tuple-element.28.refs_1_, ...), custom_call_target="tpu_custom_call" | custom-call | flops 201326592 | bytes 3145728 | tf_op jit(solution)/shard_map/near/pallas_call | solution.py:302
  20.7 1.8 %collective-permute-start.2 = (f32[32,640]{1,0:T(8,128)S(1)}, f32[32,640]{1,0:T(8,128)S(1)}, u32[]{:S(2)}, u32[]{:S(2)}) collective-permute-start(f32[32,640]{1,0:T(8,128)S(1)} %slice.8), channel_id=1, source_target_pairs={{0,4},{4,0},{8,12},{12,8},{1,5},{5,1},{9,13},{13,9},{2,6},{6,2},{1... | collective-permute-start | bytes 245768 | tf_op jit(solution)/shard_map/ppermute | solution.py:26
  22.5 0.0 collective-permute-done.3.refs_1_
  22.6 2.0 %collective-permute-start.4 = (f32[32,512]{1,0:T(8,128)S(1)}, f32[32,512]{1,0:T(8,128)S(1)}, u32[]{:S(2)}, u32[]{:S(2)}) collective-permute-start(f32[32,512]{1,0:T(8,128)S(1)} %slice_add_fusion), channel_id=1, source_target_pairs={{0,8},{4,12},{8,0},{12,4},{1,9},{5,13},{9,1},{13,5},{2,10},{6,14},... | collective-permute-start | bytes 196616 | tf_op jit(solution)/shard_map/ppermute | solution.py:26
  24.6 0.5 %own.1.own_ref = f32[32,1024]{1,0:T(8,128)S(1)} custom-call(f32[32,1536]{1,0:T(8,128)S(1)} %get-tuple-element.33.sketch_ref, f32[1536]{0:T(1024)S(1)} %copy-done.2, f32[32,128]{1,0:T(8,128)S(1)} %get-tuple-element.35.gram_ref, bf16[1536,2048]{1,0:T(8,128)(2,1)S(1)} %get-tuple-element.27.refs_0_, f32[8,2048]{1,0:T(8,128)S(1)} %get-tuple-element.28.refs_1_, ...), custom_call_target="tpu_custom_call" | custom-call | flops 201326592 | bytes 3145728 | tf_op jit(solution)/shard_map/own/pallas_call | solution.py:302
  25.1 0.0 collective-permute-done.5.refs_3_
  25.1 2.3 %collective-permute-done.6.refs_4_ = f32[32,512]{1,0:T(8,128)S(1)} collective-permute-done((f32[32,512]{1,0:T(8,128)S(1)}, f32[32,512]{1,0:T(8,128)S(1)}, u32[]{:S(2)}, u32[]{:S(2)}) %collective-permute-start.6) | collective-permute-done | bytes 65568 | tf_op jit(solution)/shard_map/ppermute | solution.py:26
  27.4 0.0 collective-permute-done.2.refs_0_
  27.4 0.7 %collective-permute-done.4.refs_2_ = f32[32,512]{1,0:T(8,128)S(1)} collective-permute-done((f32[32,512]{1,0:T(8,128)S(1)}, f32[32,512]{1,0:T(8,128)S(1)}, u32[]{:S(2)}, u32[]{:S(2)}) %collective-permute-start.4) | collective-permute-done | bytes 65568 | tf_op jit(solution)/shard_map/ppermute | solution.py:26
  28.1 2.0 %finish.1 = (f32[32,1536]{1,0:T(8,128)}, f32[32,64]{1,0:T(8,128)}, f32[32,512]{1,0:T(8,128)}, f32[64,128]{1,0:T(8,128)}) custom-call(f32[32,1536]{1,0:T(8,128)S(1)} %get-tuple-element.33.sketch_ref, bf16[512,512]{1,0:T(8,128)(2,1)S(1)} %get-tuple-element.34.to_natural_ref, f32[32,1024]{1,0:T(8,128)S(1)} %own.1.own_ref, ...), custom_call_target="tpu_custom_call" | custom-call | tf_op jit(solution)/shard_map/finish/pallas_call | solution.py:379
  (4 shorter events, 0.0 us)
Async XLA Ops:
  0.6 2.0 %copy-start.3 = (f32[2048]{0:T(1024)S(1)}, f32[2048]{0:T(1024)}, u32[]{:S(2)}) copy-start(f32[2048]{0:T(1024)} %freq_ref.5) | copy-start | bytes 24580
  0.6 2.0 %copy-start.1 = (bf16[32,2048]{1,0:T(8,128)(2,1)S(1)}, bf16[32,2048]{1,0:T(8,128)(2,1)}, u32[]{:S(2)}) copy-start(bf16[32,2048]{1,0:T(8,128)(2,1)} %basis_ref.1) | copy-start | bytes 393220
  2.6 9.7 %copy-start = (bf16[64,1536]{1,0:T(8,128)(2,1)S(1)}, bf16[64,1536]{1,0:T(8,128)(2,1)}, u32[]{:S(2)}) copy-start(bf16[64,1536]{1,0:T(8,128)(2,1)} %residual_ref.3) | copy-start | bytes 589828
  2.6 9.7 %copy-start.2 = (f32[1536]{0:T(1024)S(1)}, f32[1536]{0:T(1024)}, u32[]{:S(2)}) copy-start(f32[1536]{0:T(1024)} %weight_ref.7) | copy-start | bytes 18436
  2.7 9.7 %copy-start.4 = (s32[512]{0:T(512)S(1)}, s32[512]{0:T(512)}, u32[]{:S(2)}) copy-start(s32[512]{0:T(512)} %chosen_ref.1) | copy-start | bytes 6148
  5.1 1.6 %collective-permute-start = (f32[32,1536]{1,0:T(8,128)S(1)}, f32[32,1536]{1,0:T(8,128)S(1)}, u32[]{:S(2)}, u32[]{:S(2)}) collective-permute-start(f32[32,1536]{1,0:T(8,128)S(1)} %sketch.1), channel_id=1, source_target_pairs={{0,1},{1,0},{2,3},{3,2},{4,5},{5,4},{6,7},{7,6},{8,9},{9,8},{10,11... | collective-permute-start | bytes 589832 | tf_op jit(solution)/shard_map/ppermute | solution.py:26
  6.7 8.1 %collective-permute-start.1 = (f32[32,1536]{1,0:T(8,128)S(1)}, f32[32,1536]{1,0:T(8,128)S(1)}, u32[]{:S(2)}, u32[]{:S(2)}) collective-permute-start(f32[32,1536]{1,0:T(8,128)S(1)} %add.6.first_ref), channel_id=1, source_target_pairs={{0,2},{1,3},{2,0},{3,1},{4,6},{5,7},{6,4},{7,5},{8,10},{9,11},{10,... | collective-permute-start | bytes 589832 | tf_op jit(solution)/shard_map/ppermute | solution.py:26
  15.7 6.8 %collective-permute-start.3 = (f32[32,768]{1,0:T(8,128)S(1)}, f32[32,768]{1,0:T(8,128)S(1)}, u32[]{:S(2)}, u32[]{:S(2)}) collective-permute-start(f32[32,768]{1,0:T(8,128)S(1)} %pad_maximum_fusion), channel_id=1, source_target_pairs={{0,4},{4,0},{8,12},{12,8},{1,5},{5,1},{9,13},{13,9},{2,6},{6,2},{1... | collective-permute-start | bytes 294920 | tf_op jit(solution)/shard_map/ppermute | solution.py:26
  17.6 7.5 %collective-permute-start.5 = (f32[32,512]{1,0:T(8,128)S(1)}, f32[32,512]{1,0:T(8,128)S(1)}, u32[]{:S(2)}, u32[]{:S(2)}) collective-permute-start(f32[32,512]{1,0:T(8,128)S(1)} %get-tuple-element.40), channel_id=1, source_target_pairs={{0,12},{4,8},{8,4},{12,0},{1,13},{5,9},{9,5},{13,1},{2,14},{6,10},... | collective-permute-start | bytes 196616 | tf_op jit(solution)/shard_map/ppermute | solution.py:26
  20.1 7.3 %collective-permute-start.6 = (f32[32,512]{1,0:T(8,128)S(1)}, f32[32,512]{1,0:T(8,128)S(1)}, u32[]{:S(2)}, u32[]{:S(2)}) collective-permute-start(f32[32,512]{1,0:T(8,128)S(1)} %get-tuple-element.41), channel_id=1, source_target_pairs={{0,8},{4,12},{8,0},{12,4},{1,9},{5,13},{9,1},{13,5},{2,10},{6,14},... | collective-permute-start | bytes 196616 | tf_op jit(solution)/shard_map/ppermute | solution.py:26
  20.7 6.7 %collective-permute-start.2 = (f32[32,640]{1,0:T(8,128)S(1)}, f32[32,640]{1,0:T(8,128)S(1)}, u32[]{:S(2)}, u32[]{:S(2)}) collective-permute-start(f32[32,640]{1,0:T(8,128)S(1)} %slice.8), channel_id=1, source_target_pairs={{0,4},{4,0},{8,12},{12,8},{1,5},{5,1},{9,13},{13,9},{2,6},{6,2},{1... | collective-permute-start | bytes 245768 | tf_op jit(solution)/shard_map/ppermute | solution.py:26
  22.6 5.5 %collective-permute-start.4 = (f32[32,512]{1,0:T(8,128)S(1)}, f32[32,512]{1,0:T(8,128)S(1)}, u32[]{:S(2)}, u32[]{:S(2)}) collective-permute-start(f32[32,512]{1,0:T(8,128)S(1)} %slice_add_fusion), channel_id=1, source_target_pairs={{0,8},{4,12},{8,0},{12,4},{1,9},{5,13},{9,1},{13,5},{2,10},{6,14},... | collective-permute-start | bytes 196616 | tf_op jit(solution)/shard_map/ppermute | solution.py:26

commit v9 on v8

--- a/solution.py
+++ b/solution.py
@@ -108,11 +108,22 @@
     )(genotype)
 
 
-def sketch_kernel(half_ref, to_digits_ref, basis_ref, freq_ref, out_ref):
+def sketch_of(arranged, offset, half):
+    words = half.astype(jnp.float32).astype(jnp.int32)
+    total = lax.dot_general(
+        arranged, jnp.concatenate(digits(words), axis=1), (((1,), (1,)), ((), ())),
+        preferred_element_type=jnp.float32,
+    )
+    k = total.shape[0] // 2
+    return total[:k] + total[k:] - offset
+
+
+def first_sketch_kernel(half_ref, to_digits_ref, basis_ref, freq_ref, out_ref, arranged_ref, offset_ref):
     k, markers = basis_ref.shape
     freq = freq_ref[...].reshape(1, markers)
     scaled = basis_ref[...].astype(jnp.float32) * lax.rsqrt(2.0 * freq * (1.0 - freq))
     offset = jnp.sum(scaled * (2.0 * freq), axis=1, keepdims=True)
+    offset_ref[...] = jnp.broadcast_to(offset, offset_ref.shape)
     order = to_digits_ref[...]
     stacked = jnp.concatenate(split2(scaled), axis=0)
     pieces = [[] for _ in range(PER_WORD)]
@@ -121,23 +132,40 @@
         for j in range(PER_WORD):
             pieces[j].append(moved[:, j * LANES:(j + 1) * LANES])
     arranged = jnp.concatenate([piece for one in pieces for piece in one], axis=1)
-    words = half_ref[...].astype(jnp.float32).astype(jnp.int32)
-    total = lax.dot_general(
-        arranged, jnp.concatenate(digits(words), axis=1), (((1,), (1,)), ((), ())),
-        preferred_element_type=jnp.float32,
-    )
-    out_ref[...] = total[:k] + total[k:] - offset
-
-
-def sketch_partial(half, to_digits, basis, freq):
+    arranged_ref[...] = arranged
+    out_ref[...] = sketch_of(arranged, offset, half_ref[:out_ref.shape[1], :])
+
+
+def first_sketch(half, to_digits, basis, freq, cut):
+    k, markers = basis.shape
     return pl.pallas_call(
-        sketch_kernel,
-        out_shape=jax.ShapeDtypeStruct((basis.shape[0], half.shape[0]), jnp.float32),
+        first_sketch_kernel,
+        out_shape=(
+            jax.ShapeDtypeStruct((k, cut), jnp.float32),
+            jax.ShapeDtypeStruct((2 * k, markers), jnp.bfloat16),
+            jax.ShapeDtypeStruct((k, LANES), jnp.float32),
+        ),
         in_specs=[IN_VMEM] * 4,
-        out_specs=IN_VMEM,
+        out_specs=(IN_VMEM,) * 3,
         compiler_params=pltpu.CompilerParams(vmem_limit_bytes=VMEM_LIMIT),
         name="sketch",
     )(half, to_digits, basis, freq)
+
+
+def second_sketch_kernel(half_ref, arranged_ref, offset_ref, out_ref):
+    low = half_ref.shape[0] - out_ref.shape[1]
+    out_ref[...] = sketch_of(arranged_ref[...], offset_ref[:, 0:1], half_ref[low:, :])
+
+
+def second_sketch(half, arranged, offset, cut):
+    return pl.pallas_call(
+        second_sketch_kernel,
+        out_shape=jax.ShapeDtypeStruct((offset.shape[0], half.shape[0] - cut), jnp.float32),
+        in_specs=[IN_VMEM] * 3,
+        out_specs=IN_VMEM,
+        compiler_params=pltpu.CompilerParams(vmem_limit_bytes=VMEM_LIMIT),
+        name="more",
+    )(half, arranged, offset)
 
 
 def standard(rows, planes, freq):
@@ -154,7 +182,7 @@
 
 
 def trait_kernel(direct, half_ref, to_digits_ref, freq_ref, residual_ref, weight_ref, chosen_ref, *refs):
-    outs, (chosen_freq_ref, gathered_ref, total) = refs[:-3], refs[-3:]
+    outs, (order_ref, chosen_freq_ref, gathered_ref, total) = refs[:-4], refs[-4:]
     people, words = half_ref.shape
     markers, n_chosen = PER_WORD * words, gathered_ref.shape[1]
     chosen = chosen_ref[...].reshape(1, n_chosen) - lax.axis_index("markers") * markers
@@ -167,6 +195,8 @@
     gathered_ref[...] = gathered
     order = to_digits_ref[...]
     moved = [moved_freq(freq_ref, group, order) for group in range(markers // GROUP)]
+    for group, one in enumerate(moved):
+        order_ref[:, group * GROUP:(group + 1) * GROUP] = one[:8] + one[8:16] + one[16:]
     moved = jnp.concatenate([
         jnp.concatenate([one[:, j * LANES:(j + 1) * LANES] for one in moved], axis=1)
         for j in range(PER_WORD)
@@ -194,44 +224,38 @@
     out = pl.pallas_call(
         functools.partial(trait_kernel, direct),
         out_shape=(jax.ShapeDtypeStruct((k, r // k * n_chosen // groups), jnp.float32),) * groups + (
+            jax.ShapeDtypeStruct((8, words * PER_WORD), jnp.float32),
             jax.ShapeDtypeStruct((8, n_chosen), jnp.float32),
             jax.ShapeDtypeStruct((people, n_chosen), jnp.bfloat16),
         ),
         in_specs=[IN_VMEM] * 6,
-        out_specs=(IN_VMEM,) * (groups + 2),
+        out_specs=(IN_VMEM,) * (groups + 3),
         scratch_shapes=[pltpu.VMEM((r, n_chosen), jnp.float32)],
         compiler_params=pltpu.CompilerParams(vmem_limit_bytes=VMEM_LIMIT),
         cost_estimate=pl.CostEstimate(flops=2 * n_chosen * people * (words + 2 * r), bytes_accessed=2 * people * (words + n_chosen), transcendentals=0),
         name="traits",
     )(half, to_digits, freq, residuals, weight, chosen)
-    return out[:-2], out[-2:]
-
-
-def decode_kernel(half_ref, to_digits_ref, freq_ref, planes_ref, order_ref):
-    order = to_digits_ref[...]
-    for group in range(order_ref.shape[1] // GROUP):
-        span = slice(group * GROUP, (group + 1) * GROUP)
+    return out[:-3], out[-3:]
+
+
+def decode_kernel(half_ref, planes_ref):
+    for group in range(planes_ref.shape[1] // GROUP):
         word = half_ref[:, group * LANES:(group + 1) * LANES].astype(jnp.float32).astype(jnp.int32)
-        planes_ref[:, span] = jnp.concatenate(digits(word), axis=1)
-        moved = moved_freq(freq_ref, group, order)
-        order_ref[:, span] = moved[:8] + moved[8:16] + moved[16:]
-
-
-def decode(half, to_digits, freq):
+        planes_ref[:, group * GROUP:(group + 1) * GROUP] = jnp.concatenate(digits(word), axis=1)
+
+
+def decode(half):
     people, words = half.shape
     markers = words * PER_WORD
     return pl.pallas_call(
         decode_kernel,
-        out_shape=(
-            jax.ShapeDtypeStruct((people, markers), jnp.bfloat16),
-            jax.ShapeDtypeStruct((8, markers), jnp.float32),
-        ),
-        in_specs=[IN_VMEM] * 3,
-        out_specs=(IN_VMEM,) * 2,
+        out_shape=jax.ShapeDtypeStruct((people, markers), jnp.bfloat16),
+        in_specs=[IN_VMEM],
+        out_specs=IN_VMEM,
         compiler_params=pltpu.CompilerParams(vmem_limit_bytes=VMEM_LIMIT),
         cost_estimate=pl.CostEstimate(flops=people * markers * 16, bytes_accessed=4 * people * markers, transcendentals=0),
         name="decode",
-    )(half, to_digits, freq)
+    )(half)
 
 
 def gram_of(sketch, residual):
@@ -262,11 +286,13 @@
     return standard(rows, planes, freq)
 
 
-def far_kernel(direct, first_ref, second_ref, residual_ref, weight_ref, *refs):
+def far_kernel(direct, first_ref, first_other_ref, second_ref, second_other_ref, residual_ref, weight_ref, *refs):
     common, trait_refs, refs = refs[:4], refs[4:6], refs[6:]
     relay_ref, straight_ref, kept_ref, across_ref, sketch_ref, gram_ref = refs
     weight = weight_ref[...].reshape(1, -1)
-    sketch = (first_ref[...] + second_ref[...]) * weight
+    sketch = jnp.concatenate(
+        [first_ref[...] + first_other_ref[...], second_ref[...] + second_other_ref[...]], axis=1
+    ) * weight
     sketch_ref[...] = sketch
     gram = gram_of(sketch, residual_ref[...])
     k, room = gram.shape[0], gram_ref.shape[1] - gram.shape[1]
@@ -400,23 +426,32 @@
     groups = markers // GROUP
     direct = people_count == groups and groups == 4
     half, to_digits, to_natural = load_words(genotype)
-    sketch = sketch_partial(half, to_digits, basis, allele_freq)
-    apart = 1
-    while apart * 2 < marker_count:
-        sketch = sketch + from_partner(sketch, "markers", apart)
-        apart *= 2
-    other = from_partner(sketch, "markers", apart)
-    traits, (chosen_freq, gathered) = trait_scores(
+    cut = people // 2
+    apart = marker_count // 2
+
+    def chip_sum(part):
+        step = 1
+        while step < apart:
+            part = part + from_partner(part, "markers", step)
+            step *= 2
+        return part
+    first, arranged, offset = first_sketch(half, to_digits, basis, allele_freq, cut)
+    second = second_sketch(half, arranged, offset, cut)
+    first, second = lax.optimization_barrier((chip_sum(first), second))
+    first_other = from_partner(first, "markers", apart)
+    second = chip_sum(second)
+    second_other = from_partner(second, "markers", apart)
+    traits, (order, chosen_freq, gathered) = trait_scores(
         half, to_digits, allele_freq, residuals, person_weight, block_markers, k, direct
     )
-    planes, order = decode(half, to_digits, allele_freq)
+    planes = decode(half)
     common = planes, order, chosen_freq, gathered
     part_width = gathered.shape[1] // groups
     width = GROUP + part_width
     room = padded(k + r)
     low, high = CUT + room + traits[0].shape[1], width - CUT
     relay, straight, kept, across, sketch, gram = product_call(
-        functools.partial(far_kernel, direct), "far", (sketch, other, residuals, person_weight),
+        functools.partial(far_kernel, direct), "far", (first, first_other, second, second_other, residuals, person_weight),
         common + (traits[FAR], traits[ACROSS]), (low, high, low, high, people, room), people,
     )
 

time: 30.2 us -> 29.5 us (0.977)
  Pallas kernels: 12.9 us -> 11.9 us
  starting transfers between devices: 11.8 us -> 12.7 us
  waiting for transfers between devices: 4.58 us -> 3.93 us
    pallas_call x2 -> x3, Pallas kernels: 5.11 us -> 4.06 us  [the longest x1 1.52 us: decode(): pl.pallas_call(decode_kernel, out_shape=jax.ShapeDtypeStruct((people, mar...]
    ppermute x7 -> x9, starting transfers between devices: 11.8 us -> 12.7 us  [from_partner(): return lax.ppermute(block, axis, route)]
    ppermute x7 -> x9, waiting for transfers between devices: 4.58 us -> 3.93 us  [from_partner(): return lax.ppermute(block, axis, route)]
  transfers between devices with their start and end apart: 7 -> 9, of which waited for: 4 -> 3; matrix products, arithmetic and copies ran while one was open for 0% -> 0% of each run, Pallas kernels for 19% -> 19%
where the time goes in v9:
time: 29.5 us; the launch traced here: 29.4 us
  starting transfers between devices  12.7 us (43%)
  Pallas kernels  11.9 us (40%)
  waiting for transfers between devices  3.93 us (13%)
  between operations  0.8 us (3%)
    ppermute x9, starting transfers between devices, from_partner(): return lax.ppermute(block, axis, route)  12.7 us
    ppermute x9, waiting for transfers between devices, from_partner(): return lax.ppermute(block, axis, route)  3.93 us
    pallas_call x1, Pallas kernels, finish(): pl.pallas_call(functools.partial(finish_kernel, root_people, r, width, di...  2.04 us
    pallas_call x1, Pallas kernels, load_words(): pl.pallas_call(load_kernel, out_shape=(jax.ShapeDtypeStruct(genotype.shap...  1.97 us
    pallas_call x1, Pallas kernels, trait_scores(): pl.pallas_call(functools.partial(trait_kernel, direct), out_shape=(jax.Sh...  1.95 us
    pallas_call x3, Pallas kernels, product_call(): pl.pallas_call(kernel, out_shape=tuple((jax.ShapeDtypeStruct((k, width),...  1.84 us
    pallas_call x1, Pallas kernels, decode(): pl.pallas_call(decode_kernel, out_shape=jax.ShapeDtypeStruct((people, mar...  1.52 us
    pallas_call x1, Pallas kernels, first_sketch(): pl.pallas_call(first_sketch_kernel, out_shape=(jax.ShapeDtypeStruct((k, c...  1.44 us
  transfers between devices with their start and end apart: 9, of which 3 were waited for; matrix products, arithmetic and copies ran while one was open for 0% of the time, Pallas kernels for 19%

profile of v9, /device:TPU:0, one launch (start us, length us, event | category | flops | bytes accessed | tf_op | source)
XLA Modules:
  0.0 29.4 jit_solution(4783251580914240662)
XLA Ops:
  0.6 0.0 copy-start.3
  0.6 0.0 copy-start.1
  0.7 2.0 %load.1 = (bf16[1536,512]{1,0:T(8,128)(2,1)S(1)}, bf16[512,512]{1,0:T(8,128)(2,1)S(1)}, bf16[512,512]{1,0:T(8,128)(2,1)S(1)}) custom-call(s32[1536,512]{1,0:T(8,128)} %words_ref.1), custom_call_target="tpu_custom_call" | custom-call | bytes 4718592 | tf_op jit(solution)/shard_map/load/pallas_call | solution.py:95
  2.6 0.0 copy-done.3
  2.6 0.0 copy-done.1
  2.7 1.4 %sketch.1 = (f32[32,768]{1,0:T(8,128)S(1)}, bf16[64,2048]{1,0:T(8,128)(2,1)S(1)}, f32[32,128]{1,0:T(8,128)S(1)}) custom-call(bf16[1536,512]{1,0:T(8,128)(2,1)S(1)} %get-tuple-element.29.half_ref, bf16[512,512]{1,0:T(8,128)(2,1)S(1)} %get-tuple-element.30.to_digits_ref, bf16[32,2048]{1,0:T(8,128)(2,1)S(1)} %copy-done.1, f32[2048]{0:T(1024)S(1)} %copy-done.3), custom_call_target="tpu_custom_call" | custom-call | tf_op jit(solution)/shard_map/sketch/pallas_call | solution.py:141
  4.1 0.5 %collective-permute-start = (f32[32,768]{1,0:T(8,128)S(1)}, f32[32,768]{1,0:T(8,128)S(1)}, u32[]{:S(2)}, u32[]{:S(2)}) collective-permute-start(f32[32,768]{1,0:T(8,128)S(1)} %get-tuple-element.31), channel_id=1, source_target_pairs={{0,1},{1,0},{2,3},{3,2},{4,5},{5,4},{6,7},{7,6},{8,9},{9,8},{10,11... | collective-permute-start | bytes 294920 | tf_op jit(solution)/shard_map/ppermute | solution.py:26
  4.6 1.1 %more.1 = f32[32,768]{1,0:T(8,128)S(1)} custom-call(bf16[1536,512]{1,0:T(8,128)(2,1)S(1)} %get-tuple-element.29.half_ref, bf16[64,2048]{1,0:T(8,128)(2,1)S(1)} %get-tuple-element.32.arranged_ref, f32[32,128]{1,0:T(8,128)S(1)} %get-tuple-element.33.offset_ref), custom_call_target="tpu_custom_call" | custom-call | tf_op jit(solution)/shard_map/more/pallas_call | solution.py:161
  5.7 0.0 collective-permute-done
  5.7 0.2 collective-permute-start.2
  6.0 2.8 %collective-permute-start.1 = (f32[32,768]{1,0:T(8,128)S(1)}, f32[32,768]{1,0:T(8,128)S(1)}, u32[]{:S(2)}, u32[]{:S(2)}) collective-permute-start(f32[32,768]{1,0:T(8,128)S(1)} %add.9.first_ref), channel_id=1, source_target_pairs={{0,2},{1,3},{2,0},{3,1},{4,6},{5,7},{6,4},{7,5},{8,10},{9,11},{10,... | collective-permute-start | bytes 294920 | tf_op jit(solution)/shard_map/ppermute | solution.py:26
  8.8 0.0 collective-permute-done.2
  8.8 0.0 copy-start
  8.8 0.0 copy-start.2
  8.8 0.0 copy-start.4
  8.8 1.0 %collective-permute-start.3 = (f32[32,768]{1,0:T(8,128)S(1)}, f32[32,768]{1,0:T(8,128)S(1)}, u32[]{:S(2)}, u32[]{:S(2)}) collective-permute-start(f32[32,768]{1,0:T(8,128)S(1)} %add.10.second_ref), channel_id=1, source_target_pairs={{0,2},{1,3},{2,0},{3,1},{4,6},{5,7},{6,4},{7,5},{8,10},{9,11},{10,... | collective-permute-start | bytes 294920 | tf_op jit(solution)/shard_map/ppermute | solution.py:26
  9.9 1.5 %decode.1.refs_0_ = bf16[1536,2048]{1,0:T(8,128)(2,1)S(1)} custom-call(bf16[1536,512]{1,0:T(8,128)(2,1)S(1)} %get-tuple-element.29.half_ref), custom_call_target="tpu_custom_call" | custom-call | flops 50331648 | bytes 12582912 | tf_op jit(solution)/shard_map/decode/pallas_call | solution.py:250
  11.4 0.0 copy-done
  11.4 0.0 copy-done.2
  11.4 0.0 copy-done.4
  11.4 1.9 %traits.1 = (f32[32,256]{1,0:T(8,128)S(1)}, f32[32,256]{1,0:T(8,128)S(1)}, f32[32,256]{1,0:T(8,128)S(1)}, f32[32,256]{1,0:T(8,128)S(1)}, f32[8,2048]{1,0:T(8,128...) custom-call(bf16[1536,512]{1,0:T(8,128)(2,1)S(1)} %get-tuple-element.29.half_ref, ...), custom_call_target="tpu_custom_call" | custom-call | flops 1006632960 | bytes 3145728 | tf_op jit(solution)/shard_map/traits/pallas_call | solution.py:224
  13.4 0.0 collective-permute-done.1.first_other_ref
  13.4 0.6 %collective-permute-done.3.second_other_ref = f32[32,768]{1,0:T(8,128)S(1)} collective-permute-done((f32[32,768]{1,0:T(8,128)S(1)}, f32[32,768]{1,0:T(8,128)S(1)}, u32[]{:S(2)}, u32[]{:S(2)}) %collective-permute-start.3) | collective-permute-done | bytes 98336 | tf_op jit(solution)/shard_map/ppermute | solution.py:26
  14.0 0.9 %far.1 = (f32[32,512]{1,0:T(8,128)S(1)}, f32[32,512]{1,0:T(8,128)S(1)}, f32[32,512]{1,0:T(8,128)S(1)}, f32[32,512]{1,0:T(8,128)S(1)}, f32[32,1536]{1,0:T(8,128)S(1)}, /*index=5*/f32[32,128]{1,0:T(8,128)S(1)}) custom-call(f32[32,768]{1,0:T(8,128)S(1)} %add.9.first_ref, f32[32,768]{1,0:T(8,128)S(1)} %collective-permute-done.1.first_other_ref, ...), custom_call_target="tpu_custom_call" | custom-call | flops 729808896 | bytes 11403264 | tf_op jit(solution)/shard_map/far/pallas_call | solution.py:328
  14.9 1.9 %collective-permute-start.5 = (f32[32,768]{1,0:T(8,128)S(1)}, f32[32,768]{1,0:T(8,128)S(1)}, u32[]{:S(2)}, u32[]{:S(2)}) collective-permute-start(f32[32,768]{1,0:T(8,128)S(1)} %pad_maximum_fusion), channel_id=1, source_target_pairs={{0,4},{4,0},{8,12},{12,8},{1,5},{5,1},{9,13},{13,9},{2,6},{6,2},{1... | collective-permute-start | bytes 294920 | tf_op jit(solution)/shard_map/ppermute | solution.py:26
  16.8 2.5 %collective-permute-start.7 = (f32[32,512]{1,0:T(8,128)S(1)}, f32[32,512]{1,0:T(8,128)S(1)}, u32[]{:S(2)}, u32[]{:S(2)}) collective-permute-start(f32[32,512]{1,0:T(8,128)S(1)} %get-tuple-element.48), channel_id=1, source_target_pairs={{0,12},{4,8},{8,4},{12,0},{1,13},{5,9},{9,5},{13,1},{2,14},{6,10},... | collective-permute-start | bytes 196616 | tf_op jit(solution)/shard_map/ppermute | solution.py:26
  19.3 0.1 collective-permute-start.8
  19.4 0.5 %near.1 = f32[32,1024]{1,0:T(8,128)S(1)} custom-call(f32[32,1536]{1,0:T(8,128)S(1)} %get-tuple-element.41.sketch_ref, f32[1536]{0:T(1024)S(1)} %copy-done.2, f32[32,128]{1,0:T(8,128)S(1)} %get-tuple-element.43.gram_ref, bf16[1536,2048]{1,0:T(8,128)(2,1)S(1)} %decode.1.refs_0_, f32[8,2048]{1,0:T(8,128)S(1)} %get-tuple-element.36.refs_1_, ...), custom_call_target="tpu_custom_call" | custom-call | flops 201326592 | bytes 3145728 | tf_op jit(solution)/shard_map/near/pallas_call | solution.py:328
  19.9 1.8 %collective-permute-start.4 = (f32[32,640]{1,0:T(8,128)S(1)}, f32[32,640]{1,0:T(8,128)S(1)}, u32[]{:S(2)}, u32[]{:S(2)}) collective-permute-start(f32[32,640]{1,0:T(8,128)S(1)} %slice.8), channel_id=1, source_target_pairs={{0,4},{4,0},{8,12},{12,8},{1,5},{5,1},{9,13},{13,9},{2,6},{6,2},{1... | collective-permute-start | bytes 245768 | tf_op jit(solution)/shard_map/ppermute | solution.py:26
  21.8 0.0 collective-permute-done.5.refs_1_
  21.8 1.8 %collective-permute-start.6 = (f32[32,512]{1,0:T(8,128)S(1)}, f32[32,512]{1,0:T(8,128)S(1)}, u32[]{:S(2)}, u32[]{:S(2)}) collective-permute-start(f32[32,512]{1,0:T(8,128)S(1)} %slice_add_fusion), channel_id=1, source_target_pairs={{0,8},{4,12},{8,0},{12,4},{1,9},{5,13},{9,1},{13,5},{2,10},{6,14},... | collective-permute-start | bytes 196616 | tf_op jit(solution)/shard_map/ppermute | solution.py:26
  23.5 0.5 %own.1.own_ref = f32[32,1024]{1,0:T(8,128)S(1)} custom-call(f32[32,1536]{1,0:T(8,128)S(1)} %get-tuple-element.41.sketch_ref, f32[1536]{0:T(1024)S(1)} %copy-done.2, f32[32,128]{1,0:T(8,128)S(1)} %get-tuple-element.43.gram_ref, bf16[1536,2048]{1,0:T(8,128)(2,1)S(1)} %decode.1.refs_0_, f32[8,2048]{1,0:T(8,128)S(1)} %get-tuple-element.36.refs_1_, ...), custom_call_target="tpu_custom_call" | custom-call | flops 201326592 | bytes 3145728 | tf_op jit(solution)/shard_map/own/pallas_call | solution.py:328
  24.0 0.0 collective-permute-done.7.refs_3_
  24.0 2.6 %collective-permute-done.8.refs_4_ = f32[32,512]{1,0:T(8,128)S(1)} collective-permute-done((f32[32,512]{1,0:T(8,128)S(1)}, f32[32,512]{1,0:T(8,128)S(1)}, u32[]{:S(2)}, u32[]{:S(2)}) %collective-permute-start.8) | collective-permute-done | bytes 65568 | tf_op jit(solution)/shard_map/ppermute | solution.py:26
  26.6 0.0 collective-permute-done.4.refs_0_
  26.6 0.7 %collective-permute-done.6.refs_2_ = f32[32,512]{1,0:T(8,128)S(1)} collective-permute-done((f32[32,512]{1,0:T(8,128)S(1)}, f32[32,512]{1,0:T(8,128)S(1)}, u32[]{:S(2)}, u32[]{:S(2)}) %collective-permute-start.6) | collective-permute-done | bytes 65568 | tf_op jit(solution)/shard_map/ppermute | solution.py:26
  27.3 2.0 %finish.1 = (f32[32,1536]{1,0:T(8,128)}, f32[32,64]{1,0:T(8,128)}, f32[32,512]{1,0:T(8,128)}, f32[64,128]{1,0:T(8,128)}) custom-call(f32[32,1536]{1,0:T(8,128)S(1)} %get-tuple-element.41.sketch_ref, bf16[512,512]{1,0:T(8,128)(2,1)S(1)} %get-tuple-element.42.to_natural_ref, f32[32,1024]{1,0:T(8,128)S(1)} %own.1.own_ref, ...), custom_call_target="tpu_custom_call" | custom-call | tf_op jit(solution)/shard_map/finish/pallas_call | solution.py:405
  (5 shorter events, 0.1 us)
Async XLA Ops:
  0.6 2.0 %copy-start.3 = (f32[2048]{0:T(1024)S(1)}, f32[2048]{0:T(1024)}, u32[]{:S(2)}) copy-start(f32[2048]{0:T(1024)} %freq_ref.3) | copy-start | bytes 24580
  0.6 2.0 %copy-start.1 = (bf16[32,2048]{1,0:T(8,128)(2,1)S(1)}, bf16[32,2048]{1,0:T(8,128)(2,1)}, u32[]{:S(2)}) copy-start(bf16[32,2048]{1,0:T(8,128)(2,1)} %basis_ref.1) | copy-start | bytes 393220
  4.1 1.6 %collective-permute-start = (f32[32,768]{1,0:T(8,128)S(1)}, f32[32,768]{1,0:T(8,128)S(1)}, u32[]{:S(2)}, u32[]{:S(2)}) collective-permute-start(f32[32,768]{1,0:T(8,128)S(1)} %get-tuple-element.31), channel_id=1, source_target_pairs={{0,1},{1,0},{2,3},{3,2},{4,5},{5,4},{6,7},{7,6},{8,9},{9,8},{10,11... | collective-permute-start | bytes 294920 | tf_op jit(solution)/shard_map/ppermute | solution.py:26
  5.7 3.1 %collective-permute-start.2 = (f32[32,768]{1,0:T(8,128)S(1)}, f32[32,768]{1,0:T(8,128)S(1)}, u32[]{:S(2)}, u32[]{:S(2)}) collective-permute-start(f32[32,768]{1,0:T(8,128)S(1)} %more.1), channel_id=1, source_target_pairs={{0,1},{1,0},{2,3},{3,2},{4,5},{5,4},{6,7},{7,6},{8,9},{9,8},{10,11... | collective-permute-start | bytes 294920 | tf_op jit(solution)/shard_map/ppermute | solution.py:26
  6.0 7.4 %collective-permute-start.1 = (f32[32,768]{1,0:T(8,128)S(1)}, f32[32,768]{1,0:T(8,128)S(1)}, u32[]{:S(2)}, u32[]{:S(2)}) collective-permute-start(f32[32,768]{1,0:T(8,128)S(1)} %add.9.first_ref), channel_id=1, source_target_pairs={{0,2},{1,3},{2,0},{3,1},{4,6},{5,7},{6,4},{7,5},{8,10},{9,11},{10,... | collective-permute-start | bytes 294920 | tf_op jit(solution)/shard_map/ppermute | solution.py:26
  8.8 2.6 %copy-start = (bf16[64,1536]{1,0:T(8,128)(2,1)S(1)}, bf16[64,1536]{1,0:T(8,128)(2,1)}, u32[]{:S(2)}) copy-start(bf16[64,1536]{1,0:T(8,128)(2,1)} %residual_ref.3) | copy-start | bytes 589828
  8.8 2.6 %copy-start.2 = (f32[1536]{0:T(1024)S(1)}, f32[1536]{0:T(1024)}, u32[]{:S(2)}) copy-start(f32[1536]{0:T(1024)} %weight_ref.7) | copy-start | bytes 18436
  8.8 2.6 %copy-start.4 = (s32[512]{0:T(512)S(1)}, s32[512]{0:T(512)}, u32[]{:S(2)}) copy-start(s32[512]{0:T(512)} %chosen_ref.1) | copy-start | bytes 6148
  8.8 5.2 %collective-permute-start.3 = (f32[32,768]{1,0:T(8,128)S(1)}, f32[32,768]{1,0:T(8,128)S(1)}, u32[]{:S(2)}, u32[]{:S(2)}) collective-permute-start(f32[32,768]{1,0:T(8,128)S(1)} %add.10.second_ref), channel_id=1, source_target_pairs={{0,2},{1,3},{2,0},{3,1},{4,6},{5,7},{6,4},{7,5},{8,10},{9,11},{10,... | collective-permute-start | bytes 294920 | tf_op jit(solution)/shard_map/ppermute | solution.py:26
  14.9 6.8 %collective-permute-start.5 = (f32[32,768]{1,0:T(8,128)S(1)}, f32[32,768]{1,0:T(8,128)S(1)}, u32[]{:S(2)}, u32[]{:S(2)}) collective-permute-start(f32[32,768]{1,0:T(8,128)S(1)} %pad_maximum_fusion), channel_id=1, source_target_pairs={{0,4},{4,0},{8,12},{12,8},{1,5},{5,1},{9,13},{13,9},{2,6},{6,2},{1... | collective-permute-start | bytes 294920 | tf_op jit(solution)/shard_map/ppermute | solution.py:26
  16.8 7.2 %collective-permute-start.7 = (f32[32,512]{1,0:T(8,128)S(1)}, f32[32,512]{1,0:T(8,128)S(1)}, u32[]{:S(2)}, u32[]{:S(2)}) collective-permute-start(f32[32,512]{1,0:T(8,128)S(1)} %get-tuple-element.48), channel_id=1, source_target_pairs={{0,12},{4,8},{8,4},{12,0},{1,13},{5,9},{9,5},{13,1},{2,14},{6,10},... | collective-permute-start | bytes 196616 | tf_op jit(solution)/shard_map/ppermute | solution.py:26
  19.3 7.3 %collective-permute-start.8 = (f32[32,512]{1,0:T(8,128)S(1)}, f32[32,512]{1,0:T(8,128)S(1)}, u32[]{:S(2)}, u32[]{:S(2)}) collective-permute-start(f32[32,512]{1,0:T(8,128)S(1)} %get-tuple-element.49), channel_id=1, source_target_pairs={{0,8},{4,12},{8,0},{12,4},{1,9},{5,13},{9,1},{13,5},{2,10},{6,14},... | collective-permute-start | bytes 196616 | tf_op jit(solution)/shard_map/ppermute | solution.py:26
  19.9 6.7 %collective-permute-start.4 = (f32[32,640]{1,0:T(8,128)S(1)}, f32[32,640]{1,0:T(8,128)S(1)}, u32[]{:S(2)}, u32[]{:S(2)}) collective-permute-start(f32[32,640]{1,0:T(8,128)S(1)} %slice.8), channel_id=1, source_target_pairs={{0,4},{4,0},{8,12},{12,8},{1,5},{5,1},{9,13},{13,9},{2,6},{6,2},{1... | collective-permute-start | bytes 245768 | tf_op jit(solution)/shard_map/ppermute | solution.py:26
  21.8 5.5 %collective-permute-start.6 = (f32[32,512]{1,0:T(8,128)S(1)}, f32[32,512]{1,0:T(8,128)S(1)}, u32[]{:S(2)}, u32[]{:S(2)}) collective-permute-start(f32[32,512]{1,0:T(8,128)S(1)} %slice_add_fusion), channel_id=1, source_target_pairs={{0,8},{4,12},{8,0},{12,4},{1,9},{5,13},{9,1},{13,5},{2,10},{6,14},... | collective-permute-start | bytes 196616 | tf_op jit(solution)/shard_map/ppermute | solution.py:26

commit v10 on v9

--- a/solution.py
+++ b/solution.py
@@ -339,7 +339,7 @@
 def eliminate(system, k):
     row_at = lax.broadcasted_iota(jnp.int32, (k, 1), 0)
     shape = system.shape
-    block = 8
+    block = 16
     for start in range(0, k, block):
         columns = [
             jnp.broadcast_to(system[:, j:j + 1], shape) for j in range(start, start + block)

time: 29.5 us -> 29.4 us (level)
  no operation moved by 1% of the time
where the time goes in v10:
time: 29.4 us; the launch traced here: 29.2 us
  starting transfers between devices  12.7 us (43%)
  Pallas kernels  11.7 us (40%)
  waiting for transfers between devices  3.93 us (13%)
  between operations  0.8 us (3%)
    ppermute x9, starting transfers between devices, from_partner(): return lax.ppermute(block, axis, route)  12.7 us
    ppermute x9, waiting for transfers between devices, from_partner(): return lax.ppermute(block, axis, route)  3.93 us
    pallas_call x1, Pallas kernels, load_words(): pl.pallas_call(load_kernel, out_shape=(jax.ShapeDtypeStruct(genotype.shap...  1.97 us
    pallas_call x1, Pallas kernels, trait_scores(): pl.pallas_call(functools.partial(trait_kernel, direct), out_shape=(jax.Sh...  1.95 us
    pallas_call x1, Pallas kernels, finish(): pl.pallas_call(functools.partial(finish_kernel, root_people, r, width, di...  1.91 us
    pallas_call x3, Pallas kernels, product_call(): pl.pallas_call(kernel, out_shape=tuple((jax.ShapeDtypeStruct((k, width),...  1.84 us
    pallas_call x1, Pallas kernels, decode(): pl.pallas_call(decode_kernel, out_shape=jax.ShapeDtypeStruct((people, mar...  1.52 us
    pallas_call x1, Pallas kernels, first_sketch(): pl.pallas_call(first_sketch_kernel, out_shape=(jax.ShapeDtypeStruct((k, c...  1.44 us
  transfers between devices with their start and end apart: 9, of which 3 were waited for; matrix products, arithmetic and copies ran while one was open for 0% of the time, Pallas kernels for 19%

profile of v10, /device:TPU:0, one launch (start us, length us, event | category | flops | bytes accessed | tf_op | source)
XLA Modules:
  0.0 29.2 jit_solution(5244554705656456717)
XLA Ops:
  0.6 0.0 copy-start.3
  0.6 0.0 copy-start.1
  0.7 2.0 %load.1 = (bf16[1536,512]{1,0:T(8,128)(2,1)S(1)}, bf16[512,512]{1,0:T(8,128)(2,1)S(1)}, bf16[512,512]{1,0:T(8,128)(2,1)S(1)}) custom-call(s32[1536,512]{1,0:T(8,128)} %words_ref.1), custom_call_target="tpu_custom_call" | custom-call | bytes 4718592 | tf_op jit(solution)/shard_map/load/pallas_call | solution.py:95
  2.6 0.0 copy-done.3
  2.6 0.0 copy-done.1
  2.7 1.4 %sketch.1 = (f32[32,768]{1,0:T(8,128)S(1)}, bf16[64,2048]{1,0:T(8,128)(2,1)S(1)}, f32[32,128]{1,0:T(8,128)S(1)}) custom-call(bf16[1536,512]{1,0:T(8,128)(2,1)S(1)} %get-tuple-element.29.half_ref, bf16[512,512]{1,0:T(8,128)(2,1)S(1)} %get-tuple-element.30.to_digits_ref, bf16[32,2048]{1,0:T(8,128)(2,1)S(1)} %copy-done.1, f32[2048]{0:T(1024)S(1)} %copy-done.3), custom_call_target="tpu_custom_call" | custom-call | tf_op jit(solution)/shard_map/sketch/pallas_call | solution.py:141
  4.1 0.5 %collective-permute-start = (f32[32,768]{1,0:T(8,128)S(1)}, f32[32,768]{1,0:T(8,128)S(1)}, u32[]{:S(2)}, u32[]{:S(2)}) collective-permute-start(f32[32,768]{1,0:T(8,128)S(1)} %get-tuple-element.31), channel_id=1, source_target_pairs={{0,1},{1,0},{2,3},{3,2},{4,5},{5,4},{6,7},{7,6},{8,9},{9,8},{10,11... | collective-permute-start | bytes 294920 | tf_op jit(solution)/shard_map/ppermute | solution.py:26
  4.6 1.1 %more.1 = f32[32,768]{1,0:T(8,128)S(1)} custom-call(bf16[1536,512]{1,0:T(8,128)(2,1)S(1)} %get-tuple-element.29.half_ref, bf16[64,2048]{1,0:T(8,128)(2,1)S(1)} %get-tuple-element.32.arranged_ref, f32[32,128]{1,0:T(8,128)S(1)} %get-tuple-element.33.offset_ref), custom_call_target="tpu_custom_call" | custom-call | tf_op jit(solution)/shard_map/more/pallas_call | solution.py:161
  5.7 0.0 collective-permute-done
  5.7 0.2 collective-permute-start.2
  6.0 2.8 %collective-permute-start.1 = (f32[32,768]{1,0:T(8,128)S(1)}, f32[32,768]{1,0:T(8,128)S(1)}, u32[]{:S(2)}, u32[]{:S(2)}) collective-permute-start(f32[32,768]{1,0:T(8,128)S(1)} %add.9.first_ref), channel_id=1, source_target_pairs={{0,2},{1,3},{2,0},{3,1},{4,6},{5,7},{6,4},{7,5},{8,10},{9,11},{10,... | collective-permute-start | bytes 294920 | tf_op jit(solution)/shard_map/ppermute | solution.py:26
  8.8 0.0 collective-permute-done.2
  8.8 0.0 copy-start
  8.8 0.0 copy-start.2
  8.8 0.0 copy-start.4
  8.8 1.0 %collective-permute-start.3 = (f32[32,768]{1,0:T(8,128)S(1)}, f32[32,768]{1,0:T(8,128)S(1)}, u32[]{:S(2)}, u32[]{:S(2)}) collective-permute-start(f32[32,768]{1,0:T(8,128)S(1)} %add.10.second_ref), channel_id=1, source_target_pairs={{0,2},{1,3},{2,0},{3,1},{4,6},{5,7},{6,4},{7,5},{8,10},{9,11},{10,... | collective-permute-start | bytes 294920 | tf_op jit(solution)/shard_map/ppermute | solution.py:26
  9.9 1.5 %decode.1.refs_0_ = bf16[1536,2048]{1,0:T(8,128)(2,1)S(1)} custom-call(bf16[1536,512]{1,0:T(8,128)(2,1)S(1)} %get-tuple-element.29.half_ref), custom_call_target="tpu_custom_call" | custom-call | flops 50331648 | bytes 12582912 | tf_op jit(solution)/shard_map/decode/pallas_call | solution.py:250
  11.4 0.0 copy-done
  11.4 0.0 copy-done.2
  11.4 0.0 copy-done.4
  11.4 1.9 %traits.1 = (f32[32,256]{1,0:T(8,128)S(1)}, f32[32,256]{1,0:T(8,128)S(1)}, f32[32,256]{1,0:T(8,128)S(1)}, f32[32,256]{1,0:T(8,128)S(1)}, f32[8,2048]{1,0:T(8,128...) custom-call(bf16[1536,512]{1,0:T(8,128)(2,1)S(1)} %get-tuple-element.29.half_ref, ...), custom_call_target="tpu_custom_call" | custom-call | flops 1006632960 | bytes 3145728 | tf_op jit(solution)/shard_map/traits/pallas_call | solution.py:224
  13.4 0.0 collective-permute-done.1.first_other_ref
  13.4 0.6 %collective-permute-done.3.second_other_ref = f32[32,768]{1,0:T(8,128)S(1)} collective-permute-done((f32[32,768]{1,0:T(8,128)S(1)}, f32[32,768]{1,0:T(8,128)S(1)}, u32[]{:S(2)}, u32[]{:S(2)}) %collective-permute-start.3) | collective-permute-done | bytes 98336 | tf_op jit(solution)/shard_map/ppermute | solution.py:26
  14.0 0.9 %far.1 = (f32[32,512]{1,0:T(8,128)S(1)}, f32[32,512]{1,0:T(8,128)S(1)}, f32[32,512]{1,0:T(8,128)S(1)}, f32[32,512]{1,0:T(8,128)S(1)}, f32[32,1536]{1,0:T(8,128)S(1)}, /*index=5*/f32[32,128]{1,0:T(8,128)S(1)}) custom-call(f32[32,768]{1,0:T(8,128)S(1)} %add.9.first_ref, f32[32,768]{1,0:T(8,128)S(1)} %collective-permute-done.1.first_other_ref, ...), custom_call_target="tpu_custom_call" | custom-call | flops 729808896 | bytes 11403264 | tf_op jit(solution)/shard_map/far/pallas_call | solution.py:328
  14.9 1.9 %collective-permute-start.5 = (f32[32,768]{1,0:T(8,128)S(1)}, f32[32,768]{1,0:T(8,128)S(1)}, u32[]{:S(2)}, u32[]{:S(2)}) collective-permute-start(f32[32,768]{1,0:T(8,128)S(1)} %pad_maximum_fusion), channel_id=1, source_target_pairs={{0,4},{4,0},{8,12},{12,8},{1,5},{5,1},{9,13},{13,9},{2,6},{6,2},{1... | collective-permute-start | bytes 294920 | tf_op jit(solution)/shard_map/ppermute | solution.py:26
  16.8 2.5 %collective-permute-start.7 = (f32[32,512]{1,0:T(8,128)S(1)}, f32[32,512]{1,0:T(8,128)S(1)}, u32[]{:S(2)}, u32[]{:S(2)}) collective-permute-start(f32[32,512]{1,0:T(8,128)S(1)} %get-tuple-element.48), channel_id=1, source_target_pairs={{0,12},{4,8},{8,4},{12,0},{1,13},{5,9},{9,5},{13,1},{2,14},{6,10},... | collective-permute-start | bytes 196616 | tf_op jit(solution)/shard_map/ppermute | solution.py:26
  19.3 0.1 collective-permute-start.8
  19.4 0.5 %near.1 = f32[32,1024]{1,0:T(8,128)S(1)} custom-call(f32[32,1536]{1,0:T(8,128)S(1)} %get-tuple-element.41.sketch_ref, f32[1536]{0:T(1024)S(1)} %copy-done.2, f32[32,128]{1,0:T(8,128)S(1)} %get-tuple-element.43.gram_ref, bf16[1536,2048]{1,0:T(8,128)(2,1)S(1)} %decode.1.refs_0_, f32[8,2048]{1,0:T(8,128)S(1)} %get-tuple-element.36.refs_1_, ...), custom_call_target="tpu_custom_call" | custom-call | flops 201326592 | bytes 3145728 | tf_op jit(solution)/shard_map/near/pallas_call | solution.py:328
  19.9 1.8 %collective-permute-start.4 = (f32[32,640]{1,0:T(8,128)S(1)}, f32[32,640]{1,0:T(8,128)S(1)}, u32[]{:S(2)}, u32[]{:S(2)}) collective-permute-start(f32[32,640]{1,0:T(8,128)S(1)} %slice.8), channel_id=1, source_target_pairs={{0,4},{4,0},{8,12},{12,8},{1,5},{5,1},{9,13},{13,9},{2,6},{6,2},{1... | collective-permute-start | bytes 245768 | tf_op jit(solution)/shard_map/ppermute | solution.py:26
  21.8 0.0 collective-permute-done.5.refs_1_
  21.8 1.8 %collective-permute-start.6 = (f32[32,512]{1,0:T(8,128)S(1)}, f32[32,512]{1,0:T(8,128)S(1)}, u32[]{:S(2)}, u32[]{:S(2)}) collective-permute-start(f32[32,512]{1,0:T(8,128)S(1)} %slice_add_fusion), channel_id=1, source_target_pairs={{0,8},{4,12},{8,0},{12,4},{1,9},{5,13},{9,1},{13,5},{2,10},{6,14},... | collective-permute-start | bytes 196616 | tf_op jit(solution)/shard_map/ppermute | solution.py:26
  23.5 0.5 %own.1.own_ref = f32[32,1024]{1,0:T(8,128)S(1)} custom-call(f32[32,1536]{1,0:T(8,128)S(1)} %get-tuple-element.41.sketch_ref, f32[1536]{0:T(1024)S(1)} %copy-done.2, f32[32,128]{1,0:T(8,128)S(1)} %get-tuple-element.43.gram_ref, bf16[1536,2048]{1,0:T(8,128)(2,1)S(1)} %decode.1.refs_0_, f32[8,2048]{1,0:T(8,128)S(1)} %get-tuple-element.36.refs_1_, ...), custom_call_target="tpu_custom_call" | custom-call | flops 201326592 | bytes 3145728 | tf_op jit(solution)/shard_map/own/pallas_call | solution.py:328
  24.0 0.0 collective-permute-done.7.refs_3_
  24.0 2.6 %collective-permute-done.8.refs_4_ = f32[32,512]{1,0:T(8,128)S(1)} collective-permute-done((f32[32,512]{1,0:T(8,128)S(1)}, f32[32,512]{1,0:T(8,128)S(1)}, u32[]{:S(2)}, u32[]{:S(2)}) %collective-permute-start.8) | collective-permute-done | bytes 65568 | tf_op jit(solution)/shard_map/ppermute | solution.py:26
  26.6 0.0 collective-permute-done.4.refs_0_
  26.6 0.7 %collective-permute-done.6.refs_2_ = f32[32,512]{1,0:T(8,128)S(1)} collective-permute-done((f32[32,512]{1,0:T(8,128)S(1)}, f32[32,512]{1,0:T(8,128)S(1)}, u32[]{:S(2)}, u32[]{:S(2)}) %collective-permute-start.6) | collective-permute-done | bytes 65568 | tf_op jit(solution)/shard_map/ppermute | solution.py:26
  27.3 1.9 %finish.1 = (f32[32,1536]{1,0:T(8,128)}, f32[32,64]{1,0:T(8,128)}, f32[32,512]{1,0:T(8,128)}, f32[64,128]{1,0:T(8,128)}) custom-call(f32[32,1536]{1,0:T(8,128)S(1)} %get-tuple-element.41.sketch_ref, bf16[512,512]{1,0:T(8,128)(2,1)S(1)} %get-tuple-element.42.to_natural_ref, f32[32,1024]{1,0:T(8,128)S(1)} %own.1.own_ref, ...), custom_call_target="tpu_custom_call" | custom-call | tf_op jit(solution)/shard_map/finish/pallas_call | solution.py:405
  (5 shorter events, 0.1 us)
Async XLA Ops:
  0.6 2.0 %copy-start.3 = (f32[2048]{0:T(1024)S(1)}, f32[2048]{0:T(1024)}, u32[]{:S(2)}) copy-start(f32[2048]{0:T(1024)} %freq_ref.3) | copy-start | bytes 24580
  0.6 2.0 %copy-start.1 = (bf16[32,2048]{1,0:T(8,128)(2,1)S(1)}, bf16[32,2048]{1,0:T(8,128)(2,1)}, u32[]{:S(2)}) copy-start(bf16[32,2048]{1,0:T(8,128)(2,1)} %basis_ref.1) | copy-start | bytes 393220
  4.1 1.6 %collective-permute-start = (f32[32,768]{1,0:T(8,128)S(1)}, f32[32,768]{1,0:T(8,128)S(1)}, u32[]{:S(2)}, u32[]{:S(2)}) collective-permute-start(f32[32,768]{1,0:T(8,128)S(1)} %get-tuple-element.31), channel_id=1, source_target_pairs={{0,1},{1,0},{2,3},{3,2},{4,5},{5,4},{6,7},{7,6},{8,9},{9,8},{10,11... | collective-permute-start | bytes 294920 | tf_op jit(solution)/shard_map/ppermute | solution.py:26
  5.7 3.1 %collective-permute-start.2 = (f32[32,768]{1,0:T(8,128)S(1)}, f32[32,768]{1,0:T(8,128)S(1)}, u32[]{:S(2)}, u32[]{:S(2)}) collective-permute-start(f32[32,768]{1,0:T(8,128)S(1)} %more.1), channel_id=1, source_target_pairs={{0,1},{1,0},{2,3},{3,2},{4,5},{5,4},{6,7},{7,6},{8,9},{9,8},{10,11... | collective-permute-start | bytes 294920 | tf_op jit(solution)/shard_map/ppermute | solution.py:26
  6.0 7.4 %collective-permute-start.1 = (f32[32,768]{1,0:T(8,128)S(1)}, f32[32,768]{1,0:T(8,128)S(1)}, u32[]{:S(2)}, u32[]{:S(2)}) collective-permute-start(f32[32,768]{1,0:T(8,128)S(1)} %add.9.first_ref), channel_id=1, source_target_pairs={{0,2},{1,3},{2,0},{3,1},{4,6},{5,7},{6,4},{7,5},{8,10},{9,11},{10,... | collective-permute-start | bytes 294920 | tf_op jit(solution)/shard_map/ppermute | solution.py:26
  8.8 2.6 %copy-start = (bf16[64,1536]{1,0:T(8,128)(2,1)S(1)}, bf16[64,1536]{1,0:T(8,128)(2,1)}, u32[]{:S(2)}) copy-start(bf16[64,1536]{1,0:T(8,128)(2,1)} %residual_ref.3) | copy-start | bytes 589828
  8.8 2.6 %copy-start.2 = (f32[1536]{0:T(1024)S(1)}, f32[1536]{0:T(1024)}, u32[]{:S(2)}) copy-start(f32[1536]{0:T(1024)} %weight_ref.7) | copy-start | bytes 18436
  8.8 2.6 %copy-start.4 = (s32[512]{0:T(512)S(1)}, s32[512]{0:T(512)}, u32[]{:S(2)}) copy-start(s32[512]{0:T(512)} %chosen_ref.1) | copy-start | bytes 6148
  8.8 5.2 %collective-permute-start.3 = (f32[32,768]{1,0:T(8,128)S(1)}, f32[32,768]{1,0:T(8,128)S(1)}, u32[]{:S(2)}, u32[]{:S(2)}) collective-permute-start(f32[32,768]{1,0:T(8,128)S(1)} %add.10.second_ref), channel_id=1, source_target_pairs={{0,2},{1,3},{2,0},{3,1},{4,6},{5,7},{6,4},{7,5},{8,10},{9,11},{10,... | collective-permute-start | bytes 294920 | tf_op jit(solution)/shard_map/ppermute | solution.py:26
  14.9 6.8 %collective-permute-start.5 = (f32[32,768]{1,0:T(8,128)S(1)}, f32[32,768]{1,0:T(8,128)S(1)}, u32[]{:S(2)}, u32[]{:S(2)}) collective-permute-start(f32[32,768]{1,0:T(8,128)S(1)} %pad_maximum_fusion), channel_id=1, source_target_pairs={{0,4},{4,0},{8,12},{12,8},{1,5},{5,1},{9,13},{13,9},{2,6},{6,2},{1... | collective-permute-start | bytes 294920 | tf_op jit(solution)/shard_map/ppermute | solution.py:26
  16.8 7.2 %collective-permute-start.7 = (f32[32,512]{1,0:T(8,128)S(1)}, f32[32,512]{1,0:T(8,128)S(1)}, u32[]{:S(2)}, u32[]{:S(2)}) collective-permute-start(f32[32,512]{1,0:T(8,128)S(1)} %get-tuple-element.48), channel_id=1, source_target_pairs={{0,12},{4,8},{8,4},{12,0},{1,13},{5,9},{9,5},{13,1},{2,14},{6,10},... | collective-permute-start | bytes 196616 | tf_op jit(solution)/shard_map/ppermute | solution.py:26
  19.3 7.3 %collective-permute-start.8 = (f32[32,512]{1,0:T(8,128)S(1)}, f32[32,512]{1,0:T(8,128)S(1)}, u32[]{:S(2)}, u32[]{:S(2)}) collective-permute-start(f32[32,512]{1,0:T(8,128)S(1)} %get-tuple-element.49), channel_id=1, source_target_pairs={{0,8},{4,12},{8,0},{12,4},{1,9},{5,13},{9,1},{13,5},{2,10},{6,14},... | collective-permute-start | bytes 196616 | tf_op jit(solution)/shard_map/ppermute | solution.py:26
  19.9 6.7 %collective-permute-start.4 = (f32[32,640]{1,0:T(8,128)S(1)}, f32[32,640]{1,0:T(8,128)S(1)}, u32[]{:S(2)}, u32[]{:S(2)}) collective-permute-start(f32[32,640]{1,0:T(8,128)S(1)} %slice.8), channel_id=1, source_target_pairs={{0,4},{4,0},{8,12},{12,8},{1,5},{5,1},{9,13},{13,9},{2,6},{6,2},{1... | collective-permute-start | bytes 245768 | tf_op jit(solution)/shard_map/ppermute | solution.py:26
  21.8 5.5 %collective-permute-start.6 = (f32[32,512]{1,0:T(8,128)S(1)}, f32[32,512]{1,0:T(8,128)S(1)}, u32[]{:S(2)}, u32[]{:S(2)}) collective-permute-start(f32[32,512]{1,0:T(8,128)S(1)} %slice_add_fusion), channel_id=1, source_target_pairs={{0,8},{4,12},{8,0},{12,4},{1,9},{5,13},{9,1},{13,5},{2,10},{6,14},... | collective-permute-start | bytes 196616 | tf_op jit(solution)/shard_map/ppermute | solution.py:26

commit v11 on v10

--- a/solution.py
+++ b/solution.py
@@ -127,8 +127,11 @@
     order = to_digits_ref[...]
     stacked = jnp.concatenate(split2(scaled), axis=0)
     pieces = [[] for _ in range(PER_WORD)]
-    for group in range(markers // GROUP):
-        moved = dot32(stacked[:, group * GROUP:(group + 1) * GROUP], order).astype(jnp.bfloat16)
+    groups = markers // GROUP
+    tall = jnp.concatenate([stacked[:, group * GROUP:(group + 1) * GROUP] for group in range(groups)], axis=0)
+    tall = dot32(tall, order).astype(jnp.bfloat16)
+    for group in range(groups):
+        moved = tall[2 * k * group:2 * k * (group + 1)]
         for j in range(PER_WORD):
             pieces[j].append(moved[:, j * LANES:(j + 1) * LANES])
     arranged = jnp.concatenate([piece for one in pieces for piece in one], axis=1)

time: 29.4 us -> 29.3 us (level)
  no operation moved by 1% of the time
where the time goes in v11:
time: 29.3 us; the launch traced here: 29.1 us
  starting transfers between devices  12.7 us (43%)
  Pallas kernels  11.6 us (40%)
  waiting for transfers between devices  3.91 us (13%)
  between operations  0.81 us (3%)
    ppermute x9, starting transfers between devices, from_partner(): return lax.ppermute(block, axis, route)  12.7 us
    ppermute x9, waiting for transfers between devices, from_partner(): return lax.ppermute(block, axis, route)  3.91 us
    pallas_call x1, Pallas kernels, load_words(): pl.pallas_call(load_kernel, out_shape=(jax.ShapeDtypeStruct(genotype.shap...  1.97 us
    pallas_call x1, Pallas kernels, trait_scores(): pl.pallas_call(functools.partial(trait_kernel, direct), out_shape=(jax.Sh...  1.95 us
    pallas_call x1, Pallas kernels, finish(): pl.pallas_call(functools.partial(finish_kernel, root_people, r, width, di...  1.92 us
    pallas_call x3, Pallas kernels, product_call(): pl.pallas_call(kernel, out_shape=tuple((jax.ShapeDtypeStruct((k, width),...  1.83 us
    pallas_call x1, Pallas kernels, decode(): pl.pallas_call(decode_kernel, out_shape=jax.ShapeDtypeStruct((people, mar...  1.52 us
    pallas_call x1, Pallas kernels, first_sketch(): pl.pallas_call(first_sketch_kernel, out_shape=(jax.ShapeDtypeStruct((k, c...  1.33 us
  transfers between devices with their start and end apart: 9, of which 3 were waited for; matrix products, arithmetic and copies ran while one was open for 0% of the time, Pallas kernels for 19%

profile of v11, /device:TPU:0, one launch (start us, length us, event | category | flops | bytes accessed | tf_op | source)
XLA Modules:
  0.0 29.1 jit_solution(12239716740244499385)
XLA Ops:
  0.6 0.0 copy-start.3
  0.6 0.0 copy-start.1
  0.7 2.0 %load.1 = (bf16[1536,512]{1,0:T(8,128)(2,1)S(1)}, bf16[512,512]{1,0:T(8,128)(2,1)S(1)}, bf16[512,512]{1,0:T(8,128)(2,1)S(1)}) custom-call(s32[1536,512]{1,0:T(8,128)} %words_ref.1), custom_call_target="tpu_custom_call" | custom-call | bytes 4718592 | tf_op jit(solution)/shard_map/load/pallas_call | solution.py:95
  2.6 0.0 copy-done.3
  2.6 0.0 copy-done.1
  2.7 1.3 %sketch.1 = (f32[32,768]{1,0:T(8,128)S(1)}, bf16[64,2048]{1,0:T(8,128)(2,1)S(1)}, f32[32,128]{1,0:T(8,128)S(1)}) custom-call(bf16[1536,512]{1,0:T(8,128)(2,1)S(1)} %get-tuple-element.29.half_ref, bf16[512,512]{1,0:T(8,128)(2,1)S(1)} %get-tuple-element.30.to_digits_ref, bf16[32,2048]{1,0:T(8,128)(2,1)S(1)} %copy-done.1, f32[2048]{0:T(1024)S(1)} %copy-done.3), custom_call_target="tpu_custom_call" | custom-call | tf_op jit(solution)/shard_map/sketch/pallas_call | solution.py:144
  4.0 0.5 %collective-permute-start = (f32[32,768]{1,0:T(8,128)S(1)}, f32[32,768]{1,0:T(8,128)S(1)}, u32[]{:S(2)}, u32[]{:S(2)}) collective-permute-start(f32[32,768]{1,0:T(8,128)S(1)} %get-tuple-element.31), channel_id=1, source_target_pairs={{0,1},{1,0},{2,3},{3,2},{4,5},{5,4},{6,7},{7,6},{8,9},{9,8},{10,11... | collective-permute-start | bytes 294920 | tf_op jit(solution)/shard_map/ppermute | solution.py:26
  4.5 1.1 %more.1 = f32[32,768]{1,0:T(8,128)S(1)} custom-call(bf16[1536,512]{1,0:T(8,128)(2,1)S(1)} %get-tuple-element.29.half_ref, bf16[64,2048]{1,0:T(8,128)(2,1)S(1)} %get-tuple-element.32.arranged_ref, f32[32,128]{1,0:T(8,128)S(1)} %get-tuple-element.33.offset_ref), custom_call_target="tpu_custom_call" | custom-call | tf_op jit(solution)/shard_map/more/pallas_call | solution.py:164
  5.6 0.0 collective-permute-done
  5.6 0.2 collective-permute-start.2
  5.8 2.8 %collective-permute-start.1 = (f32[32,768]{1,0:T(8,128)S(1)}, f32[32,768]{1,0:T(8,128)S(1)}, u32[]{:S(2)}, u32[]{:S(2)}) collective-permute-start(f32[32,768]{1,0:T(8,128)S(1)} %add.9.first_ref), channel_id=1, source_target_pairs={{0,2},{1,3},{2,0},{3,1},{4,6},{5,7},{6,4},{7,5},{8,10},{9,11},{10,... | collective-permute-start | bytes 294920 | tf_op jit(solution)/shard_map/ppermute | solution.py:26
  8.7 0.0 collective-permute-done.2
  8.7 0.0 copy-start
  8.7 0.0 copy-start.2
  8.7 0.0 copy-start.4
  8.7 1.0 %collective-permute-start.3 = (f32[32,768]{1,0:T(8,128)S(1)}, f32[32,768]{1,0:T(8,128)S(1)}, u32[]{:S(2)}, u32[]{:S(2)}) collective-permute-start(f32[32,768]{1,0:T(8,128)S(1)} %add.10.second_ref), channel_id=1, source_target_pairs={{0,2},{1,3},{2,0},{3,1},{4,6},{5,7},{6,4},{7,5},{8,10},{9,11},{10,... | collective-permute-start | bytes 294920 | tf_op jit(solution)/shard_map/ppermute | solution.py:26
  9.7 1.5 %decode.1.refs_0_ = bf16[1536,2048]{1,0:T(8,128)(2,1)S(1)} custom-call(bf16[1536,512]{1,0:T(8,128)(2,1)S(1)} %get-tuple-element.29.half_ref), custom_call_target="tpu_custom_call" | custom-call | flops 50331648 | bytes 12582912 | tf_op jit(solution)/shard_map/decode/pallas_call | solution.py:253
  11.3 0.0 copy-done
  11.3 0.0 copy-done.2
  11.3 0.0 copy-done.4
  11.3 1.9 %traits.1 = (f32[32,256]{1,0:T(8,128)S(1)}, f32[32,256]{1,0:T(8,128)S(1)}, f32[32,256]{1,0:T(8,128)S(1)}, f32[32,256]{1,0:T(8,128)S(1)}, f32[8,2048]{1,0:T(8,128...) custom-call(bf16[1536,512]{1,0:T(8,128)(2,1)S(1)} %get-tuple-element.29.half_ref, ...), custom_call_target="tpu_custom_call" | custom-call | flops 1006632960 | bytes 3145728 | tf_op jit(solution)/shard_map/traits/pallas_call | solution.py:227
  13.2 0.0 collective-permute-done.1.first_other_ref
  13.3 0.6 %collective-permute-done.3.second_other_ref = f32[32,768]{1,0:T(8,128)S(1)} collective-permute-done((f32[32,768]{1,0:T(8,128)S(1)}, f32[32,768]{1,0:T(8,128)S(1)}, u32[]{:S(2)}, u32[]{:S(2)}) %collective-permute-start.3) | collective-permute-done | bytes 98336 | tf_op jit(solution)/shard_map/ppermute | solution.py:26
  13.9 0.9 %far.1 = (f32[32,512]{1,0:T(8,128)S(1)}, f32[32,512]{1,0:T(8,128)S(1)}, f32[32,512]{1,0:T(8,128)S(1)}, f32[32,512]{1,0:T(8,128)S(1)}, f32[32,1536]{1,0:T(8,128)S(1)}, /*index=5*/f32[32,128]{1,0:T(8,128)S(1)}) custom-call(f32[32,768]{1,0:T(8,128)S(1)} %add.9.first_ref, f32[32,768]{1,0:T(8,128)S(1)} %collective-permute-done.1.first_other_ref, ...), custom_call_target="tpu_custom_call" | custom-call | flops 729808896 | bytes 11403264 | tf_op jit(solution)/shard_map/far/pallas_call | solution.py:331
  14.8 1.9 %collective-permute-start.5 = (f32[32,768]{1,0:T(8,128)S(1)}, f32[32,768]{1,0:T(8,128)S(1)}, u32[]{:S(2)}, u32[]{:S(2)}) collective-permute-start(f32[32,768]{1,0:T(8,128)S(1)} %pad_maximum_fusion), channel_id=1, source_target_pairs={{0,4},{4,0},{8,12},{12,8},{1,5},{5,1},{9,13},{13,9},{2,6},{6,2},{1... | collective-permute-start | bytes 294920 | tf_op jit(solution)/shard_map/ppermute | solution.py:26
  16.7 2.5 %collective-permute-start.7 = (f32[32,512]{1,0:T(8,128)S(1)}, f32[32,512]{1,0:T(8,128)S(1)}, u32[]{:S(2)}, u32[]{:S(2)}) collective-permute-start(f32[32,512]{1,0:T(8,128)S(1)} %get-tuple-element.48), channel_id=1, source_target_pairs={{0,12},{4,8},{8,4},{12,0},{1,13},{5,9},{9,5},{13,1},{2,14},{6,10},... | collective-permute-start | bytes 196616 | tf_op jit(solution)/shard_map/ppermute | solution.py:26
  19.2 0.1 collective-permute-start.8
  19.3 0.5 %near.1 = f32[32,1024]{1,0:T(8,128)S(1)} custom-call(f32[32,1536]{1,0:T(8,128)S(1)} %get-tuple-element.41.sketch_ref, f32[1536]{0:T(1024)S(1)} %copy-done.2, f32[32,128]{1,0:T(8,128)S(1)} %get-tuple-element.43.gram_ref, bf16[1536,2048]{1,0:T(8,128)(2,1)S(1)} %decode.1.refs_0_, f32[8,2048]{1,0:T(8,128)S(1)} %get-tuple-element.36.refs_1_, ...), custom_call_target="tpu_custom_call" | custom-call | flops 201326592 | bytes 3145728 | tf_op jit(solution)/shard_map/near/pallas_call | solution.py:331
  19.8 1.8 %collective-permute-start.4 = (f32[32,640]{1,0:T(8,128)S(1)}, f32[32,640]{1,0:T(8,128)S(1)}, u32[]{:S(2)}, u32[]{:S(2)}) collective-permute-start(f32[32,640]{1,0:T(8,128)S(1)} %slice.8), channel_id=1, source_target_pairs={{0,4},{4,0},{8,12},{12,8},{1,5},{5,1},{9,13},{13,9},{2,6},{6,2},{1... | collective-permute-start | bytes 245768 | tf_op jit(solution)/shard_map/ppermute | solution.py:26
  21.6 0.0 collective-permute-done.5.refs_1_
  21.6 1.8 %collective-permute-start.6 = (f32[32,512]{1,0:T(8,128)S(1)}, f32[32,512]{1,0:T(8,128)S(1)}, u32[]{:S(2)}, u32[]{:S(2)}) collective-permute-start(f32[32,512]{1,0:T(8,128)S(1)} %slice_add_fusion), channel_id=1, source_target_pairs={{0,8},{4,12},{8,0},{12,4},{1,9},{5,13},{9,1},{13,5},{2,10},{6,14},... | collective-permute-start | bytes 196616 | tf_op jit(solution)/shard_map/ppermute | solution.py:26
  23.4 0.5 %own.1.own_ref = f32[32,1024]{1,0:T(8,128)S(1)} custom-call(f32[32,1536]{1,0:T(8,128)S(1)} %get-tuple-element.41.sketch_ref, f32[1536]{0:T(1024)S(1)} %copy-done.2, f32[32,128]{1,0:T(8,128)S(1)} %get-tuple-element.43.gram_ref, bf16[1536,2048]{1,0:T(8,128)(2,1)S(1)} %decode.1.refs_0_, f32[8,2048]{1,0:T(8,128)S(1)} %get-tuple-element.36.refs_1_, ...), custom_call_target="tpu_custom_call" | custom-call | flops 201326592 | bytes 3145728 | tf_op jit(solution)/shard_map/own/pallas_call | solution.py:331
  23.9 0.0 collective-permute-done.7.refs_3_
  23.9 2.6 %collective-permute-done.8.refs_4_ = f32[32,512]{1,0:T(8,128)S(1)} collective-permute-done((f32[32,512]{1,0:T(8,128)S(1)}, f32[32,512]{1,0:T(8,128)S(1)}, u32[]{:S(2)}, u32[]{:S(2)}) %collective-permute-start.8) | collective-permute-done | bytes 65568 | tf_op jit(solution)/shard_map/ppermute | solution.py:26
  26.5 0.0 collective-permute-done.4.refs_0_
  26.5 0.7 %collective-permute-done.6.refs_2_ = f32[32,512]{1,0:T(8,128)S(1)} collective-permute-done((f32[32,512]{1,0:T(8,128)S(1)}, f32[32,512]{1,0:T(8,128)S(1)}, u32[]{:S(2)}, u32[]{:S(2)}) %collective-permute-start.6) | collective-permute-done | bytes 65568 | tf_op jit(solution)/shard_map/ppermute | solution.py:26
  27.2 1.9 %finish.1 = (f32[32,1536]{1,0:T(8,128)}, f32[32,64]{1,0:T(8,128)}, f32[32,512]{1,0:T(8,128)}, f32[64,128]{1,0:T(8,128)}) custom-call(f32[32,1536]{1,0:T(8,128)S(1)} %get-tuple-element.41.sketch_ref, bf16[512,512]{1,0:T(8,128)(2,1)S(1)} %get-tuple-element.42.to_natural_ref, f32[32,1024]{1,0:T(8,128)S(1)} %own.1.own_ref, ...), custom_call_target="tpu_custom_call" | custom-call | tf_op jit(solution)/shard_map/finish/pallas_call | solution.py:408
  (5 shorter events, 0.1 us)
Async XLA Ops:
  0.6 2.0 %copy-start.3 = (f32[2048]{0:T(1024)S(1)}, f32[2048]{0:T(1024)}, u32[]{:S(2)}) copy-start(f32[2048]{0:T(1024)} %freq_ref.3) | copy-start | bytes 24580
  0.6 2.0 %copy-start.1 = (bf16[32,2048]{1,0:T(8,128)(2,1)S(1)}, bf16[32,2048]{1,0:T(8,128)(2,1)}, u32[]{:S(2)}) copy-start(bf16[32,2048]{1,0:T(8,128)(2,1)} %basis_ref.1) | copy-start | bytes 393220
  4.0 1.6 %collective-permute-start = (f32[32,768]{1,0:T(8,128)S(1)}, f32[32,768]{1,0:T(8,128)S(1)}, u32[]{:S(2)}, u32[]{:S(2)}) collective-permute-start(f32[32,768]{1,0:T(8,128)S(1)} %get-tuple-element.31), channel_id=1, source_target_pairs={{0,1},{1,0},{2,3},{3,2},{4,5},{5,4},{6,7},{7,6},{8,9},{9,8},{10,11... | collective-permute-start | bytes 294920 | tf_op jit(solution)/shard_map/ppermute | solution.py:26
  5.6 3.1 %collective-permute-start.2 = (f32[32,768]{1,0:T(8,128)S(1)}, f32[32,768]{1,0:T(8,128)S(1)}, u32[]{:S(2)}, u32[]{:S(2)}) collective-permute-start(f32[32,768]{1,0:T(8,128)S(1)} %more.1), channel_id=1, source_target_pairs={{0,1},{1,0},{2,3},{3,2},{4,5},{5,4},{6,7},{7,6},{8,9},{9,8},{10,11... | collective-permute-start | bytes 294920 | tf_op jit(solution)/shard_map/ppermute | solution.py:26
  5.8 7.4 %collective-permute-start.1 = (f32[32,768]{1,0:T(8,128)S(1)}, f32[32,768]{1,0:T(8,128)S(1)}, u32[]{:S(2)}, u32[]{:S(2)}) collective-permute-start(f32[32,768]{1,0:T(8,128)S(1)} %add.9.first_ref), channel_id=1, source_target_pairs={{0,2},{1,3},{2,0},{3,1},{4,6},{5,7},{6,4},{7,5},{8,10},{9,11},{10,... | collective-permute-start | bytes 294920 | tf_op jit(solution)/shard_map/ppermute | solution.py:26
  8.7 2.6 %copy-start = (bf16[64,1536]{1,0:T(8,128)(2,1)S(1)}, bf16[64,1536]{1,0:T(8,128)(2,1)}, u32[]{:S(2)}) copy-start(bf16[64,1536]{1,0:T(8,128)(2,1)} %residual_ref.3) | copy-start | bytes 589828
  8.7 2.6 %copy-start.2 = (f32[1536]{0:T(1024)S(1)}, f32[1536]{0:T(1024)}, u32[]{:S(2)}) copy-start(f32[1536]{0:T(1024)} %weight_ref.7) | copy-start | bytes 18436
  8.7 2.6 %copy-start.4 = (s32[512]{0:T(512)S(1)}, s32[512]{0:T(512)}, u32[]{:S(2)}) copy-start(s32[512]{0:T(512)} %chosen_ref.1) | copy-start | bytes 6148
  8.7 5.2 %collective-permute-start.3 = (f32[32,768]{1,0:T(8,128)S(1)}, f32[32,768]{1,0:T(8,128)S(1)}, u32[]{:S(2)}, u32[]{:S(2)}) collective-permute-start(f32[32,768]{1,0:T(8,128)S(1)} %add.10.second_ref), channel_id=1, source_target_pairs={{0,2},{1,3},{2,0},{3,1},{4,6},{5,7},{6,4},{7,5},{8,10},{9,11},{10,... | collective-permute-start | bytes 294920 | tf_op jit(solution)/shard_map/ppermute | solution.py:26
  14.8 6.8 %collective-permute-start.5 = (f32[32,768]{1,0:T(8,128)S(1)}, f32[32,768]{1,0:T(8,128)S(1)}, u32[]{:S(2)}, u32[]{:S(2)}) collective-permute-start(f32[32,768]{1,0:T(8,128)S(1)} %pad_maximum_fusion), channel_id=1, source_target_pairs={{0,4},{4,0},{8,12},{12,8},{1,5},{5,1},{9,13},{13,9},{2,6},{6,2},{1... | collective-permute-start | bytes 294920 | tf_op jit(solution)/shard_map/ppermute | solution.py:26
  16.7 7.2 %collective-permute-start.7 = (f32[32,512]{1,0:T(8,128)S(1)}, f32[32,512]{1,0:T(8,128)S(1)}, u32[]{:S(2)}, u32[]{:S(2)}) collective-permute-start(f32[32,512]{1,0:T(8,128)S(1)} %get-tuple-element.48), channel_id=1, source_target_pairs={{0,12},{4,8},{8,4},{12,0},{1,13},{5,9},{9,5},{13,1},{2,14},{6,10},... | collective-permute-start | bytes 196616 | tf_op jit(solution)/shard_map/ppermute | solution.py:26
  19.2 7.3 %collective-permute-start.8 = (f32[32,512]{1,0:T(8,128)S(1)}, f32[32,512]{1,0:T(8,128)S(1)}, u32[]{:S(2)}, u32[]{:S(2)}) collective-permute-start(f32[32,512]{1,0:T(8,128)S(1)} %get-tuple-element.49), channel_id=1, source_target_pairs={{0,8},{4,12},{8,0},{12,4},{1,9},{5,13},{9,1},{13,5},{2,10},{6,14},... | collective-permute-start | bytes 196616 | tf_op jit(solution)/shard_map/ppermute | solution.py:26
  19.8 6.7 %collective-permute-start.4 = (f32[32,640]{1,0:T(8,128)S(1)}, f32[32,640]{1,0:T(8,128)S(1)}, u32[]{:S(2)}, u32[]{:S(2)}) collective-permute-start(f32[32,640]{1,0:T(8,128)S(1)} %slice.8), channel_id=1, source_target_pairs={{0,4},{4,0},{8,12},{12,8},{1,5},{5,1},{9,13},{13,9},{2,6},{6,2},{1... | collective-permute-start | bytes 245768 | tf_op jit(solution)/shard_map/ppermute | solution.py:26
  21.6 5.5 %collective-permute-start.6 = (f32[32,512]{1,0:T(8,128)S(1)}, f32[32,512]{1,0:T(8,128)S(1)}, u32[]{:S(2)}, u32[]{:S(2)}) collective-permute-start(f32[32,512]{1,0:T(8,128)S(1)} %slice_add_fusion), channel_id=1, source_target_pairs={{0,8},{4,12},{8,0},{12,4},{1,9},{5,13},{9,1},{13,5},{2,10},{6,14},... | collective-permute-start | bytes 196616 | tf_op jit(solution)/shard_map/ppermute | solution.py:26
